TPU v7x, 32 devices: a whole 2x2x4 slice. The times are simulated.
32 devices in a mesh: fsdp: 4 (over y, x), tensor: 8 (over z, core).
Axes of the slice: x: 2, y: 2, z: 4, core: 2. Of those that a mesh axis runs over, the one named last changes fastest.
Arguments:
- hidden_in: bfloat16 [16384, 1536], P(('fsdp', 'tensor')), may hold values from -6 to 6
- norm_gain: bfloat16 [1536], P('fsdp'), may hold values from 0.25 to 1.75
- in_gate: bfloat16 [1536, 3072], P('fsdp', 'tensor'), may hold values from -0.15625 to 0.15625
- in_inner: bfloat16 [1536, 3072], P('fsdp', 'tensor')
- in_state: bfloat16 [1536, 256], P('fsdp'), may hold values from -0.15625 to 0.15625
- in_step: bfloat16 [1536, 48], P('fsdp', 'tensor'), may hold values from -0.15625 to 0.15625
- conv_inner: bfloat16 [4, 48, 64], P(None, 'tensor', 'fsdp'), may hold values from -3 to 3
- conv_inner_shift: bfloat16 [48, 64], P('tensor', 'fsdp'), may hold values from -3 to 3
- conv_state: bfloat16 [4, 256], P(None, 'fsdp'), may hold values from -3 to 3
- conv_state_shift: bfloat16 [256], P('fsdp'), may hold values from -3 to 3
- step_offset: bfloat16 [48], P('fsdp'), may hold values from -6 to -2
- log_rate: bfloat16 [48], P('fsdp'), may hold values from 0 to 2.09375
- skip_gain: bfloat16 [48], P('fsdp'), may hold values from 0.5 to 2
- inner_gain: bfloat16 [48, 64], P('tensor', 'fsdp'), may hold values from 0.25 to 1.75
- out_weight: bfloat16 [3072, 1536], P('tensor', 'fsdp'), may hold values from -0.109375 to 0.109375
- segment_ids: int32 [16384], P('fsdp'), may hold values from 0 to 16, as said below
- grad_out: bfloat16 [16384, 1536], P(('fsdp', 'tensor')), may hold values from -6 to 6
Outputs:
- layer_out: bfloat16 [16384, 1536], P(('fsdp', 'tensor'))
- grad_hidden: bfloat16 [16384, 1536], P(('fsdp', 'tensor'))
- grad_norm_gain: float32 [1536], P('fsdp')
- grad_in_gate: float32 [1536, 3072], P('fsdp', 'tensor')
- grad_in_inner: float32 [1536, 3072], P('fsdp', 'tensor')
- grad_in_state: float32 [1536, 256], P('fsdp')
- grad_in_step: float32 [1536, 48], P('fsdp', 'tensor')
- grad_conv_inner: float32 [4, 48, 64], P(None, 'tensor', 'fsdp')
- grad_conv_inner_shift: float32 [48, 64], P('tensor', 'fsdp')
- grad_conv_state: float32 [4, 256], P(None, 'fsdp')
- grad_conv_state_shift: float32 [256], P('fsdp')
- grad_step_offset: float32 [48], P('fsdp')
- grad_log_rate: float32 [48], P('fsdp')
- grad_skip_gain: float32 [48], P('fsdp')
- grad_inner_gain: float32 [48, 64], P('tensor', 'fsdp')
- grad_out_weight: float32 [3072, 1536], P('tensor', 'fsdp')
Inputs may be any that keep to these rules, and one draw needn't show every extreme that they name: `segment_ids`: each sequence of 1024 consecutive tokens is a pack of documents: ids start at 0 in every sequence and rise by one at each document's first token. The largest id is reached in some sequence of every draw.
All inputs are finite; a program needn't handle non-finite values.
Results may differ from a plain program's by a relative error of at most 0.025.
Values may be sent and summed in bfloat16 or wider, within the bound.
A program may use at most 256 MiB of HBM per device.

v0:
```python
import jax
import jax.numpy as jnp
from jax import lax
from jax.sharding import PartitionSpec as P

H = 48
P_SIZE = 64
K = 4
SPAN = 256
SEQ = 1024


EPSILON = 1e-05


def causal_conv(values, seq_docs, kernel, shift_term):
    length_all = values.shape[0]
    taps = kernel.shape[0]
    total = shift_term[None, :] + kernel[taps - 1][None, :] * values
    for shift_by in range(1, taps):
        earlier = jnp.concatenate(
            [jnp.zeros((shift_by, values.shape[1]), values.dtype), values[: length_all - shift_by]],
            0,
        )
        earlier_docs = jnp.concatenate(
            [jnp.full((shift_by,), -1, seq_docs.dtype), seq_docs[: length_all - shift_by]], 0
        )
        total = total + kernel[taps - 1 - shift_by][None, :] * jnp.where(
            (earlier_docs == seq_docs)[:, None], earlier, 0.0
        )
    return total


def state_scan(inputs, steps, decay, bmat, cmat, seq_docs):
    length_all = inputs.shape[0]
    heads = inputs.shape[1]
    width = inputs.shape[2]
    states_n = bmat.shape[1]
    blocks = length_all // SPAN
    logs = (steps * decay[None, :]).reshape(blocks, SPAN, heads)
    cumul = jnp.cumsum(logs, axis=1)
    weighted = (inputs * steps[:, :, None]).reshape(blocks, SPAN, heads, width)
    b_blocks = bmat.reshape(blocks, SPAN, states_n)
    c_blocks = cmat.reshape(blocks, SPAN, states_n)
    doc_blocks = seq_docs.reshape(blocks, SPAN)
    order = jnp.arange(SPAN)
    causal = (order[:, None] >= order[None, :])[None] & (
        doc_blocks[:, :, None] == doc_blocks[:, None, :]
    )
    causal_heads = causal[:, :, :, None]
    differ = cumul[:, :, None, :] - cumul[:, None, :, :]
    kernel = jnp.where(causal_heads, jnp.exp(jnp.where(causal_heads, differ, 0.0)), 0.0)
    scores = jnp.einsum("cin,cjn->cij", c_blocks, b_blocks, precision=lax.Precision.HIGHEST)
    local_out = jnp.einsum(
        "cijh,cjhp->cihp", kernel * scores[:, :, :, None], weighted, precision=lax.Precision.HIGHEST
    )
    last_log = cumul[:, -1, :]
    last_doc = doc_blocks[:, -1]
    to_end = jnp.where(
        (doc_blocks == last_doc[:, None])[:, :, None], jnp.exp(last_log[:, None, :] - cumul), 0.0
    )
    block_states = jnp.einsum(
        "cjh,cjhp,cjn->chpn", to_end, weighted, b_blocks, precision=lax.Precision.HIGHEST
    )
    carried = jnp.zeros((heads, width, states_n), inputs.dtype)
    prior_doc = doc_blocks[0, 0]
    outputs = []
    for block in range(blocks):
        from_start = jnp.where(
            (doc_blocks[block] == prior_doc)[:, None], jnp.exp(cumul[block]), 0.0
        )
        carried_out = jnp.einsum(
            "ih,in,hpn->ihp", from_start, c_blocks[block], carried, precision=lax.Precision.HIGHEST
        )
        outputs.append(local_out[block] + carried_out)
        keeping = jnp.where(last_doc[block] == prior_doc, jnp.exp(last_log[block]), 0.0)
        carried = keeping[:, None, None] * carried + block_states[block]
        prior_doc = last_doc[block]
    return jnp.concatenate(outputs, 0)


def mixer_block(
    gate_pre,
    inner_pre,
    state_pre,
    step_pre,
    seq_docs,
    kernel_inner,
    shift_inner,
    kernel_state,
    shift_state,
    offsets,
    rates,
    skips,
):
    heads = offsets.shape[0]
    length_all = gate_pre.shape[0]
    width = inner_pre.shape[1] // heads
    states_n = state_pre.shape[1] // 2
    inner_act = jax.nn.silu(causal_conv(inner_pre, seq_docs, kernel_inner, shift_inner))
    state_act = jax.nn.silu(causal_conv(state_pre, seq_docs, kernel_state, shift_state))
    steps = jax.nn.softplus(step_pre + offsets[None, :])
    decay = -jnp.exp(rates)
    inputs = inner_act.reshape(length_all, heads, width)
    scanned = state_scan(
        inputs, steps, decay, state_act[:, :states_n], state_act[:, states_n:], seq_docs
    )
    scanned = scanned + skips[None, :, None] * inputs
    return scanned.reshape(length_all, heads * width) * jax.nn.silu(gate_pre)


def on_device(
    hidden_in,
    norm_gain,
    in_gate,
    in_inner,
    in_state,
    in_step,
    conv_inner,
    conv_inner_shift,
    conv_state,
    conv_state_shift,
    step_offset,
    log_rate,
    skip_gain,
    inner_gain,
    out_weight,
    segment_ids,
    grad_out,
):
    gathered = (
        lax.all_gather(norm_gain, "fsdp", axis=0, tiled=True),
        lax.all_gather(in_gate, "fsdp", axis=0, tiled=True),
        lax.all_gather(in_inner, "fsdp", axis=0, tiled=True),
        lax.all_gather(in_state, "fsdp", axis=0, tiled=True),
        lax.all_gather(in_step, "fsdp", axis=0, tiled=True),
        lax.all_gather(conv_inner, "fsdp", axis=2, tiled=True),
        lax.all_gather(conv_inner_shift, "fsdp", axis=1, tiled=True),
        lax.all_gather(conv_state, "fsdp", axis=1, tiled=True),
        lax.all_gather(conv_state_shift, "fsdp", axis=0, tiled=True),
        lax.all_gather(step_offset, "fsdp", axis=0, tiled=True),
        lax.all_gather(log_rate, "fsdp", axis=0, tiled=True),
        lax.all_gather(skip_gain, "fsdp", axis=0, tiled=True),
        lax.all_gather(inner_gain, "fsdp", axis=1, tiled=True),
        lax.all_gather(out_weight, "fsdp", axis=1, tiled=True),
    )
    (
        full_gain,
        gate_cols,
        inner_cols,
        state_cols,
        step_cols,
        conv_inner_full,
        conv_inner_shift_full,
        conv_state_full,
        conv_state_shift_full,
        offset_full,
        rate_full,
        skip_full,
        inner_gain_full,
        out_rows_full,
    ) = gathered
    inner_local = gate_cols.shape[1]
    state_width = state_cols.shape[1]
    heads_local = step_cols.shape[1]
    first_head = lax.axis_index("tensor") * heads_local
    projection = jnp.concatenate([gate_cols, inner_cols, state_cols, step_cols], 1)
    head_projection = jnp.concatenate([gate_cols, inner_cols, step_cols], 1)
    params = (
        conv_inner_full.astype(jnp.float32).reshape(K, inner_local),
        conv_inner_shift_full.astype(jnp.float32).reshape(inner_local),
        conv_state_full.astype(jnp.float32),
        conv_state_shift_full.astype(jnp.float32),
        lax.dynamic_slice_in_dim(offset_full.astype(jnp.float32), first_head, heads_local),
        lax.dynamic_slice_in_dim(rate_full.astype(jnp.float32), first_head, heads_local),
        lax.dynamic_slice_in_dim(skip_full.astype(jnp.float32), first_head, heads_local),
    )
    gain_inner = inner_gain_full.astype(jnp.float32).reshape(inner_local)
    gain_outer = full_gain.astype(jnp.float32)
    hidden = hidden_in.astype(jnp.float32)
    inv_rms = lax.rsqrt(jnp.mean(hidden * hidden, -1, keepdims=True) + EPSILON)
    normed = (hidden * inv_rms * gain_outer).astype(jnp.bfloat16)
    projected = jnp.dot(
        lax.all_gather(normed, "tensor", axis=0, tiled=True),
        projection,
        preferred_element_type=jnp.float32,
    )
    group_rows = projected.shape[0]
    seqs = group_rows // SEQ
    gate_pre = projected[:, :inner_local]
    inner_pre = projected[:, inner_local : 2 * inner_local]
    state_pre = projected[:, 2 * inner_local : 2 * inner_local + state_width]
    step_pre = projected[:, 2 * inner_local + state_width :]
    seq_docs = segment_ids.reshape(seqs, SEQ)
    stacked = tuple(
        (
            part.reshape(seqs, SEQ, part.shape[1])
            for part in (gate_pre, inner_pre, state_pre, step_pre)
        )
    )

    def forward_one(items):
        return mixer_block(items[0], items[1], items[2], items[3], items[4], *params)

    gated = lax.map(forward_one, stacked + (seq_docs,)).reshape(group_rows, inner_local)
    inner_width = H * P_SIZE
    squares = lax.psum(jnp.sum(gated * gated, -1).astype(jnp.bfloat16), "tensor").astype(
        jnp.float32
    )
    inner_inv = lax.rsqrt(squares / inner_width + EPSILON)[:, None]
    normed_inner = (gated * inner_inv * gain_inner).astype(jnp.bfloat16)
    mixed = lax.psum_scatter(
        jnp.dot(normed_inner, out_rows_full, preferred_element_type=jnp.float32).astype(
            jnp.bfloat16
        ),
        "tensor",
        scatter_dimension=0,
        tiled=True,
    ).astype(jnp.float32)
    layer_out = (hidden + mixed).astype(jnp.bfloat16)
    normed_all, upstream = (
        lax.all_gather(normed, "tensor", axis=0, tiled=True),
        lax.all_gather(grad_out, "tensor", axis=0, tiled=True),
    )
    cotangent = grad_out.astype(jnp.float32)
    grad_out_part = lax.dot_general(
        normed_inner, upstream, (((0,), (0,)), ((), ())), preferred_element_type=jnp.float32
    )
    d_inner = lax.dot_general(
        upstream, out_rows_full, (((1,), (1,)), ((), ())), preferred_element_type=jnp.float32
    )
    grad_gain_inner = jnp.sum(d_inner * gated * inner_inv, 0)
    scaled = d_inner * gain_inner
    products = lax.psum(jnp.sum(gated * scaled, -1), "tensor")
    d_gated = inner_inv * scaled - gated * inner_inv**3 * (products / inner_width)[:, None]

    def backward_one(items):
        docs_one = items[4]

        def local_map(gate_in, inner_in, state_in, step_in, *weights):
            return mixer_block(gate_in, inner_in, state_in, step_in, docs_one, *weights)

        unused, pull = jax.vjp(local_map, items[0], items[1], items[2], items[3], *params)
        return pull(items[5])

    pulled = lax.map(backward_one, stacked + (seq_docs, d_gated.reshape(seqs, SEQ, inner_local)))
    d_gate_low = pulled[0].reshape(group_rows, inner_local).astype(jnp.bfloat16)
    d_inner_low = pulled[1].reshape(group_rows, inner_local).astype(jnp.bfloat16)
    d_step_low = pulled[3].reshape(group_rows, heads_local).astype(jnp.bfloat16)
    d_heads = jnp.concatenate([d_gate_low, d_inner_low, d_step_low], 1)
    d_state = lax.psum_scatter(
        pulled[2].reshape(group_rows, state_width).astype(jnp.bfloat16),
        "tensor",
        scatter_dimension=0,
        tiled=True,
    )
    (
        grad_conv_in,
        grad_conv_in_shift,
        grad_conv_st,
        grad_conv_st_shift,
        grad_offset,
        grad_rate,
        grad_skip,
    ) = [jnp.sum(part, 0) for part in pulled[4:]]
    grad_heads = lax.dot_general(
        normed_all, d_heads, (((0,), (0,)), ((), ())), preferred_element_type=jnp.float32
    )
    grad_state_part = lax.dot_general(
        normed, d_state, (((0,), (0,)), ((), ())), preferred_element_type=jnp.float32
    )
    state_back = lax.dot_general(
        d_state, state_cols, (((1,), (1,)), ((), ())), preferred_element_type=jnp.float32
    )
    d_normed = (
        lax.psum_scatter(
            lax.dot_general(
                d_heads,
                head_projection,
                (((1,), (1,)), ((), ())),
                preferred_element_type=jnp.float32,
            ).astype(jnp.bfloat16),
            "tensor",
            scatter_dimension=0,
            tiled=True,
        ).astype(jnp.float32)
        + state_back
    )
    grad_gain_outer = jnp.sum(d_normed * hidden * inv_rms, 0)
    weighted_back = d_normed * gain_outer
    d_hidden = inv_rms * weighted_back - hidden * inv_rms**3 * jnp.mean(
        hidden * weighted_back, -1, keepdims=True
    )
    grad_hidden = (cotangent + d_hidden).astype(jnp.bfloat16)

    def place_heads(values):
        return lax.dynamic_update_slice_in_dim(jnp.zeros((H,), jnp.float32), values, first_head, 0)

    scattered = (
        lax.psum_scatter(grad_gain_outer, "fsdp", scatter_dimension=0, tiled=True),
        lax.psum_scatter(grad_heads[:, :inner_local], "fsdp", scatter_dimension=0, tiled=True),
        lax.psum_scatter(
            grad_heads[:, inner_local : 2 * inner_local], "fsdp", scatter_dimension=0, tiled=True
        ),
        lax.psum_scatter(grad_state_part, "fsdp", scatter_dimension=0, tiled=True),
        lax.psum_scatter(grad_heads[:, 2 * inner_local :], "fsdp", scatter_dimension=0, tiled=True),
        lax.psum_scatter(
            grad_conv_in.reshape(K, heads_local, P_SIZE), "fsdp", scatter_dimension=2, tiled=True
        ),
        lax.psum_scatter(
            grad_conv_in_shift.reshape(heads_local, P_SIZE), "fsdp", scatter_dimension=1, tiled=True
        ),
        lax.psum_scatter(grad_conv_st, "fsdp", scatter_dimension=1, tiled=True),
        lax.psum_scatter(grad_conv_st_shift, "fsdp", scatter_dimension=0, tiled=True),
        lax.psum_scatter(place_heads(grad_offset), "fsdp", scatter_dimension=0, tiled=True),
        lax.psum_scatter(place_heads(grad_rate), "fsdp", scatter_dimension=0, tiled=True),
        lax.psum_scatter(place_heads(grad_skip), "fsdp", scatter_dimension=0, tiled=True),
        lax.psum_scatter(
            grad_gain_inner.reshape(heads_local, P_SIZE), "fsdp", scatter_dimension=1, tiled=True
        ),
        lax.psum_scatter(grad_out_part, "fsdp", scatter_dimension=1, tiled=True),
    )
    shared = (
        lax.psum(scattered[0].astype(jnp.bfloat16), "tensor").astype(jnp.float32),
        lax.psum(scattered[3].astype(jnp.bfloat16), "tensor").astype(jnp.float32),
        lax.psum(scattered[7].astype(jnp.bfloat16), "tensor").astype(jnp.float32),
        lax.psum(scattered[8].astype(jnp.bfloat16), "tensor").astype(jnp.float32),
        lax.psum(scattered[9].astype(jnp.bfloat16), "tensor").astype(jnp.float32),
        lax.psum(scattered[10].astype(jnp.bfloat16), "tensor").astype(jnp.float32),
        lax.psum(scattered[11].astype(jnp.bfloat16), "tensor").astype(jnp.float32),
    )
    return (
        layer_out,
        grad_hidden,
        shared[0],
        scattered[1],
        scattered[2],
        shared[1],
        scattered[4],
        scattered[5],
        scattered[6],
        shared[2],
        shared[3],
        shared[4],
        shared[5],
        shared[6],
        scattered[12],
        scattered[13],
    )


def solution(mesh):
    return jax.shard_map(
        on_device,
        mesh=mesh,
        in_specs=(
            P(("fsdp", "tensor"), None),
            P("fsdp"),
            P("fsdp", "tensor"),
            P("fsdp", "tensor"),
            P("fsdp", None),
            P("fsdp", "tensor"),
            P(None, "tensor", "fsdp"),
            P("tensor", "fsdp"),
            P(None, "fsdp"),
            P("fsdp"),
            P("fsdp"),
            P("fsdp"),
            P("fsdp"),
            P("tensor", "fsdp"),
            P("tensor", "fsdp"),
            P("fsdp"),
            P(("fsdp", "tensor"), None),
        ),
        out_specs=(
            P(("fsdp", "tensor"), None),
            P(("fsdp", "tensor"), None),
            P("fsdp"),
            P("fsdp", "tensor"),
            P("fsdp", "tensor"),
            P("fsdp", None),
            P("fsdp", "tensor"),
            P(None, "tensor", "fsdp"),
            P("tensor", "fsdp"),
            P(None, "fsdp"),
            P("fsdp"),
            P("fsdp"),
            P("fsdp"),
            P("fsdp"),
            P("tensor", "fsdp"),
            P("tensor", "fsdp"),
        ),
        check_vma=False,
    )
```

profile of v0, /device:TPU:0, one launch (start us, length us, event | category | flops | bytes accessed | tf_op | source)
XLA Modules:
  0.0 1901.2 jit_solution(14562134062098720228)
XLA Ops:
  90.0 99.3 %all-gather.10.cloned.1.call-done = bf16[4096,1536]{1,0:T(8,128)(2,1)} async-done(((bf16[512,1536]{1,0:T(8,128)(2,1)}), bf16[4096,1536]{1,0:T(8,128)(2,1)}) %all-gather.10.cloned.1.call-update) | async-done | bytes 12582928 | tf_op jit(solution)/shard_map/all_gather | solution.py:184
  189.4 20.2 %fusion.214 = f32[4096,1030]{0,1:T(8,128)} fusion(bf16[4096,1536]{1,0:T(8,128)(2,1)} %all-gather.10.cloned.1.call-done, bf16[1536,6]{1,0:T(8,128)(2,1)S(1)} %copy.430, bf16[1536,256]{1,0:T(8,128)(2,1)S(1)} %all_gather.55, bf16[1536,384]{1,0:T(8,128)(2,1)} %all-gather.14.cloned.1.call-done, bf16[1536,384]{1,0:T(8,128)(2,1)} %all-gather.12.cloned.1.call-done), kind=kOutput, calls=%fused_computation.424 | convolution fusion | flops 12973056000 | bytes 32622592 | tf_op jit(solution)/shard_map/dot_general | solution.py:183
  243.2 200.4 %while.47 = (s32[]{:T(128)}, f32[4,1024,384]{1,2,0:T(8,128)}, f32[6,64]{1,0:T(8,128)}, f32[4,384]{1,0:T(4,128)S(1)}, f32[4,1024,384]{1,2,0:T(8,128)}, /*index=5*...) while((s32[]{:T(128)}, f32[4,1024,384]{1,2,0:T(8,128)}, ...), condition=%wide.wide.region_4.5_spmd, body=%wide.wide.region_1.4_spmd.sunk | while | flops 2842484736 | bytes 98474744 | solution.py:205
  453.8 14.8 psum.63
  482.5 25.9 %psum.64 = f32[4096]{0:T(1024)S(1)} all-reduce(f32[4096]{0:T(1024)S(1)} %get-tuple-element.973), channel_id=1, replica_groups=mesh['fsdp'=4,'tensor'=8] {'tensor'}, use_global_device_ids=true, to_apply=%region_9.10 | all-reduce | flops 4096 | bytes 32768 | tf_op jit(solution)/shard_map/psum | solution.py:234
  518.5 815.8 %while.48 = (s32[]{:T(128)}, bf16[4,1024,384]{2,1,0:T(8,128)(2,1)}, bf16[4,1024,384]{2,1,0:T(8,128)(2,1)}, bf16[4,1024,256]{2,1,0:T(8,128)(2,1)}, bf16[4,1024,6]...) while((s32[]{:T(128)}, bf16[4,1024,384]{2,1,0:T(8,128)(2,1)}, ...), condition=%wide.wide.region_37.38_spmd, body=%wide.wide.region_10.37_spmd.sunk | while | flops 8392002560 | bytes 370372224 | solution.py:246
  674.7 30.2 %reduce-window.66 = f32[4,6,2,128]{3,2,1,0:T(2,128)S(1)} reduce-window(f32[4,6,2,128]{3,2,1,0:T(2,128)S(1)} %reshape.1310, f32[]{:T(128)} %constant.191.clone.1..sunk.1), window={size=1x1x1x128 pad=0_0x0_0x0_0x0_127}, to_apply=%region_21.21 | reduce-window | flops 780288 | bytes 49156 | tf_op jit(solution)/shard_map/reduce-window.20
  784.9 18.1 bitcast_add_fusion.5
  883.2 30.2 %reduce-window.66 = f32[4,6,2,128]{3,2,1,0:T(2,128)S(1)} reduce-window(f32[4,6,2,128]{3,2,1,0:T(2,128)S(1)} %reshape.1310, f32[]{:T(128)} %constant.191.clone.1..sunk.1), window={size=1x1x1x128 pad=0_0x0_0x0_0x0_127}, to_apply=%region_21.21 | reduce-window | flops 780288 | bytes 49156 | tf_op jit(solution)/shard_map/reduce-window.20
  1079.7 30.2 %reduce-window.66 = f32[4,6,2,128]{3,2,1,0:T(2,128)S(1)} reduce-window(f32[4,6,2,128]{3,2,1,0:T(2,128)S(1)} %reshape.1310, f32[]{:T(128)} %constant.191.clone.1..sunk.1), window={size=1x1x1x128 pad=0_0x0_0x0_0x0_127}, to_apply=%region_21.21 | reduce-window | flops 780288 | bytes 49156 | tf_op jit(solution)/shard_map/reduce-window.20
  1190.0 18.1 bitcast_add_fusion.5
  1288.3 30.2 %reduce-window.66 = f32[4,6,2,128]{3,2,1,0:T(2,128)S(1)} reduce-window(f32[4,6,2,128]{3,2,1,0:T(2,128)S(1)} %reshape.1310, f32[]{:T(128)} %constant.191.clone.1..sunk.1), window={size=1x1x1x128 pad=0_0x0_0x0_0x0_127}, to_apply=%region_21.21 | reduce-window | flops 780288 | bytes 49156 | tf_op jit(solution)/shard_map/reduce-window.20
  1334.4 34.2 %reduce-scatter.19.cloned.1.call-done = bf16[512,256]{1,0:T(8,128)(2,1)} async-done(((bf16[4096,256]{1,0:T(8,128)(2,1)}), bf16[512,256]{1,0:T(8,128)(2,1)}) %reduce-scatter.19.cloned.1.call-update) | async-done | bytes 262160 | tf_op jit(solution)/shard_map/reduce_scatter | solution.py:251
  1373.5 15.6 fusion.233
  1403.6 18.6 convolution_convert_fusion
  1451.9 17.8 reduce-scatter.23.cloned.1.call-done
  1471.9 38.5 %reduce-scatter.21.cloned.1.call-done = f32[384,384]{0,1:T(8,128)} async-done(((f32[1536,384]{0,1:T(8,128)}), f32[384,384]{0,1:T(8,128)}) %reduce-scatter.21.cloned.1.call-update) | async-done | bytes 589840 | tf_op jit(solution)/shard_map/reduce_scatter | solution.py:301
  1512.4 55.5 %all-reduce.68.cloned.1.call-done = bf16[384,256]{1,0:T(8,128)(2,1)} async-done(((bf16[384,256]{1,0:T(8,128)(2,1)}), bf16[384,256]{1,0:T(8,128)(2,1)}) %all-reduce.68.cloned.1.call-update) | async-done | bytes 196624 | tf_op jit(solution)/shard_map/psum | solution.py:325
  1569.6 128.7 %reduce-scatter.17.cloned.1.call-done = bf16[512,1536]{1,0:T(8,128)(2,1)} async-done(((bf16[4096,1536]{1,0:T(8,128)(2,1)}), bf16[512,1536]{1,0:T(8,128)(2,1)}) %reduce-scatter.17.cloned.1.call-update) | async-done | bytes 1572880 | tf_op jit(solution)/shard_map/reduce_scatter | solution.py:276
  1702.8 16.7 all-reduce.63
  1719.8 14.5 all-reduce.64
  1739.5 89.0 %reduce-scatter.15.cloned.1.call-done = bf16[512,1536]{1,0:T(8,128)(2,1)} async-done(((bf16[4096,1536]{1,0:T(8,128)(2,1)}), bf16[512,1536]{1,0:T(8,128)(2,1)}) %reduce-scatter.15.cloned.1.call-update) | async-done | bytes 1572880 | tf_op jit(solution)/shard_map/reduce_scatter | solution.py:212
  1833.7 19.5 %reduce-scatter.27.cloned.1.call-done = f32[384,6]{0,1:T(8,128)} async-done(((f32[1536,6]{0,1:T(8,128)}), f32[384,6]{0,1:T(8,128)}) %reduce-scatter.27.cloned.1.call-update) | async-done | bytes 9232 | tf_op jit(solution)/shard_map/reduce_scatter | solution.py:306
  1853.1 41.2 %reduce-scatter.29.cloned.1.call-done = f32[384,384]{1,0:T(8,128)} async-done(((f32[384,1536]{1,0:T(8,128)}), f32[384,384]{1,0:T(8,128)}) %reduce-scatter.29.cloned.1.call-update) | async-done | bytes 589840 | tf_op jit(solution)/shard_map/reduce_scatter | solution.py:321
  (2394 shorter events, 1026.9 us)
Async XLA Ops:
  7.2 82.8 %all-gather.12.cloned.1.call-start = ((), (), s32[]{:S(2)}) async-start(), calls=%async_computation.10 | async-start | bytes 1474560 | tf_op jit(solution)/shard_map/all_gather | solution.py:133
  7.9 82.1 %all-gather.14.cloned.1.call-start = ((), (), s32[]{:S(2)}) async-start(), calls=%async_computation.11 | async-start | bytes 1474560 | tf_op jit(solution)/shard_map/all_gather | solution.py:134
  8.7 180.7 %all-gather.10.cloned.1.call-start = ((), (), s32[]{:S(2)}) async-start(), calls=%async_computation.9 | async-start | bytes 14155776 | tf_op jit(solution)/shard_map/all_gather | solution.py:184
  23.7 56.0 %copy-start.166 = (bf16[384,256]{1,0:T(8,128)(2,1)S(1)}, bf16[384,256]{1,0:T(8,128)(2,1)}, u32[]{:S(2)}) copy-start(bf16[384,256]{1,0:T(8,128)(2,1)} %param.25) | copy-start | bytes 589828
  23.7 444.9 %all-gather.16.cloned.1.call-start = ((), (), s32[]{:S(2)}) async-start(), calls=%async_computation.12 | async-start | bytes 1474560 | tf_op jit(solution)/shard_map/all_gather | solution.py:145
  24.3 444.4 %all-gather.18.cloned.1.call-start = ((), (), s32[]{:S(2)}) async-start(), calls=%async_computation.14 | async-start | bytes 14155776 | tf_op jit(solution)/shard_map/all_gather | solution.py:223
  24.9 1343.7 %reduce-scatter.19.cloned.1.call-start = ((), (), s32[]{:S(2)}) async-start(), calls=%async_computation.16 | async-start | bytes 2359296 | tf_op jit(solution)/shard_map/reduce_scatter | solution.py:251
  79.7 129.9 %copy-start.126 = (bf16[1536,6]{1,0:T(8,128)(2,1)}, bf16[1536,6]{1,0:T(8,128)(2,1)S(1)}, u32[]{:S(2)}) copy-start(bf16[1536,6]{1,0:T(8,128)(2,1)S(1)} %copy.430) | copy-start | bytes 55300
  90.0 119.6 %copy-start.105 = (bf16[1536,256]{1,0:T(8,128)(2,1)}, bf16[1536,256]{1,0:T(8,128)(2,1)S(1)}, u32[]{:S(2)}) copy-start(bf16[1536,256]{1,0:T(8,128)(2,1)S(1)} %all_gather.55) | copy-start | bytes 2359300
  1334.4 67.4 %reduce-scatter.25.cloned.1.call-start = ((), (), s32[]{:S(2)}) async-start(), calls=%async_computation.19 | async-start | bytes 1966080 | tf_op jit(solution)/shard_map/reduce_scatter | solution.py:305
  1371.4 79.7 %reduce-scatter.31.cloned.1.call-start = ((), (), s32[]{:S(2)}) async-start(), calls=%async_computation.23 | async-start | bytes 163840
  1373.4 96.3 %reduce-scatter.23.cloned.1.call-start = ((), (), s32[]{:S(2)}) async-start(), calls=%async_computation.18 | async-start | bytes 2949120 | tf_op jit(solution)/shard_map/reduce_scatter | solution.py:302
  1392.8 117.5 %reduce-scatter.21.cloned.1.call-start = ((), (), s32[]{:S(2)}) async-start(), calls=%async_computation.17 | async-start | bytes 2949120 | tf_op jit(solution)/shard_map/reduce_scatter | solution.py:301
  1393.4 174.5 %all-reduce.68.cloned.1.call-start = ((), (), s32[]{:S(2)}) async-start(), calls=%async_computation.20 | async-start | bytes 393216 | tf_op jit(solution)/shard_map/psum | solution.py:325
  1403.5 294.8 %reduce-scatter.17.cloned.1.call-start = ((), (), s32[]{:S(2)}) async-start(), calls=%async_computation.15 | async-start | bytes 14155776 | tf_op jit(solution)/shard_map/reduce_scatter | solution.py:276
  1422.2 406.3 %reduce-scatter.15.cloned.1.call-start = ((), (), s32[]{:S(2)}) async-start(), calls=%async_computation.13 | async-start | bytes 14155776 | tf_op jit(solution)/shard_map/reduce_scatter | solution.py:212
  1434.8 418.3 %reduce-scatter.27.cloned.1.call-start = ((), (), s32[]{:S(2)}) async-start(), calls=%async_computation.21 | async-start | bytes 61440 | tf_op jit(solution)/shard_map/reduce_scatter | solution.py:306
  1436.3 458.0 %reduce-scatter.29.cloned.1.call-start = ((), (), s32[]{:S(2)}) async-start(), calls=%async_computation.22 | async-start | bytes 2949120 | tf_op jit(solution)/shard_map/reduce_scatter | solution.py:321
  1446.5 251.8 %copy-start.52 = (bf16[512,1536]{1,0:T(8,128)(2,1)S(1)}, bf16[512,1536]{1,0:T(8,128)(2,1)}, u32[]{:S(2)}) copy-start(bf16[512,1536]{1,0:T(8,128)(2,1)} %param.21) | copy-start | bytes 4718596
  1446.5 251.8 %copy-start.132 = (bf16[512,256]{1,0:T(8,128)(2,1)S(1)}, bf16[512,256]{1,0:T(8,128)(2,1)}, u32[]{:S(2)}) copy-start(bf16[512,256]{1,0:T(8,128)(2,1)} %reduce-scatter.19.cloned.1.call-done) | copy-start | bytes 786436
  1446.6 251.7 %copy-start.182 = (f32[1536]{0:T(1024)S(1)}, f32[1536]{0:T(1024)}, u32[]{:S(2)}) copy-start(f32[1536]{0:T(1024)} %copy-done.181) | copy-start | bytes 18436
  1446.6 251.7 %copy-start.194 = (f32[512]{0:T(512)S(1)}, f32[512]{0:T(512)}, u32[]{:S(2)}) copy-start(f32[512]{0:T(512)} %copy-done.193) | copy-start | bytes 6148
  1569.6 258.9 %copy-start.65 = (bf16[512,1536]{1,0:T(8,128)(2,1)S(1)}, bf16[512,1536]{1,0:T(8,128)(2,1)}, u32[]{:S(2)}) copy-start(bf16[512,1536]{1,0:T(8,128)(2,1)} %param.37) | copy-start | bytes 4718596
  1569.6 258.9 %copy-start.197 = (f32[512]{0:T(512)S(1)}, f32[512]{0:T(512)}, u32[]{:S(2)}) copy-start(f32[512]{0:T(512)} %get-tuple-element.1164) | copy-start | bytes 6148
  (747 other events, 6700.5 us)
Sparse Core Ops, SparseCore 0:
  9.9 30.5 all-gather.11
  42.3 27.9 all-gather.13
  72.5 116.8 all-gather.9
  191.0 25.7 all-gather.15
  218.3 116.7 all-gather.17
  1334.5 34.0 reduce-scatter.18
  1372.2 29.5 reduce-scatter.24
  1405.1 23.8 reduce-scatter.30
  1432.3 37.3 reduce-scatter.22
  1472.9 37.3 reduce-scatter.20
  1513.3 54.5 all-reduce.67
  1570.1 128.1 reduce-scatter.16
  1700.6 127.8 reduce-scatter.14
  1831.7 21.4 reduce-scatter.26
  1856.9 37.4 reduce-scatter.28
where the time goes:
time: 1910 us; the launch traced here: 1900 us
  waiting for transfers between devices  535 us (28%)
  other arithmetic  433 us (23%)
  matrix products  390 us (20%)
  local copies, waits for them, and re-layouts  336 us (18%)
  blocking collectives  139 us (7%)
  loops' own time  48.8 us (3%)
    another operation x50, other arithmetic  181 us
    dot_general x16, matrix products, state_scan(): jnp.einsum('cijh,cjhp->cihp', kernel * scores[:, :, :, None], weighted, p...  155 us
    reduce_scatter x1, waiting for transfers between devices, on_device(): lax.psum_scatter(lax.dot_general(d_heads, head_projection, (((1,), (1,)),...  129 us
    all_gather x1, waiting for transfers between devices, on_device(): lax.all_gather(normed, 'tensor', axis=0, tiled=True)  99.3 us
    reduce_scatter x1, waiting for transfers between devices, on_device(): lax.psum_scatter(jnp.dot(normed_inner, out_rows_full, preferred_element_t...  89 us
    dot_general x60, matrix products, state_scan(): jnp.einsum('ih,in,hpn->ihp', from_start, c_blocks[block], carried, precis...  68.7 us
    psum x1, waiting for transfers between devices, on_device(): lax.psum(scattered[3].astype(jnp.bfloat16), 'tensor').astype(jnp.float32)  55.5 us
    slice x48, local copies, waits for them, and re-layouts, causal_conv(): values[:length_all - shift_by]  51.9 us
  transfers between devices with their start and end apart: 15, of which 10 were waited for; matrix products, arithmetic and copies ran while one was open for 18% of the time, Pallas kernels for 0%

commit v1 on v0

v1 whole, which is shorter than its diff:
```python
import functools

import jax
import jax.numpy as jnp
from jax import lax
from jax.sharding import PartitionSpec as P
from jax.experimental import pallas as pl
from jax.experimental.pallas import tpu as pltpu

SEQ = 1024
L = 128
CH = SEQ // L
K = 4
GH = 6
GW = 384
EPSILON = 1e-05
LOG2E = 1.4426950408889634
F32 = jnp.float32
BF = jnp.bfloat16
ST, CU, EE, FF, SG = 0, 8, 16, 24, 32


def mm(a, b, dims=((1,), (0,))):
    return lax.dot_general(a, b, (dims, ((), ())), preferred_element_type=F32)


def split2(x):
    hi = x.astype(BF)
    return hi, (x - hi.astype(F32)).astype(BF)


def split3(x):
    hi = x.astype(BF)
    rest = x - hi.astype(F32)
    mid = rest.astype(BF)
    return hi, mid, (rest - mid.astype(F32)).astype(BF)


def sigmoid(v):
    return 1.0 / (1.0 + jnp.exp(-v))


def back_conv_input(window, k):
    return window[8 - k : 8 - k + L]


def prep_body(state_ref, step_ref, tok_ref, row_ref, convst_ref, head_ref,
              bc_ref, bct_ref, g_ref, pack_ref, cumt_ref, pad_ref):
    pad_ref[pl.ds(0, 8), :] = jnp.zeros((8, 256), F32)
    pad_ref[pl.ds(8, SEQ), :] = state_ref[...]
    lane = lax.broadcasted_iota(jnp.int32, (L, L), 1)
    sub = lax.broadcasted_iota(jnp.int32, (L, L), 0)
    tri = (sub >= lane).astype(BF)
    offset = head_ref[0:1, :]
    decay = head_ref[1:2, :]
    taps = [convst_ref[k : k + 1, :] for k in range(K)]
    shift = convst_ref[K : K + 1, :]

    def chunk(c, _):
        base = pl.multiple_of(c * L, L)
        rows = pl.ds(base, L)
        tok = tok_ref[rows, :]
        window = pad_ref[pl.ds(base, L + 8), :]
        total = shift + taps[K - 1] * back_conv_input(window, 0)
        for k in range(1, K):
            total = total + taps[K - 1 - k] * (back_conv_input(window, k) * tok[:, 2 + k : 3 + k])
        act = total * sigmoid(total)
        low = act.astype(BF)
        bc_ref[rows, :] = low
        bct_ref[c] = jnp.concatenate([act[:, :128].T, act[:, 128:].T], 0).astype(BF)
        scores = mm(low[:, 128:], low[:, :128], ((1,), (1,)))
        same = (tok[:, 0:1] == row_ref[c][0:1, :]) & (sub >= lane)
        g_ref[c] = jnp.where(same, scores, 0.0)
        v = step_ref[rows, :] + offset
        steps = jnp.maximum(v, 0.0) + jnp.log1p(jnp.exp(-jnp.abs(v)))
        logs = steps * (decay * LOG2E)
        hi, mid, lo = split3(logs)
        cum = mm(tri, hi) + mm(tri, mid) + mm(tri, lo)
        last = cum[L - 1 : L, :]
        enter = jnp.exp2(cum) * tok[:, 1:2]
        leave = jnp.exp2(last - cum) * tok[:, 2:3]
        sig = sigmoid(v)
        cumt = cum.T
        zeros = jnp.zeros((L, 2), F32)
        for g in range(4):
            part = slice(GH * g, GH * g + GH)
            pieces = []
            for values in (steps, cum, enter, leave, sig):
                pieces += [values[:, part], zeros]
            pieces.append(jnp.zeros((L, 88), F32))
            pack_ref[g, rows, :] = jnp.concatenate(pieces, 1)
            cumt_ref[g, c] = jnp.concatenate([cumt[part, :], jnp.zeros((2, L), F32)], 0)
        return 0

    lax.fori_loop(0, CH, chunk, 0)


def vm(*shape):
    return pl.BlockSpec(memory_space=pltpu.VMEM)


def prep(state_pre, step_pre, tok, row, convst, head):
    return pl.pallas_call(
        prep_body,
        out_shape=(
            jax.ShapeDtypeStruct((SEQ, 256), BF),
            jax.ShapeDtypeStruct((CH, 256, L), BF),
            jax.ShapeDtypeStruct((CH, L, L), F32),
            jax.ShapeDtypeStruct((4, SEQ, 128), F32),
            jax.ShapeDtypeStruct((4, CH, 8, L), F32),
        ),
        in_specs=[vm()] * 6,
        out_specs=[vm()] * 5,
        scratch_shapes=[pltpu.VMEM((SEQ + 8, 256), F32)],
        compiler_params=pltpu.CompilerParams(vmem_limit_bytes=56 * 2**20),
        name="prep",
    )(state_pre, step_pre, tok, row, convst, head)


def pair_lanes(pack, first, q):
    lane = lax.broadcasted_iota(jnp.int32, (pack.shape[0], 128), 1)
    a = pack[:, first + 2 * q : first + 2 * q + 1]
    b = pack[:, first + 2 * q + 1 : first + 2 * q + 2]
    return jnp.where(lane < 64, a, b)


def spread(pack, first):
    return jnp.concatenate([pair_lanes(pack, first, q) for q in range(3)], 1)


def block_diag(x):
    lane = lax.broadcasted_iota(jnp.int32, x.shape, 1)
    zero = jnp.zeros_like(x)
    return jnp.concatenate([jnp.where(lane < 64, x, zero), jnp.where(lane < 64, zero, x)], 0)


def decay_kernel(pack, cumt, h):
    return jnp.exp2(jnp.minimum(pack[:, CU + h : CU + h + 1] - cumt[h : h + 1, :], 0.0))


def conv_of(window, tok, par):
    total = par[K : K + 1, :] + par[K - 1 : K, :] * back_conv_input(window, 0)
    for k in range(1, K):
        total = total + par[K - 1 - k : K - k, :] * (back_conv_input(window, k) * tok[:, 2 + k : 3 + k])
    return total


P_SHIFT, P_SKIP, P_GAIN = 4, 5, 6


def fwd_body(inner_ref, gate_ref, par_ref, tok_ref, bc_ref, bct_ref, g_ref, pack_ref, cumt_ref,
             gated_ref, states_ref, ss_ref, pad_ref, st_ref):
    pad_ref[pl.ds(0, 8), :] = jnp.zeros((8, GW), F32)
    pad_ref[pl.ds(8, SEQ), :] = inner_ref[...]
    st_ref[...] = jnp.zeros_like(st_ref)
    par = par_ref[...]

    @pl.when(pl.program_id(0) == 0)
    def _():
        ss_ref[...] = jnp.zeros_like(ss_ref)

    def chunk(c, _):
        base = pl.multiple_of(c * L, L)
        rows = pl.ds(base, L)
        tok = tok_ref[rows, :]
        u = conv_of(pad_ref[pl.ds(base, L + 8), :], tok, par)
        act = u * sigmoid(u)
        pack = pack_ref[0, rows, :]
        cumt = cumt_ref[0, c]
        g = g_ref[c]
        weighted = act * spread(pack, ST)
        low = weighted.astype(BF)
        enter = spread(pack, EE)
        state = st_ref[...]
        low_state = state.astype(BF)
        states_ref[0, c] = low_state
        y = mm(bc_ref[rows, 128:], low_state) * enter
        locals_ = []
        for q in range(3):
            kernels = [(g * decay_kernel(pack, cumt, 2 * q + e)).astype(BF) for e in range(2)]
            locals_.append(mm(jnp.concatenate(kernels, 1), block_diag(low[:, 128 * q : 128 * q + 128])))
        y = y + jnp.concatenate(locals_, 1)
        out = weighted * spread(pack, FF)
        st_ref[...] = enter[L - 1 : L, :] * state + mm(bct_ref[c, pl.ds(0, 128), :], out.astype(BF))
        ssd = y + par[P_SKIP : P_SKIP + 1, :] * act
        gate = gate_ref[rows, :]
        gated = ssd * (gate * sigmoid(gate))
        gated_ref[rows, :] = gated
        sq = gated * gated
        ss_ref[rows, :] += sq[:, :128] + sq[:, 128:256] + sq[:, 256:]
        return 0

    lax.fori_loop(0, CH, chunk, 0)


def whole_spec(shape):
    return pl.BlockSpec(shape, lambda g: (0,) * len(shape))


def fwd(inner_pre, gate_pre, par, tok, bc, bct, gs, pack, cumt):
    cols = pl.BlockSpec((SEQ, GW), lambda g: (0, g))
    return pl.pallas_call(
        fwd_body,
        grid=(4,),
        out_shape=(
            jax.ShapeDtypeStruct((SEQ, 4 * GW), F32),
            jax.ShapeDtypeStruct((4, CH, 128, GW), BF),
            jax.ShapeDtypeStruct((SEQ, 128), F32),
        ),
        in_specs=[
            cols, cols, pl.BlockSpec((8, GW), lambda g: (0, g)),
            whole_spec((SEQ, 128)), whole_spec((SEQ, 256)), whole_spec((CH, 256, L)), whole_spec((CH, L, L)),
            pl.BlockSpec((1, SEQ, 128), lambda g: (g, 0, 0)),
            pl.BlockSpec((1, CH, 8, L), lambda g: (g, 0, 0, 0)),
        ],
        out_specs=(
            cols,
            pl.BlockSpec((1, CH, 128, GW), lambda g: (g, 0, 0, 0)),
            whole_spec((SEQ, 128)),
        ),
        scratch_shapes=[pltpu.VMEM((SEQ + 8, GW), F32), pltpu.VMEM((128, GW), F32)],
        compiler_params=pltpu.CompilerParams(vmem_limit_bytes=56 * 2**20),
        name="mixer_forward",
    )(inner_pre, gate_pre, par, tok, bc, bct, gs, pack, cumt)


def bwd_body(inner_ref, gate_ref, dinner_ref, par_ref, tok_ref, inv_ref, bc_ref, bct_ref, g_ref, pack_ref,
             cumt_ref, states_ref, decay_ref, state_pre_ref, convst_ref, row_ref,
             dgate_ref, dpre_ref, dstep_ref, dstate_ref, pgrad_ref, hgrad_ref, sgrad_ref,
             pad_ref, rt_ref, dg_ref, dbc_ref, spad_ref):
    group = pl.program_id(0)
    pad_ref[pl.ds(0, 8), :] = jnp.zeros((8, GW), F32)
    pad_ref[pl.ds(8, SEQ), :] = inner_ref[...]
    rt_ref[...] = jnp.zeros_like(rt_ref)
    pgrad_ref[...] = jnp.zeros_like(pgrad_ref)
    par = par_ref[...]
    decay = decay_ref[0]

    @pl.when(group == 0)
    def _():
        dg_ref[...] = jnp.zeros_like(dg_ref)
        dbc_ref[...] = jnp.zeros_like(dbc_ref)
        dstep_ref[...] = jnp.zeros_like(dstep_ref)
        hgrad_ref[...] = jnp.zeros_like(hgrad_ref)

    lane = lax.broadcasted_iota(jnp.int32, (L, L), 1)
    sub = lax.broadcasted_iota(jnp.int32, (L, L), 0)
    upper = (sub <= lane).astype(BF)
    per_head = (lax.broadcasted_iota(jnp.int32, (GW, 128), 0) >> 6
                == lax.broadcasted_iota(jnp.int32, (GW, 128), 1)).astype(BF)

    def head_sums(x):
        hi, lo = split2(x)
        return mm(hi, per_head) + mm(lo, per_head)

    def chunk(step, later):
        c = CH - 1 - step
        base = pl.multiple_of(c * L, L)
        rows = pl.ds(base, L)
        tok = tok_ref[rows, :]
        window = pad_ref[pl.ds(base, L + 8), :]
        u = conv_of(window, tok, par)
        su = sigmoid(u)
        act = u * su
        pack = pack_ref[0, rows, :]
        cumt = cumt_ref[0, c]
        g = g_ref[c]
        steps = spread(pack, ST)
        enter = spread(pack, EE)
        leave = spread(pack, FF)
        weighted = act * steps
        low = weighted.astype(BF)
        low_state = states_ref[0, c]
        bmat = bc_ref[rows, :128]
        cmat = bc_ref[rows, 128:]
        diags = [block_diag(low[:, 128 * q : 128 * q + 128]) for q in range(3)]
        decays = [decay_kernel(pack, cumt, h) for h in range(GH)]
        kernels = [jnp.concatenate([(g * decays[2 * q + e]).astype(BF) for e in range(2)], 1) for q in range(3)]
        y = mm(cmat, low_state) * enter + jnp.concatenate([mm(kernels[q], diags[q]) for q in range(3)], 1)
        skip = par[P_SKIP : P_SKIP + 1, :]
        ssd = y + skip * act
        gate = gate_ref[rows, :]
        sg = sigmoid(gate)
        silu = gate * sg
        scaled = dinner_ref[rows, :] * par[P_GAIN : P_GAIN + 1, :]
        inv = inv_ref[rows, :]
        d_gated = inv[:, 0:1] * scaled - (ssd * silu) * inv[:, 1:2]
        dy = d_gated * silu
        dgate_ref[rows, :] = (d_gated * ssd * sg * (1.0 + gate * (1.0 - sg))).astype(BF)
        dy_low = dy.astype(BF)
        dy_in = (dy * enter).astype(BF)
        rt = rt_ref[...]
        rt_low = rt.astype(BF)
        carried = mm(bmat, rt_low) * leave
        pieces = []
        d_scores = jnp.zeros((L, L), F32)
        for q in range(3):
            dq = dy_low[:, 128 * q : 128 * q + 128]
            dm = mm(dq, diags[q], ((1,), (1,)))
            d_scores = d_scores + dm[:, :L] * decays[2 * q] + dm[:, L:] * decays[2 * q + 1]
            both = mm(kernels[q], dq, ((0,), (0,)))
            pieces.append(jnp.where(lane < 64, both[:L], both[L:]))
        d_weighted = jnp.concatenate(pieces, 1) + carried
        dg_ref[c] += d_scores
        out = (weighted * leave).astype(BF)
        dbc_ref[rows, 128:] += mm(dy_in, low_state, ((1,), (1,)))
        dbc_ref[rows, :128] += mm(out, rt_low, ((1,), (1,)))
        keep = enter[L - 1 : L, :]
        low32 = low.astype(F32)
        d_cum = head_sums(dy_low.astype(F32) * y - low32 * d_weighted)
        at_end = jnp.sum(low32 * carried, 0, keepdims=True) + keep * jnp.sum(rt * low_state.astype(F32), 0, keepdims=True)
        d_last = head_sums(jnp.concatenate([at_end, jnp.zeros((7, GW), F32)], 0))[0:1, :]
        hi, mid, lo = split3(d_cum)
        d_log = mm(upper, hi) + mm(upper, mid) + mm(upper, lo) + d_last
        rt_ref[...] = keep * rt + mm(bct_ref[c, pl.ds(128, 128), :], dy_in)
        d_step = head_sums(act * d_weighted) + decay[0:1, :] * d_log
        heads = lane < GH
        d_step_pre = jnp.where(heads, d_step * jnp.roll(pack, -SG, 1), 0.0)
        dstep_ref[rows, :] += pltpu.roll(d_step_pre, GH * group, 1)
        rate = jnp.sum(jnp.where(heads, pack, 0.0) * d_log, 0, keepdims=True) * decay[0:1, :]
        offs = jnp.sum(d_step_pre, 0, keepdims=True)
        hgrad_ref[0:1, :] += pltpu.roll(jnp.concatenate([rate, jnp.zeros((7, 128), F32)], 0), GH * group, 1)[0:1]
        hgrad_ref[1:2, :] += pltpu.roll(jnp.concatenate([offs, jnp.zeros((7, 128), F32)], 0), GH * group, 1)[0:1]
        d_act = skip * dy + steps * d_weighted
        du = d_act * su * (1.0 + u * (1.0 - su))
        pgrad_ref[K : K + 1, :] += jnp.sum(du, 0, keepdims=True)
        pgrad_ref[P_SKIP : P_SKIP + 1, :] += jnp.sum(dy * act, 0, keepdims=True)
        for k in range(K):
            moved = back_conv_input(window, k)
            if k:
                moved = moved * tok[:, 2 + k : 3 + k]
            pgrad_ref[K - 1 - k : K - k, :] += jnp.sum(du * moved, 0, keepdims=True)
        ahead = jnp.concatenate([du, later], 0)
        d_pre = par[K - 1 : K, :] * du
        for k in range(1, K):
            d_pre = d_pre + par[K - 1 - k : K - k, :] * (ahead[k : k + L] * tok[:, 5 + k : 6 + k])
        dpre_ref[rows, :] = d_pre.astype(BF)
        return du[:8]

    lax.fori_loop(0, CH, chunk, jnp.zeros((8, GW), F32))

    @pl.when(group == pl.num_programs(0) - 1)
    def _():
        spad_ref[pl.ds(0, 8), :] = jnp.zeros((8, 256), F32)
        spad_ref[pl.ds(8, SEQ), :] = state_pre_ref[...]
        sgrad_ref[...] = jnp.zeros_like(sgrad_ref)
        cst = convst_ref[...]

        def last(step, later):
            c = CH - 1 - step
            base = pl.multiple_of(c * L, L)
            rows = pl.ds(base, L)
            tok = tok_ref[rows, :]
            same = (tok[:, 0:1] == row_ref[c][0:1, :]) & (sub >= lane)
            ds = jnp.where(same, dg_ref[c], 0.0).astype(BF)
            d_c = dbc_ref[rows, 128:] + mm(ds, bc_ref[rows, :128])
            d_b = dbc_ref[rows, :128] + mm(ds, bc_ref[rows, 128:], ((0,), (0,)))
            window = spad_ref[pl.ds(base, L + 8), :]
            w = conv_of(window, tok, cst)
            sw = sigmoid(w)
            dw = jnp.concatenate([d_b, d_c], 1) * (sw * (1.0 + w * (1.0 - sw)))
            sgrad_ref[K : K + 1, :] += jnp.sum(dw, 0, keepdims=True)
            for k in range(K):
                moved = back_conv_input(window, k)
                if k:
                    moved = moved * tok[:, 2 + k : 3 + k]
                sgrad_ref[K - 1 - k : K - k, :] += jnp.sum(dw * moved, 0, keepdims=True)
            ahead = jnp.concatenate([dw, later], 0)
            d_pre = cst[K - 1 : K, :] * dw
            for k in range(1, K):
                d_pre = d_pre + cst[K - 1 - k : K - k, :] * (ahead[k : k + L] * tok[:, 5 + k : 6 + k])
            dstate_ref[rows, :] = d_pre.astype(BF)
            return dw[:8]

        lax.fori_loop(0, CH, last, jnp.zeros((8, 256), F32))


def bwd(inner_pre, gate_pre, d_inner, par, tok, inv, bc, bct, gs, pack, cumt, states, decay, state_pre, convst, row):
    cols = pl.BlockSpec((SEQ, GW), lambda g: (0, g))
    pcol = pl.BlockSpec((8, GW), lambda g: (0, g))
    return pl.pallas_call(
        bwd_body,
        grid=(4,),
        out_shape=(
            jax.ShapeDtypeStruct((SEQ, 4 * GW), BF),
            jax.ShapeDtypeStruct((SEQ, 4 * GW), BF),
            jax.ShapeDtypeStruct((SEQ, 128), F32),
            jax.ShapeDtypeStruct((SEQ, 256), BF),
            jax.ShapeDtypeStruct((8, 4 * GW), F32),
            jax.ShapeDtypeStruct((8, 128), F32),
            jax.ShapeDtypeStruct((8, 256), F32),
        ),
        in_specs=[
            cols, cols, cols, pcol,
            whole_spec((SEQ, 128)), whole_spec((SEQ, 128)), whole_spec((SEQ, 256)), whole_spec((CH, 256, L)),
            whole_spec((CH, L, L)),
            pl.BlockSpec((1, SEQ, 128), lambda g: (g, 0, 0)),
            pl.BlockSpec((1, CH, 8, L), lambda g: (g, 0, 0, 0)),
            pl.BlockSpec((1, CH, 128, GW), lambda g: (g, 0, 0, 0)),
            pl.BlockSpec((1, 8, 128), lambda g: (g, 0, 0)),
            whole_spec((SEQ, 256)), whole_spec((8, 256)), whole_spec((CH, 8, L)),
        ],
        out_specs=(
            cols, cols, whole_spec((SEQ, 128)), whole_spec((SEQ, 256)), pcol, whole_spec((8, 128)), whole_spec((8, 256)),
        ),
        scratch_shapes=[
            pltpu.VMEM((SEQ + 8, GW), F32),
            pltpu.VMEM((128, GW), F32),
            pltpu.VMEM((CH, L, L), F32),
            pltpu.VMEM((SEQ, 256), F32),
            pltpu.VMEM((SEQ + 8, 256), F32),
        ],
        compiler_params=pltpu.CompilerParams(vmem_limit_bytes=56 * 2**20),
        name="mixer_backward",
    )(inner_pre, gate_pre, d_inner, par, tok, inv, bc, bct, gs, pack, cumt, states, decay, state_pre, convst, row)


def on_device(fsdp, halves, hidden_in, norm_gain, in_gate, in_inner, in_state, in_step, conv_inner, conv_inner_shift,
              conv_state, conv_state_shift, step_offset, log_rate, skip_gain, inner_gain, out_weight, segment_ids,
              grad_out):
    both = ("fsdp", "zz")
    depth, width = in_gate.shape
    model = depth * fsdp
    inner = width * halves
    heads_dev = in_step.shape[1]
    heads = heads_dev * halves
    heads_all = 2 * heads
    unit = conv_inner.shape[2] * fsdp
    inner_all = 2 * inner
    core = lax.axis_index("core")
    zz = lax.axis_index("zz")
    rows = hidden_in.shape[0]

    def swap(x):
        return lax.ppermute(x, "core", [(0, 1), (1, 0)])

    def both_cores(own, other):
        return jnp.where(core == 0, jnp.concatenate([own, other], 0), jnp.concatenate([other, own], 0))

    small = [norm_gain, in_step, conv_inner, conv_inner_shift, conv_state, conv_state_shift, step_offset, log_rate,
             skip_gain, inner_gain]
    flat = jnp.concatenate([v.reshape(-1) for v in small])
    got = lax.all_gather(flat, both, axis=0).reshape(fsdp, halves, -1)
    parts = []
    at = 0
    for v in small:
        parts.append(got[:, :, at : at + v.size].reshape((fsdp, halves) + v.shape))
        at += v.size
    gain_outer = parts[0][:, 0].reshape(model).astype(F32)
    step_cols = parts[1].transpose(0, 2, 1, 3).reshape(model, heads)
    conv_in = parts[2].transpose(2, 1, 3, 0, 4).reshape(K, inner).astype(F32)
    shift_in = parts[3].transpose(1, 2, 0, 3).reshape(1, inner).astype(F32)
    conv_st = parts[4][:, 0].transpose(1, 0, 2).reshape(K, -1).astype(F32)
    shift_st = parts[5][:, 0].reshape(1, -1).astype(F32)
    gain_in = parts[9].transpose(1, 2, 0, 3).reshape(1, inner).astype(F32)

    def my_heads(v):
        return v.reshape(halves, 2, heads_dev)[:, core].reshape(heads).astype(F32)

    offset = my_heads(parts[6][:, 0].reshape(heads_all))
    decay = -jnp.exp(my_heads(parts[7][:, 0].reshape(heads_all)))
    skip = my_heads(parts[8][:, 0].reshape(heads_all))
    state_cols = lax.all_gather(in_state, "fsdp", axis=0, tiled=True)

    def columns(w):
        return lax.all_gather(w, both, axis=0).reshape(fsdp, halves, depth, width).transpose(0, 2, 1, 3).reshape(model, inner)

    inner_cols = columns(in_inner)
    gate_cols = columns(in_gate)
    out_rows = lax.all_gather(out_weight, both, axis=0).reshape(fsdp, halves, width, depth).transpose(1, 2, 0, 3).reshape(inner, model)

    par = jnp.concatenate([conv_in, shift_in, jnp.repeat(skip, unit)[None], gain_in, jnp.zeros((1, inner), F32)], 0)
    convst = jnp.concatenate([conv_st, shift_st, jnp.zeros((3, 256), F32)], 0)
    head = jnp.pad(jnp.stack([offset, decay]), ((0, 6), (0, 128 - heads)))
    decay_g = jnp.pad(decay.reshape(heads // GH, 1, GH), ((0, 0), (0, 7), (0, 128 - GH)))

    docs = lax.dynamic_slice_in_dim(segment_ids, zz * SEQ, SEQ)
    blocks = docs.reshape(CH, L)
    prior = jnp.concatenate([jnp.full((1,), -1, docs.dtype), blocks[:-1, -1]])
    masks = [docs, (blocks == prior[:, None]).reshape(SEQ), (blocks == blocks[:, -1:]).reshape(SEQ)]
    for k in range(1, K):
        masks.append(jnp.concatenate([jnp.zeros((k,), bool), docs[k:] == docs[:-k]]))
    for k in range(1, K):
        masks.append(jnp.concatenate([docs[k:] == docs[:-k], jnp.zeros((k,), bool)]))
    tok = jnp.pad(jnp.stack([m.astype(F32) for m in masks], 1), ((0, 0), (0, 128 - len(masks))))
    row = jnp.broadcast_to(blocks.astype(F32)[:, None, :], (CH, 8, L))

    hidden_all = both_cores(hidden_in, swap(hidden_in)).astype(F32)
    cot_all = both_cores(grad_out, swap(grad_out))
    inv_rms = lax.rsqrt(jnp.mean(hidden_all * hidden_all, -1, keepdims=True) + EPSILON)
    normed = (hidden_all * inv_rms * gain_outer).astype(BF)
    small_cols = jnp.concatenate([state_cols, jnp.pad(step_cols, ((0, 0), (0, 128 - heads)))], 1)
    pre_small = mm(normed, small_cols)
    state_pre = pre_small[:, :256]
    step_pre = pre_small[:, 256:]
    inner_pre = mm(normed, inner_cols)
    gate_pre = mm(normed, gate_cols)
    bc, bct, gs, pack, cumt = prep(state_pre, step_pre, tok, row, convst, head)
    gated, states, ss = fwd(inner_pre, gate_pre, par, tok, bc, bct, gs, pack, cumt)
    ss_own = jnp.sum(ss, -1)
    squares = ss_own + swap(ss_own)
    inner_inv = lax.rsqrt(squares / inner_all + EPSILON)[:, None]
    normed_inner = (gated * inner_inv * gain_in).astype(BF)
    mixed = mm(normed_inner, out_rows)

    def to_own(x):
        own = lax.dynamic_slice_in_dim(x, core * rows, rows)
        other = lax.dynamic_slice_in_dim(x, (1 - core) * rows, rows)
        return own + swap(other.astype(BF)).astype(F32)

    layer_out = (hidden_in.astype(F32) + to_own(mixed)).astype(BF)
    grad_out_part = mm(normed_inner, cot_all, ((0,), (0,)))
    d_inner = mm(cot_all, out_rows, ((1,), (1,)))
    grad_gain_in = jnp.sum(d_inner * gated * inner_inv, 0)
    prod_own = jnp.sum(gated * d_inner * gain_in, -1)
    products = prod_own + swap(prod_own)
    inv_pack = jnp.pad(
        jnp.stack([inner_inv[:, 0], inner_inv[:, 0] ** 3 * products / inner_all], 1), ((0, 0), (0, 126))
    )
    d_gate, d_pre, d_step, d_state, pgrad, hgrad, sgrad = bwd(
        inner_pre, gate_pre, d_inner, par, tok, inv_pack, bc, bct, gs, pack, cumt, states, decay_g, state_pre, convst, row
    )
    d_step = d_step.astype(BF)
    d_small = jnp.concatenate([d_state, d_step], 1)
    d_normed = to_own(
        mm(d_gate, gate_cols, ((1,), (1,))) + mm(d_pre, inner_cols, ((1,), (1,))) + mm(d_small, small_cols, ((1,), (1,)))
    )
    hidden = hidden_in.astype(F32)
    inv_own = lax.dynamic_slice_in_dim(inv_rms, core * rows, rows)
    grad_gain_outer = jnp.sum(d_normed * hidden * inv_own, 0)
    weighted_back = d_normed * gain_outer
    d_hidden = inv_own * weighted_back - hidden * inv_own**3 * jnp.mean(hidden * weighted_back, -1, keepdims=True)
    grad_hidden = (grad_out.astype(F32) + d_hidden).astype(BF)

    def scatter_columns(g):
        g = g.astype(BF).reshape(fsdp, depth, halves, width).transpose(0, 2, 1, 3).reshape(fsdp * halves, depth, width)
        return lax.psum_scatter(g, both, scatter_dimension=0).astype(F32)

    grad_gate = scatter_columns(mm(normed, d_gate, ((0,), (0,))))
    grad_inner = scatter_columns(mm(normed, d_pre, ((0,), (0,))))
    grad_small = mm(normed, d_small, ((0,), (0,)))
    grad_out_weight = grad_out_part.astype(BF).reshape(halves, width, fsdp, depth).transpose(2, 0, 1, 3)
    grad_out_weight = lax.psum_scatter(
        grad_out_weight.reshape(fsdp * halves, width, depth), both, scatter_dimension=0
    ).astype(F32)
    grad_state = lax.psum_scatter(grad_small[:, :256].astype(BF), "fsdp", scatter_dimension=0, tiled=True)
    grad_state = lax.psum(grad_state, ("zz", "core")).astype(F32)

    own_heads = [
        grad_small[:, 256 : 256 + heads].reshape(fsdp, depth, halves, heads_dev).transpose(0, 2, 1, 3),
        pgrad[:K].reshape(K, halves, heads_dev, fsdp, -1).transpose(3, 1, 0, 2, 4),
        pgrad[K].reshape(halves, heads_dev, fsdp, -1).transpose(2, 0, 1, 3),
        grad_gain_in.reshape(halves, heads_dev, fsdp, -1).transpose(2, 0, 1, 3),
    ]
    sizes = [v.shape[2:] for v in own_heads]
    stacked = jnp.concatenate([v.reshape(fsdp * halves, -1) for v in own_heads], 1)
    mine = lax.psum_scatter(stacked, both, scatter_dimension=0)
    outs = []
    at = 0
    for s in sizes:
        n = 1
        for d in s:
            n *= d
        outs.append(mine[at : at + n].reshape(s))
        at += n
    grad_step, grad_conv_in, grad_conv_in_shift, grad_gain_inner = outs

    def place(v):
        v = v.reshape(halves, 1, heads_dev)
        zero = jnp.zeros_like(v)
        return jnp.where(core == 0, jnp.concatenate([v, zero], 1), jnp.concatenate([zero, v], 1)).reshape(heads_all)

    skip_sum = jnp.sum(pgrad[P_SKIP].reshape(heads, unit), 1)
    shared = [grad_gain_outer.reshape(fsdp, depth), sgrad[:K].reshape(K, fsdp, -1).transpose(1, 0, 2), sgrad[K].reshape(fsdp, -1)]
    shared += [place(v).reshape(fsdp, -1) for v in (hgrad[1, :heads], hgrad[0, :heads], skip_sum)]
    sizes = [v.shape[1:] for v in shared]
    stacked = jnp.concatenate([v.reshape(fsdp, -1) for v in shared], 1)
    mine = lax.psum(stacked, ("fsdp", "zz", "core"))
    mine = lax.dynamic_index_in_dim(mine, lax.axis_index("fsdp"), keepdims=False)
    outs = []
    at = 0
    for s in sizes:
        n = 1
        for d in s:
            n *= d
        outs.append(mine[at : at + n].reshape(s))
        at += n
    grad_norm_gain, grad_conv_st, grad_conv_st_shift, grad_offset, grad_rate, grad_skip = outs
    return (layer_out, grad_hidden, grad_norm_gain, grad_gate, grad_inner, grad_state, grad_step, grad_conv_in,
            grad_conv_in_shift, grad_conv_st, grad_conv_st_shift, grad_offset, grad_rate, grad_skip, grad_gain_inner,
            grad_out_weight)


def solution(mesh):
    fsdp = mesh.shape["fsdp"]
    halves = mesh.shape["tensor"] // 2
    fine = jax.sharding.Mesh(mesh.devices.reshape(fsdp, halves, 2), ("fsdp", "zz", "core"))
    tensor = ("zz", "core")
    tokens = P(("fsdp", "zz", "core"), None)
    grid = P("fsdp", tensor)
    heads = P(tensor, "fsdp")
    return jax.shard_map(
        functools.partial(on_device, fsdp, halves),
        mesh=fine,
        in_specs=(
            tokens, P("fsdp"), grid, grid, P("fsdp", None), grid, P(None, tensor, "fsdp"), heads, P(None, "fsdp"),
            P("fsdp"), P("fsdp"), P("fsdp"), P("fsdp"), heads, heads, P("fsdp"), tokens,
        ),
        out_specs=(
            tokens, tokens, P("fsdp"), grid, grid, P("fsdp", None), grid, P(None, tensor, "fsdp"), heads,
            P(None, "fsdp"), P("fsdp"), P("fsdp"), P("fsdp"), P("fsdp"), heads, heads,
        ),
        check_vma=False,
    )
```

time: 1910 us -> 1100 us (0.58)
  other arithmetic: 433 us -> 25.4 us
  matrix products: 390 us -> 98 us
  local copies, waits for them, and re-layouts: 336 us -> 132 us
  waiting for transfers between devices: 535 us -> 663 us
  Pallas kernels: 0 us -> 106 us
  blocking collectives: 139 us -> 54.3 us
  loops' own time: 48.8 us -> 0 us
    dot_general x116 -> x12, matrix products: 390 us -> 98 us  [mm(): return lax.dot_general(a, b, (dims, ((), ())), preferred_element_type=F32)]
    another operation x50 -> x5, other arithmetic: 181 us -> 1.51 us  [the longest x1 1.27 us: on_device(): head = jnp.pad(jnp.stack([offset, decay]), ((0, 6), (0, 128 - heads)))]
    pallas_call x0 -> x3, Pallas kernels: none -> 106 us  [the longest x1 65.6 us: bwd(): pl.pallas_call(bwd_body, grid=(4,), out_shape=(jax.ShapeDtypeStruct((SEQ,...]
    unnamed x16 -> x13, waiting for transfers between devices: 3.13 us -> 104 us
    slice x130 -> x22, local copies, waits for them, and re-layouts: 86 us -> 13 us  [the longest x7 6.39 us: on_device(): outs.append(mine[at:at + n].reshape(s))]
    while x1443 -> x0, local copies, waits for them, and re-layouts: 72.9 us -> none
    reduce_sum x41 -> x4, other arithmetic: 70.7 us -> 7.13 us  [the longest x1 3.01 us: on_device(): grad_gain_outer = jnp.sum(d_normed * hidden * inv_own, 0)]
    psum x1, waiting for transfers between devices: 55.5 us -> 0.01 us  [on_device(): grad_state = lax.psum(grad_state, ('zz', 'core')).astype(F32)]
  transfers between devices with their start and end apart: 15 -> 16, of which waited for: 10 -> 10; matrix products, arithmetic and copies ran while one was open for 18% -> 20% of each run, Pallas kernels for 0% -> 4%
where the time goes in v1:
time: 1100 us
  waiting for transfers between devices  663 us (60%)
  local copies, waits for them, and re-layouts  132 us (12%)
  Pallas kernels  106 us (10%)
  matrix products  98 us (9%)
  blocking collectives  54.3 us (5%)
  other arithmetic  25.4 us (2%)
  between operations  16 us (1%)
    reduce_scatter x2, waiting for transfers between devices, scatter_columns(): return lax.psum_scatter(g, both, scatter_dimension=0).astype(F32)  280 us
    reduce_scatter x1, waiting for transfers between devices, on_device(): lax.psum_scatter(grad_out_weight.reshape(fsdp * halves, width, depth), bo...  138 us
    all_gather x2, waiting for transfers between devices, columns(): lax.all_gather(w, both, axis=0).reshape(fsdp, halves, depth, width)  110 us
    unnamed x13, waiting for transfers between devices  104 us
    dot_general x12, matrix products, mm(): return lax.dot_general(a, b, (dims, ((), ())), preferred_element_type=F32)  98 us
    pallas_call x1, Pallas kernels, bwd(): pl.pallas_call(bwd_body, grid=(4,), out_shape=(jax.ShapeDtypeStruct((SEQ,...  65.6 us
    psum x1, blocking collectives, on_device(): mine = lax.psum(stacked, ('fsdp', 'zz', 'core'))  39.6 us
    pallas_call x1, Pallas kernels, fwd(): pl.pallas_call(fwd_body, grid=(4,), out_shape=(jax.ShapeDtypeStruct((SEQ,...  31.7 us
  transfers between devices with their start and end apart: 16, of which 10 were waited for; matrix products, arithmetic and copies ran while one was open for 20% of the time, Pallas kernels for 4%

profile of v1, /device:TPU:0, one launch (start us, length us, event | category | flops | bytes accessed | tf_op | source)
XLA Modules:
  0.0 1095.9 jit_solution(9296954134198029949)
XLA Ops:
  24.6 14.7 %all_gather.33 = bf16[1536,256]{1,0:T(8,128)(2,1)} all-gather(bf16[384,256]{1,0:T(8,128)(2,1)S(1)} %copy-done.15), channel_id=1, replica_groups=mesh['fsdp'=4,'zz'=4,'core'=2] {'fsdp'}, dimensions={0}, use_global_device_ids=true | all-gather | bytes 983040 | tf_op jit(solution)/shard_map/all_gather | solution.py:463
  39.3 85.5 %all-reduce.23.cloned.1.call-done = bf16[57920]{0:T(1024)(128)(2,1)} async-done(((bf16[57920]{0:T(1024)(128)(2,1)}), bf16[57920]{0:T(1024)(128)(2,1)}) %all-reduce.23.cloned.1.call-update) | async-done | bytes 115856
  151.4 9.1 prep.1
  160.5 46.7 %all-gather.10.cloned.1.call-done = bf16[6144,384]{1,0:T(8,128)(2,1)} async-done(((bf16[384,384]{1,0:T(8,128)(2,1)}), bf16[6144,384]{1,0:T(8,128)(2,1)}) %all-gather.10.cloned.1.call-update) | async-done | bytes 4718608 | tf_op jit(solution)/shard_map/all_gather | solution.py:466
  216.2 9.8 fusion.39.gate_ref
  226.0 63.1 %all-gather.8.cloned.1.call-done = bf16[6144,384]{1,0:T(8,128)(2,1)} async-done(((bf16[384,384]{1,0:T(8,128)(2,1)}), bf16[6144,384]{1,0:T(8,128)(2,1)}) %all-gather.8.cloned.1.call-update) | async-done | bytes 4718608 | tf_op jit(solution)/shard_map/all_gather | solution.py:466
  296.4 11.4 %fusion.41.inner_ref = f32[1024,1536]{1,0:T(8,128)} fusion(bf16[1536,1536]{1,0:T(8,128)(2,1)S(1)} %bitcast.117, f32[1536]{0:T(1024)S(1)} %reshape.402, f32[1024]{0:T(1024)S(1)} %add_rsqrt_fusion.1, bf16[512,1536]{1,0:T(8,128)(2,1)S(1)} %copy-done.1, bf16[512,1536]{1,0:T(8,128)(2,1)} %collective-permute-done, pred[]{:T(512)S(6)} %eq.43), kind=kOutput, calls=%fused_computation.116 | convolution fusion | flops 4852285440 | bytes 14166017 | tf_op jit(solution)/shard_map/dot_general | solution.py:24
  307.7 31.7 %mixer_forward.1 = (f32[1024,1536]{1,0:T(8,128)}, bf16[4,8,128,384]{3,2,1,0:T(8,128)(2,1)}, f32[1024,128]{1,0:T(8,128)}) custom-call(f32[1024,1536]{1,0:T(8,128)} %fusion.41.inner_ref, f32[1024,1536]{1,0:T(8,128)} %fusion.39.gate_ref, f32[8,1536]{1,0:T(8,128)} %concatenate.91.par_ref, f32[1024,128]{1,0:T(8,128)} %pad.30.tok_ref, ...), custom_call_target="tpu_custom_call" | custom-call | tf_op jit(solution)/shard_map/mixer_forward/pallas_call | solution.py:202
  341.0 29.8 %all-gather.12.cloned.1.call-done = bf16[6144,384]{1,0:T(8,128)(2,1)} async-done(((bf16[384,384]{1,0:T(8,128)(2,1)}), bf16[6144,384]{1,0:T(8,128)(2,1)}) %all-gather.12.cloned.1.call-update) | async-done | bytes 4718608 | tf_op jit(solution)/shard_map/all_gather | solution.py:470
  378.2 12.9 %multiply_reduce_fusion = (f32[1536]{0:T(1024)}, f32[1024]{0:T(1024)S(1)}, f32[1024,1536]{1,0:T(8,128)}) fusion(f32[1024]{0:T(1024)S(1)} %add_rsqrt_fusion, f32[1024,1536]{1,0:T(8,128)} %get-tuple-element.36, f32[1536]{0:T(1024)S(1)} %reshape.416, bf16[1536,1536]{1,0:T(8,128)(2,1)S(1)} %bitcast.119, bf16[512,1536]{1,0:T(8,128)(2,1)} %collective-permute-done.3, ...), kind=kOutput, calls=%fused_computation.8 | convolution fusion | flops 4853855744 | bytes 20467712 | tf_op jit(solution)/shard_map/dot_general | solution.py:24
  393.4 65.6 %mixer_backward.1 = (bf16[1024,1536]{1,0:T(8,128)(2,1)}, bf16[1024,1536]{1,0:T(8,128)(2,1)}, f32[1024,128]{1,0:T(8,128)}, bf16[1024,256]{1,0:T(8,128)(2,1)}, f32...) custom-call(f32[1024,1536]{1,0:T(8,128)} %fusion.41.inner_ref, f32[1024,1536]{1,0:T(8,128)} %fusion.39.gate_ref, ...), custom_call_target="tpu_custom_call" | custom-call | tf_op jit(solution)/shard_map/mixer_backward/pallas_call | solution.py:381
  478.9 13.1 %reduce-scatter.13.cloned.1.call-done = bf16[384,256]{1,0:T(8,128)(2,1)} async-done(((bf16[1536,256]{1,0:T(8,128)(2,1)}), bf16[384,256]{1,0:T(8,128)(2,1)}) %reduce-scatter.13.cloned.1.call-update) | async-done | bytes 196624
  493.8 11.5 %convolution_convert_fusion = bf16[1536,1536]{1,0:T(8,128)(2,1)} fusion(bf16[512,1536]{1,0:T(8,128)(2,1)} %collective-permute-done.3, bf16[512,1536]{1,0:T(8,128)(2,1)} %param.33, pred[]{:T(512)S(6)} %eq.43, f32[1024,1536]{1,0:T(8,128)} %get-tuple-element.36, f32[1536]{0:T(1024)S(1)} %copy-done.19, f32[1024]{0:T(1024)S(1)} %add_rsqrt_fusion), kind=kOutput, calls=%fused_computation.2 | convolution fusion | flops 4853071872 | bytes 14166017 | tf_op jit(solution)/shard_map/dot_general | solution.py:24
  505.3 9.1 reshape.400
  519.7 9.5 convolution_convert_fusion.2
  529.3 9.1 reshape.384
  543.8 9.8 convolution_convert_fusion.1
  553.6 9.1 reshape.386
  568.1 8.0 fusion.45
  586.7 8.8 fusion.34
  615.0 39.6 %psum.14 = f32[4,740]{1,0:T(4,128)S(1)} all-reduce(f32[4,740]{1,0:T(4,128)S(1)} %concatenate.111), channel_id=1, replica_groups=mesh['fsdp'=4,'zz'=4,'core'=2] {'fsdp','zz','core'}, use_global_device_ids=true, to_apply=%region_6.7 | all-reduce | flops 2960 | bytes 23680 | tf_op jit(solution)/shard_map/psum | solution.py:578
  664.6 138.0 %reduce-scatter.11.cloned.1.call-done = bf16[1,384,384]{2,1,0:T(8,128)(2,1)} async-done(((bf16[16,384,384]{2,1,0:T(8,128)(2,1)}), bf16[1,384,384]{2,1,0:T(8,128)(2,1)}) %reduce-scatter.11.cloned.1.call-update) | async-done | bytes 294928 | tf_op jit(solution)/shard_map/reduce_scatter | solution.py:543
  804.5 140.7 %reduce-scatter.7.cloned.1.call-done = bf16[1,384,384]{2,1,0:T(8,128)(2,1)} async-done(((bf16[16,384,384]{2,1,0:T(8,128)(2,1)}), bf16[1,384,384]{2,1,0:T(8,128)(2,1)}) %reduce-scatter.7.cloned.1.call-update) | async-done | bytes 294928 | tf_op jit(solution)/shard_map/reduce_scatter | solution.py:537
  947.0 139.7 %reduce-scatter.9.cloned.1.call-done = bf16[1,384,384]{2,1,0:T(8,128)(2,1)} async-done(((bf16[16,384,384]{2,1,0:T(8,128)(2,1)}), bf16[1,384,384]{2,1,0:T(8,128)(2,1)}) %reduce-scatter.9.cloned.1.call-update) | async-done | bytes 294928 | tf_op jit(solution)/shard_map/reduce_scatter | solution.py:537
  (252 shorter events, 153.6 us)
Async XLA Ops:
  7.2 17.4 %copy-start.15 = (bf16[384,256]{1,0:T(8,128)(2,1)S(1)}, bf16[384,256]{1,0:T(8,128)(2,1)}, u32[]{:S(2)}) copy-start(bf16[384,256]{1,0:T(8,128)(2,1)} %param.21) | copy-start | bytes 589828
  7.2 117.6 %all-reduce.23.cloned.1.call-start = ((), (), s32[]{:S(2)}) async-start(), calls=%async_computation.11 | async-start | bytes 233472
  17.8 189.4 %all-gather.10.cloned.1.call-start = ((), (), s32[]{:S(2)}) async-start(), calls=%async_computation.9 | async-start | bytes 5013504 | tf_op jit(solution)/shard_map/all_gather | solution.py:466
  18.6 270.5 %all-gather.8.cloned.1.call-start = ((), (), s32[]{:S(2)}) async-start(), calls=%async_computation.8 | async-start | bytes 5013504 | tf_op jit(solution)/shard_map/all_gather | solution.py:466
  19.3 351.5 %all-gather.12.cloned.1.call-start = ((), (), s32[]{:S(2)}) async-start(), calls=%async_computation.10 | async-start | bytes 5013504 | tf_op jit(solution)/shard_map/all_gather | solution.py:470
  19.9 472.1 %reduce-scatter.13.cloned.1.call-start = ((), (), s32[]{:S(2)}) async-start(), calls=%async_computation.12 | async-start | bytes 983040
  20.0 357.8 %collective-permute-start.3 = (bf16[512,1536]{1,0:T(8,128)(2,1)}, bf16[512,1536]{1,0:T(8,128)(2,1)}, u32[]{:S(2)}, u32[]{:S(2)}) collective-permute-start(bf16[512,1536]{1,0:T(8,128)(2,1)} %param.33), channel_id=1, source_target_pairs={{0,1},{1,0},{2,3},{3,2},{4,5},{5,4},{6,7},{7,6},{8,9},{9,8},{10,11... | collective-permute-start | bytes 4718600 | tf_op jit(solution)/shard_map/ppermute | solution.py:435
  20.5 122.1 %collective-permute-start = (bf16[512,1536]{1,0:T(8,128)(2,1)}, bf16[512,1536]{1,0:T(8,128)(2,1)}, u32[]{:S(2)}, u32[]{:S(2)}) collective-permute-start(bf16[512,1536]{1,0:T(8,128)(2,1)} %param.17), channel_id=1, source_target_pairs={{0,1},{1,0},{2,3},{3,2},{4,5},{5,4},{6,7},{7,6},{8,9},{9,8},{10,11... | collective-permute-start | bytes 4718600 | tf_op jit(solution)/shard_map/ppermute | solution.py:435
  39.3 103.3 %copy-start.1 = (bf16[512,1536]{1,0:T(8,128)(2,1)S(1)}, bf16[512,1536]{1,0:T(8,128)(2,1)}, u32[]{:S(2)}) copy-start(bf16[512,1536]{1,0:T(8,128)(2,1)} %param.17) | copy-start | bytes 4718596
  307.7 33.2 %copy-start.13 = (f32[4,6,4,16]{3,2,1,0:T(4,128)S(1)}, f32[4,6,4,16]{3,2,1,0:T(4,128)}, u32[]{:S(2)}) copy-start(f32[4,6,4,16]{3,2,1,0:T(4,128)} %copy-done.12) | copy-start | bytes 18436
  340.8 36.9 %collective-permute-start.1 = (f32[1024]{0:T(1024)S(1)}, f32[1024]{0:T(1024)S(1)}, u32[]{:S(2)}, u32[]{:S(2)}) collective-permute-start(f32[1024]{0:T(1024)S(1)} %reduce_sum.64), channel_id=1, source_target_pairs={{0,1},{1,0},{2,3},{3,2},{4,5},{5,4},{6,7},{7,6},{8,9},{9,8},{10,11... | collective-permute-start | bytes 12296 | tf_op jit(solution)/shard_map/ppermute | solution.py:435
  341.0 36.7 %copy-start.18 = (f32[1536]{0:T(1024)}, f32[1536]{0:T(1024)S(1)}, u32[]{:S(2)}) copy-start(f32[1536]{0:T(1024)S(1)} %reshape.416) | copy-start | bytes 18436
  377.7 13.4 %copy-start.4 = (bf16[192,8,4,384]{3,1,2,0:T(8,128)(2,1)}, bf16[192,8,4,384]{3,1,2,0:T(8,128)(2,1)S(1)}, u32[]{:S(2)}) copy-start(bf16[192,8,4,384]{3,1,2,0:T(8,128)(2,1)S(1)} %copy.158) | copy-start | bytes 14155780
  378.2 12.9 %copy-start.21 = (f32[4,1,6]{2,1,0:T(1,128)S(1)}, f32[4,1,6]{2,1,0:T(1,128)}, u32[]{:S(2)}) copy-start(f32[4,1,6]{2,1,0:T(1,128)} %get-tuple-element.124) | copy-start | bytes 292
  391.1 1.2 collective-permute-start.4
  467.1 137.3 %all-reduce.25.cloned.1.call-start = ((), (), s32[]{:S(2)}) async-start(), calls=%async_computation.13 | async-start | bytes 376832
  471.8 22.0 %copy-start.19 = (f32[1536]{0:T(1024)S(1)}, f32[1536]{0:T(1024)}, u32[]{:S(2)}) copy-start(f32[1536]{0:T(1024)} %copy-done.18) | copy-start | bytes 18436
  478.9 184.0 %all-reduce.21.cloned.1.call-start = ((), (), s32[]{:S(2)}) async-start(), calls=%async_computation.6 | async-start | bytes 393216 | tf_op jit(solution)/shard_map/psum | solution.py:547
  493.8 308.9 %reduce-scatter.11.cloned.1.call-start = ((), (), s32[]{:S(2)}) async-start(), calls=%async_computation.7 | async-start | bytes 5013504 | tf_op jit(solution)/shard_map/reduce_scatter | solution.py:543
  519.7 425.5 %reduce-scatter.7.cloned.1.call-start = ((), (), s32[]{:S(2)}) async-start(), calls=%async_computation.4 | async-start | bytes 5013504 | tf_op jit(solution)/shard_map/reduce_scatter | solution.py:537
  543.7 543.1 %reduce-scatter.9.cloned.1.call-start = ((), (), s32[]{:S(2)}) async-start(), calls=%async_computation.5 | async-start | bytes 5013504 | tf_op jit(solution)/shard_map/reduce_scatter | solution.py:537
  568.1 18.6 %slice-start = ((s8[4718592]{0:T(1024)(128)(4,1)}), s8[4194304]{0:T(1024)(128)(4,1)S(1)}, s32[]{:S(2)}) async-start(s8[4718592]{0:T(1024)(128)(4,1)} %bitcast.120), calls=%async_computation.14 | async-start | bytes 8388608
  586.7 25.2 %collective-permute-start.5 = (bf16[512,1536]{1,0:T(8,128)(2,1)}, bf16[512,1536]{1,0:T(8,128)(2,1)S(1)}, u32[]{:S(2)}, u32[]{:S(2)}) collective-permute-start(bf16[512,1536]{1,0:T(8,128)(2,1)} %dynamic-slice_convert_fusion), channel_id=1, source_target_pairs={{0,1},{1,0},{2,3},{3,2},{4,5},{5,4},{6,7},{7,6},{8,9},{9,8},{10,11... | collective-permute-start | bytes 4718600 | tf_op jit(solution)/shard_map/ppermute | solution.py:435
  598.6 58.5 %collective-permute-start.2 = (bf16[512,1536]{1,0:T(8,128)(2,1)}, bf16[512,1536]{1,0:T(8,128)(2,1)}, u32[]{:S(2)}, u32[]{:S(2)}) collective-permute-start(bf16[512,1536]{1,0:T(8,128)(2,1)} %dynamic-slice_convert_fusion.1), channel_id=1, source_target_pairs={{0,1},{1,0},{2,3},{3,2},{4,5},{5,4},{6,7},{7,6},{8,9},{9,8},{10,11... | collective-permute-start | bytes 4718600 | tf_op jit(solution)/shard_map/ppermute | solution.py:435
  (18 other events, 83.0 us)
Sparse Core Ops, SparseCore 0:
  18.0 106.7 all-reduce.22
  127.5 79.6 all-gather.9
  210.0 79.0 all-gather.7
  291.7 79.0 all-gather.11
  467.2 24.7 reduce-scatter.12
  497.7 106.6 all-reduce.24
  607.4 53.6 all-reduce.20
  666.3 136.3 reduce-scatter.10
  808.7 136.5 reduce-scatter.6
  950.2 136.4 reduce-scatter.8

commit v2 on v1

--- a/solution.py
+++ b/solution.py
@@ -415,6 +415,1102 @@
     )(inner_pre, gate_pre, d_inner, par, tok, inv, bc, bct, gs, pack, cumt, states, decay, state_pre, convst, row)
 
 
+def prep_chunks(state_ref, step_ref, tok_ref, row_ref, convst_ref, head_ref,
+                bc_ref, bct_ref, g_ref, pack_ref, cumt_ref, pad_ref):
+    pad_ref[pl.ds(0, 8), :] = jnp.zeros((8, 256), F32)
+    pad_ref[pl.ds(8, SEQ), :] = state_ref[...]
+    lane = lax.broadcasted_iota(jnp.int32, (L, L), 1)
+    sub = lax.broadcasted_iota(jnp.int32, (L, L), 0)
+    tri = (sub >= lane).astype(BF)
+    offset = head_ref[0:1, :]
+    decay = head_ref[1:2, :]
+    convst = convst_ref[...]
+
+    def chunk(c, _):
+        base = pl.multiple_of(c * L, L)
+        rows = pl.ds(base, L)
+        tok = tok_ref[rows, :]
+        total = conv_of(pad_ref[pl.ds(base, L + 8), :], tok, convst)
+        act = total * sigmoid(total)
+        low = act.astype(BF)
+        bc_ref[rows, :] = low
+        bct_ref[c] = jnp.concatenate([act[:, :128].T, act[:, 128:].T], 0).astype(BF)
+        scores = mm(low[:, 128:], low[:, :128], ((1,), (1,)))
+        same = (tok[:, 0:1] == row_ref[pl.ds(c, 1), :]) & (sub >= lane)
+        g_ref[c] = jnp.where(same, scores, 0.0)
+        v = step_ref[rows, :] + offset
+        steps = jnp.maximum(v, 0.0) + jnp.log1p(jnp.exp(-jnp.abs(v)))
+        logs = steps * (decay * LOG2E)
+        hi, mid, lo = split3(logs)
+        cum = mm(tri, hi) + mm(tri, mid) + mm(tri, lo)
+        last = cum[L - 1 : L, :]
+        enter = jnp.exp2(cum) * tok[:, 1:2]
+        leave = jnp.exp2(last - cum) * tok[:, 2:3]
+        sig = sigmoid(v)
+        cumt = cum.T
+        for g in range(4):
+            part = slice(16 * g, 16 * g + 8)
+            pieces = [values[:, part] for values in (steps, cum, enter, leave, sig)]
+            pieces.append(jnp.zeros((L, 88), F32))
+            pack_ref[g, rows, :] = jnp.concatenate(pieces, 1)
+            cumt_ref[g, c] = cumt[part, :]
+        return 0
+
+    lax.fori_loop(0, CH, chunk, 0)
+
+
+def fwd_chunks(pre_ref, par_ref, tok_ref, bc_ref, bct_ref, g_ref, pack_ref, cumt_ref,
+               gated_ref, states_ref, ss_ref, st_ref):
+    st_ref[...] = jnp.zeros_like(st_ref)
+    par = par_ref[...]
+
+    def chunk(c, _):
+        base = pl.multiple_of(c * L, L)
+        rows = pl.ds(base, L)
+        tok = tok_ref[rows, :]
+        u = conv_of(pre_ref[pl.ds(base, L + 8), :GW], tok, par)
+        act = u * sigmoid(u)
+        pack = pack_ref[rows, :]
+        cumt = cumt_ref[c]
+        g = g_ref[c]
+        weighted = act * spread(pack, ST)
+        low = weighted.astype(BF)
+        enter = spread(pack, EE)
+        state = st_ref[...]
+        low_state = state.astype(BF)
+        states_ref[c] = low_state
+        y = mm(bc_ref[rows, 128:], low_state) * enter
+        locals_ = []
+        for q in range(3):
+            kernels = [(g * decay_kernel(pack, cumt, 2 * q + e)).astype(BF) for e in range(2)]
+            locals_.append(mm(jnp.concatenate(kernels, 1), block_diag(low[:, 128 * q : 128 * q + 128])))
+        y = y + jnp.concatenate(locals_, 1)
+        out = weighted * spread(pack, FF)
+        st_ref[...] = enter[L - 1 : L, :] * state + mm(bct_ref[c, pl.ds(0, 128), :], out.astype(BF))
+        ssd = y + par[P_SKIP : P_SKIP + 1, :] * act
+        gate = pre_ref[pl.ds(base + 8, L), GW:]
+        gated = ssd * (gate * sigmoid(gate))
+        gated_ref[rows, :] = gated.astype(BF)
+        sq = gated * gated
+        ss_ref[rows, :] += sq[:, :128] + sq[:, 128:256] + sq[:, 256:]
+        return 0
+
+    lax.fori_loop(0, CH, chunk, 0)
+
+
+def bwd_chunks(group, z_k, tick, pre_ref, dinner_ref, par_ref, tok_ref, inv_ref, bc_ref, bct_ref, g_ref, pack_ref,
+               cumt_ref, states_ref, hpar_ref, dcat_ref, dstep_ref, pgrad_ref, hgrad_ref, rt_ref, dg_ref, dbc_ref):
+    rt_ref[...] = jnp.zeros_like(rt_ref)
+    pgrad_ref[...] = jnp.zeros_like(pgrad_ref)
+    par = par_ref[...]
+    decay = pltpu.roll(hpar_ref[...], (128 - 16 * group) % 128, 1)[1:2, :]
+    lane = lax.broadcasted_iota(jnp.int32, (L, L), 1)
+    sub = lax.broadcasted_iota(jnp.int32, (L, L), 0)
+    upper = (sub <= lane).astype(BF)
+    per_head = (lax.broadcasted_iota(jnp.int32, (GW, 128), 0) >> 6
+                == lax.broadcasted_iota(jnp.int32, (GW, 128), 1)).astype(BF)
+
+    def head_sums(x):
+        hi, lo = split2(x)
+        return mm(hi, per_head) + mm(lo, per_head)
+
+    def chunk(step, later):
+        tick(step)
+        c = CH - 1 - step
+        base = pl.multiple_of(c * L, L)
+        rows = pl.ds(base, L)
+        tok = tok_ref[rows, :]
+        window = pre_ref[pl.ds(base, L + 8), :GW]
+        u = conv_of(window, tok, par)
+        su = sigmoid(u)
+        act = u * su
+        pack = pack_ref[rows, :]
+        cumt = cumt_ref[c]
+        g = g_ref[c]
+        steps = spread(pack, ST)
+        enter = spread(pack, EE)
+        leave = spread(pack, FF)
+        weighted = act * steps
+        low = weighted.astype(BF)
+        low_state = states_ref[c]
+        bmat = bc_ref[rows, :128]
+        cmat = bc_ref[rows, 128:]
+        diags = [block_diag(low[:, 128 * q : 128 * q + 128]) for q in range(3)]
+        decays = [decay_kernel(pack, cumt, h) for h in range(GH)]
+        kernels = [jnp.concatenate([(g * decays[2 * q + e]).astype(BF) for e in range(2)], 1) for q in range(3)]
+        y = mm(cmat, low_state) * enter + jnp.concatenate([mm(kernels[q], diags[q]) for q in range(3)], 1)
+        skip = par[P_SKIP : P_SKIP + 1, :]
+        ssd = y + skip * act
+        gate = pre_ref[pl.ds(base + 8, L), GW:]
+        sg = sigmoid(gate)
+        silu = gate * sg
+        scaled = dinner_ref[rows, :] * par[P_GAIN : P_GAIN + 1, :]
+        inv = inv_ref[rows, :]
+        d_gated = inv[:, 0:1] * scaled - (ssd * silu) * inv[:, 1:2]
+        dy = d_gated * silu
+        dcat_ref[rows, GW:] = (d_gated * ssd * sg * (1.0 + gate * (1.0 - sg))).astype(BF)
+        dy_low = dy.astype(BF)
+        dy_in = (dy * enter).astype(BF)
+        rt = rt_ref[...]
+        rt_low = rt.astype(BF)
+        carried = mm(bmat, rt_low) * leave
+        pieces = []
+        d_scores = jnp.zeros((L, L), F32)
+        for q in range(3):
+            dq = dy_low[:, 128 * q : 128 * q + 128]
+            dm = mm(dq, diags[q], ((1,), (1,)))
+            d_scores = d_scores + dm[:, :L] * decays[2 * q] + dm[:, L:] * decays[2 * q + 1]
+            both = mm(kernels[q], dq, ((0,), (0,)))
+            pieces.append(jnp.where(lane < 64, both[:L], both[L:]))
+        d_weighted = jnp.concatenate(pieces, 1) + carried
+        dg_ref[c] += d_scores
+        out = (weighted * leave).astype(BF)
+        dbc_ref[rows, 128:] += mm(dy_in, low_state, ((1,), (1,)))
+        dbc_ref[rows, :128] += mm(out, rt_low, ((1,), (1,)))
+        keep = enter[L - 1 : L, :]
+        low32 = low.astype(F32)
+        d_cum = head_sums(dy_low.astype(F32) * y - low32 * d_weighted)
+        at_end = jnp.sum(low32 * carried, 0, keepdims=True) + keep * jnp.sum(rt * low_state.astype(F32), 0, keepdims=True)
+        d_last = head_sums(jnp.concatenate([at_end, jnp.zeros((7, GW), F32)], 0))[0:1, :]
+        hi, mid, lo = split3(d_cum)
+        d_log = mm(upper, hi) + mm(upper, mid) + mm(upper, lo) + d_last
+        rt_ref[...] = keep * rt + mm(bct_ref[c, pl.ds(128, 128), :], dy_in)
+        d_step = head_sums(act * d_weighted) + decay * d_log
+        heads = lane < GH
+        d_step_pre = jnp.where(heads, d_step * pltpu.roll(pack, 128 - SG, 1), 0.0)
+        dstep_ref[rows, :] += pltpu.roll(d_step_pre, 16 * group, 1).astype(BF)
+        rate = jnp.sum(jnp.where(heads, pack, 0.0) * d_log, 0, keepdims=True) * decay
+        offs = jnp.sum(d_step_pre, 0, keepdims=True)
+        hgrad_ref[0:1, :] += pltpu.roll(jnp.concatenate([rate, jnp.zeros((7, 128), F32)], 0), 16 * z_k, 1)[0:1]
+        hgrad_ref[1:2, :] += pltpu.roll(jnp.concatenate([offs, jnp.zeros((7, 128), F32)], 0), 16 * z_k, 1)[0:1]
+        d_act = skip * dy + steps * d_weighted
+        du = d_act * su * (1.0 + u * (1.0 - su))
+        pgrad_ref[K : K + 1, :] += jnp.sum(du, 0, keepdims=True)
+        pgrad_ref[P_SKIP : P_SKIP + 1, :] += jnp.sum(dy * act, 0, keepdims=True)
+        for k in range(K):
+            moved = back_conv_input(window, k)
+            if k:
+                moved = moved * tok[:, 2 + k : 3 + k]
+            pgrad_ref[K - 1 - k : K - k, :] += jnp.sum(du * moved, 0, keepdims=True)
+        ahead = jnp.concatenate([du, later], 0)
+        d_pre = par[K - 1 : K, :] * du
+        for k in range(1, K):
+            d_pre = d_pre + par[K - 1 - k : K - k, :] * (ahead[k : k + L] * tok[:, 5 + k : 6 + k])
+        dcat_ref[rows, :GW] = d_pre.astype(BF)
+        return du[:8]
+
+    lax.fori_loop(0, CH, chunk, jnp.zeros((8, GW), F32))
+
+
+def state_chunks(statepre_ref, cst_ref, tok_ref, row_ref, bc_ref, dg_ref, dbc_ref, dstate_ref, sgrad_ref, spad_ref):
+    spad_ref[pl.ds(0, 8), :] = jnp.zeros((8, 256), F32)
+    spad_ref[pl.ds(8, SEQ), :] = statepre_ref[...]
+    sgrad_ref[...] = jnp.zeros_like(sgrad_ref)
+    cst = cst_ref[...]
+    lane = lax.broadcasted_iota(jnp.int32, (L, L), 1)
+    sub = lax.broadcasted_iota(jnp.int32, (L, L), 0)
+
+    def last(step, later):
+        c = CH - 1 - step
+        base = pl.multiple_of(c * L, L)
+        rows = pl.ds(base, L)
+        tok = tok_ref[rows, :]
+        same = (tok[:, 0:1] == row_ref[pl.ds(c, 1), :]) & (sub >= lane)
+        ds = jnp.where(same, dg_ref[c], 0.0).astype(BF)
+        d_c = dbc_ref[rows, 128:] + mm(ds, bc_ref[rows, :128])
+        d_b = dbc_ref[rows, :128] + mm(ds, bc_ref[rows, 128:], ((0,), (0,)))
+        window = spad_ref[pl.ds(base, L + 8), :]
+        w = conv_of(window, tok, cst)
+        sw = sigmoid(w)
+        dw = jnp.concatenate([d_b, d_c], 1) * (sw * (1.0 + w * (1.0 - sw)))
+        sgrad_ref[K : K + 1, :] += jnp.sum(dw, 0, keepdims=True)
+        for k in range(K):
+            moved = back_conv_input(window, k)
+            if k:
+                moved = moved * tok[:, 2 + k : 3 + k]
+            sgrad_ref[K - 1 - k : K - k, :] += jnp.sum(dw * moved, 0, keepdims=True)
+        ahead = jnp.concatenate([dw, later], 0)
+        d_pre = cst[K - 1 : K, :] * dw
+        for k in range(1, K):
+            d_pre = d_pre + cst[K - 1 - k : K - k, :] * (ahead[k : k + L] * tok[:, 5 + k : 6 + k])
+        dstate_ref[rows, :] = d_pre.astype(BF)
+        return dw[:8]
+
+    lax.fori_loop(0, CH, last, jnp.zeros((8, 256), F32))
+
+
+MESH = pl.DeviceIdType.MESH
+VMEM_LIMIT = 63 * 2**20
+R_GAIN, R_CONV, R_SHIFT, R_INNER, R_OFF, R_RATE, R_SKIP, R_CST = 6, 7, 11, 12, 13, 14, 15, 16
+SMALL = 32
+
+
+class Links:
+    def __init__(self, send_sems):
+        self.send_sems = send_sems
+        self.number = {}
+        self.like = {}
+        self.ended = set()
+
+    def send(self, name, src, dst, recv_sem, device, like=None):
+        at = self.number.setdefault(name, len(self.number))
+        self.like[name] = src if like is None else like
+        pltpu.make_async_remote_copy(
+            src_ref=src, dst_ref=dst, send_sem=self.send_sems.at[at], recv_sem=recv_sem,
+            device_id=device, device_id_type=MESH,
+        ).start()
+
+    def arrived(self, dst, recv_sem, device):
+        pltpu.make_async_remote_copy(
+            src_ref=dst, dst_ref=dst, send_sem=self.send_sems.at[0], recv_sem=recv_sem,
+            device_id=device, device_id_type=MESH,
+        ).wait_recv()
+
+    def left(self, name, recv_sem, device):
+        self.ended.add(name)
+        like = self.like[name]
+        pltpu.make_async_remote_copy(
+            src_ref=like, dst_ref=like, send_sem=self.send_sems.at[self.number[name]], recv_sem=recv_sem,
+            device_id=device, device_id_type=MESH,
+        ).wait_send()
+
+    def finish(self, recv_sem, device):
+        for name in self.number:
+            if name not in self.ended:
+                self.left(name, recv_sem, device)
+
+
+class Place:
+    def __init__(self):
+        self.f = lax.axis_index("fsdp")
+        self.z = lax.axis_index("zz")
+        self.c = lax.axis_index("core")
+        f, c = self.f, self.c
+        y, x = f // 2, f % 2
+        by_x = y * 2 + 1 - x
+        by_y = (1 - y) * 2 + x
+        self.f2 = by_x * (1 - c) + by_y * c
+        self.f3 = by_y * (1 - c) + by_x * c
+        self.f4 = 3 - f
+        z_low, z_high = self.z % 2, self.z // 2
+        self.zk = [((z_high + k // 2) % 2) * 2 + (z_low + k % 2) % 2 for k in range(4)]
+
+    def at(self, f=None, z=None, c=None):
+        return (self.f if f is None else f, self.z if z is None else z, self.c if c is None else c)
+
+    def near(self):
+        devices = [self.at(z=self.zk[k]) for k in (1, 2, 3)]
+        return devices + [self.at(f=self.f2), self.at(f=self.f3), self.at(f=self.f4), self.at(c=1 - self.c)]
+
+    def greet(self):
+        for device in self.near():
+            pl.semaphore_signal(pltpu.get_barrier_semaphore(), inc=1, device_id=device, device_id_type=MESH)
+
+    def greeted(self):
+        pl.semaphore_wait(pltpu.get_barrier_semaphore(), len(self.near()))
+
+
+def piece(inout_ref, out_ref, m, f, z):
+    depth = out_ref.shape[2] // 4
+    at = pl.ds(pl.multiple_of(f * depth, depth), depth)
+    if m == 2:
+        return out_ref.at[z, :, at]
+    return inout_ref.at[z, at, pl.ds(m * GW, GW)]
+
+
+def iota(shape, dim):
+    return lax.broadcasted_iota(jnp.int32, shape, dim)
+
+
+def own_block(f, rows, unit):
+    return ((iota((rows, GW), 1) & 63) == f * unit + iota((rows, GW), 0)).astype(BF)
+
+
+def at_block(f, rows, size):
+    row = iota((rows, GW), 0)
+    return ((iota((rows, GW), 1) == f * size + row) & (row < size)).astype(BF)
+
+
+def spread_units(values, place):
+    rows = mm(values, place)
+    return jnp.sum(jnp.where((iota(rows.shape, 1) >> 6) == iota(rows.shape, 0), rows, 0.0), 0, keepdims=True)
+
+
+def small_block(f, vec_ref, step_ref, conv_ref, shift_ref, gain_ref, cst_ref):
+    units = own_block(f, conv_ref.shape[2], conv_ref.shape[2])
+    states = at_block(f, cst_ref.shape[1], cst_ref.shape[1])
+    heads = at_block(f, 16, 12)
+    steps = jnp.concatenate([step_ref[...].astype(F32), jnp.zeros((step_ref.shape[0], 128 - GH), F32)], 1).T
+    rows = [steps[:GH], vec_ref[0:1, :]]
+    rows += [spread_units(conv_ref[k], units) for k in range(K)]
+    rows += [spread_units(shift_ref[...], units), spread_units(gain_ref[...], units)]
+    rows.append(mm(vec_ref[2:5, :16].astype(BF), heads))
+    rows.append(mm(cst_ref[...], states))
+    rows.append(mm(vec_ref[1:2, :64].astype(BF), states))
+    rows.append(jnp.zeros((SMALL - 21, GW), F32))
+    return jnp.concatenate(rows, 0).astype(BF)
+
+
+def token_masks(docs, tok_ref):
+    lane, sub = iota((CH, L), 1), iota((CH, L), 0)
+    masks = [docs, jnp.where((sub > 0) & (docs == pltpu.roll(docs, 1, 0)[:, L - 1 : L]), 1.0, 0.0)]
+    masks.append(jnp.where(docs == docs[:, L - 1 : L], 1.0, 0.0))
+    for k in range(1, K):
+        moved = pltpu.roll(docs, k, 1)
+        before = jnp.where(lane < k, pltpu.roll(moved, 1, 0), moved)
+        masks.append(jnp.where((before == docs) & ((sub > 0) | (lane >= k)), 1.0, 0.0))
+    for k in range(1, K):
+        moved = pltpu.roll(docs, L - k, 1)
+        after = jnp.where(lane >= L - k, pltpu.roll(moved, CH - 1, 0), moved)
+        masks.append(jnp.where((after == docs) & ((sub < CH - 1) | (lane < L - k)), 1.0, 0.0))
+    for c in range(CH):
+        rows = [m[c : c + 1, :] for m in masks] + [jnp.zeros((128 - len(masks), L), F32)]
+        tok_ref[pl.ds(c * L, L), :] = jnp.concatenate(rows, 0).T
+
+
+def forward_kernel(model, hid_ref, cot_ref, w0_ref, w1_ref, w2_ref, wst_ref, vec_ref, step_ref, conv_ref, shift_ref, gain_ref,
+                   cvst_ref, seg_ref,
+                   normt_out, cot_out, win_out, wout_out, pre_out, dinner_out, nin_out, nint_out, states_out,
+                   bc_ref, bct_ref, g_ref, pack_ref, cumt_ref, par_ref, hpar_ref, cst_ref, stw_ref, stbuf, gains_ref,
+                   statepre_ref, invp_ref, gaingrad_ref, tok_ref, docs_ref,
+                   small_ref, hall, call, win, wout, sbuf, pre, flip, ninner, gated, states, dinner, ss_ref, ssr_ref, pr_ref, prr_ref,
+                   spad_ref, st_ref, stepre_ref,
+                   sends, recvs, small_recvs, state_recvs, core_recvs, outs_sem, pre_sem, back_sem):
+    here = Place()
+    z, zk = here.z, here.zk
+    rows_own = hid_ref.shape[0]
+    depth = model // 4
+    links = Links(sends)
+    shards = [w0_ref, w1_ref, w2_ref]
+    outs = []
+
+    def put(src, dst):
+        copy = pltpu.make_async_copy(src, dst, outs_sem.at[len(outs)])
+        copy.start()
+        outs.append(copy)
+
+    here.greet()
+    small_ref[...] = small_block(here.f, vec_ref, step_ref, conv_ref, shift_ref, gain_ref, cvst_ref)
+    here.greeted()
+    for k in (1, 2, 3):
+        links.send(("small", k), small_ref, sbuf.at[here.f, z], small_recvs.at[k], here.at(z=zk[k]))
+    mine = pl.ds(pl.multiple_of(here.c * rows_own, rows_own), rows_own)
+    links.send("hidden", hid_ref, hall.at[mine], core_recvs.at[0], here.at(c=1 - here.c))
+    sbuf[here.f, z] = small_ref[...]
+
+    def recv_sem(m, f, z_):
+        return recvs.at[m, f, z_]
+
+    def push_z(m):
+        for k in (1, 2, 3):
+            links.send(("z", m, k), shards[m], piece(win, wout, m, here.f, z), recv_sem(m, here.f, z), here.at(z=zk[k]))
+
+    def first(m, k):
+        src = shards[m] if k == 0 else piece(win, wout, m, here.f, zk[k])
+        if k:
+            links.arrived(src, recv_sem(m, here.f, zk[k]), here.at(z=zk[k]))
+        dst = piece(win, wout, m, here.f, zk[k])
+        links.send(("first", m, k, 2), src, dst, recv_sem(m, here.f, zk[k]), here.at(f=here.f2))
+        links.send(("first", m, k, 3), src, dst, recv_sem(m, here.f, zk[k]), here.at(f=here.f3))
+
+    def second(m, k):
+        src = piece(win, wout, m, here.f2, zk[k])
+        links.arrived(src, recv_sem(m, here.f2, zk[k]), here.at(f=here.f2))
+        links.send(("second", m, k), src, src, recv_sem(m, here.f2, zk[k]), here.at(f=here.f3))
+
+    def third(m, k):
+        for f in (here.f3, here.f4):
+            src = piece(win, wout, m, f, zk[k])
+            links.arrived(src, recv_sem(m, f, zk[k]), here.at(f=here.f3))
+
+    push_z(0)
+    push_z(1)
+    first(0, 0)
+    first(1, 0)
+    first(2, 0)
+    half_state = pl.ds(pl.multiple_of(here.c * 128, 128), 128)
+    rest_state = pl.ds(pl.multiple_of(128 - here.c * 128, 128), 128)
+    links.send(("state", 0), wst_ref.at[:, half_state], stbuf.at[here.f, :, half_state], state_recvs.at[0], here.at(f=here.f2))
+    links.send(("state", 1), wst_ref.at[:, half_state], stbuf.at[here.f, :, half_state], state_recvs.at[1], here.at(f=here.f3))
+    links.send("cot", cot_ref, call.at[mine], core_recvs.at[1], here.at(c=1 - here.c))
+    win[z, pl.ds(pl.multiple_of(here.f * depth, depth), depth), pl.ds(0, GW)] = w0_ref[...]
+    win[z, pl.ds(pl.multiple_of(here.f * depth, depth), depth), pl.ds(GW, GW)] = w1_ref[...]
+    wout[z, :, pl.ds(pl.multiple_of(here.f * depth, depth), depth)] = w2_ref[...]
+    stbuf[here.f] = wst_ref[...]
+    hall[mine] = hid_ref[...]
+    call[mine] = cot_ref[...]
+    docs = seg_ref[pl.ds(pl.multiple_of(z * CH, CH), CH), :].astype(F32)
+    docs_ref[...] = docs
+    token_masks(docs, tok_ref)
+    for k in (1, 2, 3):
+        links.arrived(sbuf.at[here.f, zk[k]], small_recvs.at[k], here.at(z=zk[k]))
+    links.send(("small", 4), sbuf.at[here.f], sbuf.at[here.f], small_recvs.at[4], here.at(f=here.f2))
+    links.send(("small", 5), sbuf.at[here.f], sbuf.at[here.f], small_recvs.at[5], here.at(f=here.f3))
+    links.arrived(sbuf.at[here.f2], small_recvs.at[4], here.at(f=here.f2))
+    links.send(("small", 6), sbuf.at[here.f2], sbuf.at[here.f2], small_recvs.at[6], here.at(f=here.f3))
+    def state_of(f, part):
+        return stbuf.at[f, :, part]
+
+    links.arrived(state_of(here.f2, half_state), state_recvs.at[0], here.at(f=here.f2))
+    links.send(("state", 2), state_of(here.f2, half_state), state_of(here.f2, half_state), state_recvs.at[2], here.at(f=here.f3))
+    links.send(("state", 3), state_of(here.f2, half_state), state_of(here.f2, half_state), state_recvs.at[3], here.at(c=1 - here.c))
+    other = pl.ds(pl.multiple_of((1 - here.c) * rows_own, rows_own), rows_own)
+    links.arrived(hall.at[other], core_recvs.at[0], here.at(c=1 - here.c))
+    push_z(2)
+    first(0, 1)
+    second(0, 0)
+    links.arrived(sbuf.at[here.f3], small_recvs.at[5], here.at(f=here.f3))
+    links.arrived(sbuf.at[here.f4], small_recvs.at[6], here.at(f=here.f3))
+
+    shared = sum(sbuf[f, 0].astype(F32) for f in range(4))
+    gain_outer = jnp.concatenate([sbuf[f, 0][R_GAIN : R_GAIN + 1, :].astype(F32) for f in range(4)], 1)
+    gains_ref[...] = jnp.broadcast_to(gain_outer, (8, model))
+    cst_ref[...] = jnp.concatenate([shared[R_CST : R_CST + 5, :256], jnp.zeros((3, 256), F32)], 0)
+    lane8 = lax.broadcasted_iota(jnp.int32, (8, 128), 1)
+    heads8 = jnp.concatenate([shared[R_OFF : R_SKIP + 1, :128], jnp.zeros((5, 128), F32)], 0)
+    own_heads = jnp.zeros((8, 128), F32)
+    spread_heads = (lax.broadcasted_iota(jnp.int32, (128, GW), 1) >> 6
+                    == lax.broadcasted_iota(jnp.int32, (128, GW), 0)).astype(BF)
+    stw_ref[...] = jnp.zeros_like(stw_ref)
+    for k in range(4):
+        turned = pltpu.roll(heads8, 128 - (2 * zk[k] + here.c) * GH, 1)
+        own_heads = own_heads + pltpu.roll(jnp.where(lane8 < GH, turned, 0.0), 16 * k, 1)
+        group = sum(sbuf[f, zk[k]].astype(F32) for f in range(4))
+        skips = mm(turned.astype(BF), spread_heads)[2:3, :]
+        par_ref[k] = jnp.concatenate(
+            [group[R_CONV : R_CONV + 5], skips, group[R_INNER : R_INNER + 1], jnp.zeros((1, GW), F32)], 0
+        )
+        for f in range(4):
+            block = sbuf[f, zk[k]][:16].astype(F32)
+            keep = lax.broadcasted_iota(jnp.int32, block.shape, 0) < GH
+            stw_ref[pl.ds(16 * k, 16), pl.ds(depth * f, depth)] = jnp.where(keep, block, 0.0).astype(BF)
+    decay = -jnp.exp(own_heads[1:2, :])
+    hpar_ref[...] = jnp.concatenate([own_heads[0:1], decay, own_heads[2:3], jnp.zeros((5, 128), F32)], 0)
+
+    def norm(i, _):
+        rows = pl.ds(pl.multiple_of(i * L, L), L)
+        x = hall[rows, :].astype(F32)
+        inv = lax.rsqrt(jnp.sum(x * x, 1, keepdims=True) / model + EPSILON)
+        hall[rows, :] = (x * inv * gain_outer).astype(BF)
+        return 0
+
+    lax.fori_loop(0, SEQ // L, norm, 0)
+    first(1, 1)
+    second(1, 0)
+    links.arrived(state_of(here.f3, half_state), state_recvs.at[1], here.at(f=here.f3))
+    links.send(("state", 4), state_of(here.f3, half_state), state_of(here.f3, half_state), state_recvs.at[4], here.at(c=1 - here.c))
+    links.arrived(state_of(here.f4, half_state), state_recvs.at[2], here.at(f=here.f3))
+    links.send(("state", 5), state_of(here.f4, half_state), state_of(here.f4, half_state), state_recvs.at[5], here.at(c=1 - here.c))
+    for n, f in ((3, here.f3), (4, here.f2), (5, here.f4)):
+        links.arrived(state_of(f, rest_state), state_recvs.at[n], here.at(c=1 - here.c))
+
+    TILE = 256
+
+    def project_small(i, _):
+        rows = pl.ds(pl.multiple_of(i * TILE, TILE), TILE)
+        total = jnp.zeros((TILE, 256), F32)
+        for f in range(4):
+            total = total + mm(hall[rows, pl.ds(depth * f, depth)], stbuf[f])
+        statepre_ref[rows, :] = total
+        steps = mm(hall[rows, :], stw_ref[...], ((1,), (1,)))
+        stepre_ref[rows, :] = jnp.concatenate([steps, jnp.zeros((TILE, 64), F32)], 1)
+        return 0
+
+    lax.fori_loop(0, SEQ // TILE, project_small, 0)
+
+    def turn(i, _):
+        for half in range(2):
+            lanes = pl.ds(pl.multiple_of(i * 256 + half * 128, 128), 128)
+            flip[lanes, :] = hall[:, lanes].T
+        return 0
+
+    lax.fori_loop(0, model // 256, turn, 0)
+    TURNED = len(outs)
+    put(flip, normt_out)
+    prep_chunks(statepre_ref, stepre_ref, tok_ref, docs_ref, cst_ref, hpar_ref, bc_ref, bct_ref, g_ref, pack_ref, cumt_ref,
+                spad_ref)
+    units = [(k, m) for k in range(4) for m in (0, 1)] + [(k, 2) for k in range(4)]
+    done = [3, 1]
+
+    def advance(i):
+        while done[0] < min(i + 3, len(units) - 1) or done[1] < min(i + 1, len(units) - 1):
+            if done[0] < min(i + 3, len(units) - 1):
+                done[0] += 1
+                k, m = units[done[0]]
+                if (k, m) != (0, 2):
+                    first(m, k)
+            if done[1] < min(i + 1, len(units) - 1):
+                done[1] += 1
+                k, m = units[done[1]]
+                second(m, k)
+
+    links.arrived(call.at[other], core_recvs.at[1], here.at(c=1 - here.c))
+    put(call, cot_out)
+    ss_ref[...] = jnp.zeros_like(ss_ref)
+    for slot in range(2):
+        pre[slot, pl.ds(0, 8), :] = jnp.zeros((8, 2 * GW), F32)
+    pre_copies = []
+    for k in range(4):
+        advance(2 * k)
+        third(0, k)
+        advance(2 * k + 1)
+        third(1, k)
+        slot = k % 2
+        if k >= 2:
+            pre_copies[k - 2].wait()
+
+        def project(i, _, slot=slot, k=k):
+            rows = pl.ds(pl.multiple_of(i * TILE, TILE), TILE)
+            to = pl.ds(pl.multiple_of(i * TILE + 8, 8), TILE)
+            pre[slot, to, :] = mm(hall[rows, :], win[zk[k]])
+            return 0
+
+        lax.fori_loop(0, SEQ // TILE, project, 0)
+        copy = pltpu.make_async_copy(pre.at[slot, pl.ds(8, SEQ)], pre_out.at[k], pre_sem.at[k])
+        copy.start()
+        pre_copies.append(copy)
+        put(win.at[zk[k]], win_out.at[k])
+        advance(2 * k + 2)
+        fwd_chunks(pre.at[slot], par_ref.at[k], tok_ref, bc_ref, bct_ref, g_ref, pack_ref.at[k], cumt_ref.at[k],
+                   gated.at[k], states.at[k], ss_ref, st_ref)
+        put(states.at[k], states_out.at[k])
+    pre_copies[2].wait()
+    pre_copies[3].wait()
+
+    links.send("squares", ss_ref, ssr_ref, core_recvs.at[2], here.at(c=1 - here.c))
+    advance(8)
+    links.arrived(ssr_ref, core_recvs.at[2], here.at(c=1 - here.c))
+    inner_all = 2 * 4 * GW
+
+    def inner_norm(i, _):
+        rows = pl.ds(pl.multiple_of(i * L, L), L)
+        total = jnp.sum(ss_ref[rows, :] + ssr_ref[rows, :], 1, keepdims=True)
+        inv = lax.rsqrt(total / inner_all + EPSILON)
+        invp_ref[rows, :] = jnp.broadcast_to(inv, (L, 128))
+        for k in range(4):
+            gain = par_ref[k, P_GAIN : P_GAIN + 1, :]
+            low = (gated[k, rows, :].astype(F32) * inv * gain).astype(BF)
+            ninner[k, rows, :] = low
+            flip[pl.ds(k * GW, GW), rows] = low.T
+        pr_ref[rows, :] = jnp.zeros((L, 128), F32)
+        return 0
+
+    outs[TURNED].wait()
+    outs[TURNED] = None
+    lax.fori_loop(0, SEQ // L, inner_norm, 0)
+    put(ninner, nin_out)
+    put(flip, nint_out)
+    back_copies = []
+    for k in range(4):
+        advance(8 + k)
+        third(2, k)
+        slot = k % 2
+        if k >= 2:
+            back_copies[k - 2].wait()
+        gaingrad_ref[k] = jnp.zeros((8, GW), F32)
+
+        def back(i, _, slot=slot, k=k):
+            rows = pl.ds(pl.multiple_of(i * TILE, TILE), TILE)
+            d = mm(call[rows, :], wout[zk[k]], ((1,), (1,)))
+            dinner[slot, rows, :] = d
+            both = d * gated[k, rows, :].astype(F32)
+            gaingrad_ref[k, 0:1, :] += jnp.sum(both * invp_ref[rows, 0:1], 0, keepdims=True)
+            both = both * par_ref[k, P_GAIN : P_GAIN + 1, :]
+            pr_ref[rows, :] += both[:, :128] + both[:, 128:256] + both[:, 256:]
+            return 0
+
+        lax.fori_loop(0, SEQ // TILE, back, 0)
+        copy = pltpu.make_async_copy(dinner.at[slot], dinner_out.at[k], back_sem.at[k])
+        copy.start()
+        back_copies.append(copy)
+        put(wout.at[zk[k]], wout_out.at[k])
+    links.send("products", pr_ref, prr_ref, core_recvs.at[3], here.at(c=1 - here.c))
+    links.arrived(prr_ref, core_recvs.at[3], here.at(c=1 - here.c))
+
+    def scale(i, _):
+        rows = pl.ds(pl.multiple_of(i * L, L), L)
+        total = jnp.sum(pr_ref[rows, :] + prr_ref[rows, :], 1, keepdims=True)
+        inv = invp_ref[rows, :]
+        lane = lax.broadcasted_iota(jnp.int32, (L, 128), 1)
+        invp_ref[rows, :] = jnp.where(lane == 0, inv, inv * inv * inv * (total / inner_all))
+        return 0
+
+    lax.fori_loop(0, SEQ // L, scale, 0)
+    back_copies[2].wait()
+    back_copies[3].wait()
+    for copy in outs:
+        if copy is not None:
+            copy.wait()
+    links.finish(core_recvs.at[0], here.at(c=1 - here.c))
+
+
+def forward_call(model, hidden, cot, *args):
+    rows = hidden.shape[0]
+    any_ = pl.BlockSpec(memory_space=pl.ANY)
+    sds = jax.ShapeDtypeStruct
+    inner = 4 * GW
+    depth = model // 4
+    return pl.pallas_call(
+        functools.partial(forward_kernel, model),
+        out_shape=(
+            sds((model, SEQ), BF), sds((SEQ, model), BF), sds((4, model, 2 * GW), BF), sds((4, GW, model), BF),
+            sds((4, SEQ, 2 * GW), F32), sds((4, SEQ, GW), F32), sds((4, SEQ, GW), BF),
+            sds((4 * GW, SEQ), BF), sds((4, CH, 128, GW), BF),
+            sds((SEQ, 256), BF), sds((CH, 256, L), BF), sds((CH, L, L), F32), sds((4, SEQ, 128), F32),
+            sds((4, CH, 8, L), F32), sds((4, 8, GW), F32), sds((8, 128), F32), sds((8, 256), F32),
+            sds((64, model), BF), sds((4, depth, 256), BF), sds((8, model), F32), sds((SEQ, 256), F32), sds((SEQ, 128), F32),
+            sds((4, 8, GW), F32), sds((SEQ, 128), F32), sds((CH, L), F32),
+        ),
+        in_specs=[vm()] * (2 + len(args)),
+        out_specs=tuple([any_] * 9 + [vm()] * 16),
+        scratch_shapes=[
+            pltpu.VMEM((SMALL, GW), BF),
+            pltpu.VMEM((SEQ, model), BF),
+            pltpu.VMEM((SEQ, model), BF),
+            pltpu.VMEM((4, model, 2 * GW), BF),
+            pltpu.VMEM((4, GW, model), BF),
+            pltpu.VMEM((4, 4, SMALL, GW), BF),
+            pltpu.VMEM((2, SEQ + 8, 2 * GW), F32),
+            pltpu.VMEM((model, SEQ), BF),
+            pltpu.VMEM((4, SEQ, GW), BF),
+            pltpu.VMEM((4, SEQ, GW), BF),
+            pltpu.VMEM((4, CH, 128, GW), BF),
+            pltpu.VMEM((2, SEQ, GW), F32),
+            pltpu.VMEM((SEQ, 128), F32),
+            pltpu.VMEM((SEQ, 128), F32),
+            pltpu.VMEM((SEQ, 128), F32),
+            pltpu.VMEM((SEQ, 128), F32),
+            pltpu.VMEM((SEQ + 8, 256), F32),
+            pltpu.VMEM((128, GW), F32),
+            pltpu.VMEM((SEQ, 128), F32),
+            pltpu.SemaphoreType.DMA((64,)),
+            pltpu.SemaphoreType.DMA((3, 4, 4)),
+            pltpu.SemaphoreType.DMA((7,)),
+            pltpu.SemaphoreType.DMA((6,)),
+            pltpu.SemaphoreType.DMA((4,)),
+            pltpu.SemaphoreType.DMA((16,)),
+            pltpu.SemaphoreType.DMA((4,)),
+            pltpu.SemaphoreType.DMA((4,)),
+        ],
+        compiler_params=pltpu.CompilerParams(vmem_limit_bytes=VMEM_LIMIT, collective_id=1, has_side_effects=True),
+        name="gather_and_forward",
+    )(hidden, cot, *args)
+
+
+ORDER = (3, 2, 1, 0)
+
+
+def backward_kernel(model, hid_ref, tok_ref, row_ref, inv_ref, bc_ref, bct_ref, g_ref, cumt_ref, par_ref,
+                    hpar_ref, cst_ref, stw_ref, stbuf_ref, statepre_ref, gaingrad_ref, gains_ref,
+                    normt_in, cot_in, win_in, wout_in, pre_in, dinner_in, nin_in, nint_in, states_in, pack_in,
+                    layer_out, hidden_out, ginner_ref, ggate_ref, gout_ref, gstate_ref, gsmall_ref, gother_ref,
+                    normt, cot, win, pre, dinner, states, pack, acc, half, halfr, dcat, parts, recv1, recv2, recv3,
+                    sparts, ssend, srecv, srecv1, srecv2, srecv3, srecvc, qparts, qrecv1, qrecv3, qsend, qrecvc,
+                    dstep, dstate, pgrad, hgrad, sgrad, rt_ref, dg_ref, dbc_ref, spad_ref,
+                    sends, recv_sems, core_sems, load_sems, credit1, credit2):
+    here = Place()
+    zk = here.zk
+    f, f2, f3, f4 = here.f, here.f2, here.f3, here.f4
+    links = Links(sends)
+    depth = model // 4
+    rows_own = hid_ref.shape[0]
+    mine = pl.ds(pl.multiple_of(here.c * rows_own, rows_own), rows_own)
+    across = pl.ds(pl.multiple_of((1 - here.c) * rows_own, rows_own), rows_own)
+    units = [(k, 2) for k in ORDER] + [(k, m) for k in ORDER for m in (0, 1)]
+    ROWS = 128
+
+    loads = {}
+
+    def load(name, src, dst, sem):
+        copy = pltpu.make_async_copy(src, dst, load_sems.at[sem])
+        copy.start()
+        loads[name] = copy
+
+    wouts = [halfr.at[1, pl.ds(0, GW)], half.at[pl.ds(0, GW)]]
+
+    def nin(i):
+        return dcat.at[:, pl.ds(GW * (i % 2), GW)]
+
+    def load_out(i):
+        k = ORDER[i]
+        load(("nin", i), nin_in.at[k], nin(i), 2 * (i % 2))
+        load(("wout", i), wout_in.at[k], wouts[i % 2], 2 * (i % 2) + 1)
+
+    def load_group(i):
+        k = ORDER[i]
+        load(("pre", i), pre_in.at[k], pre.at[pl.ds(8, SEQ)], 8)
+        load(("dinner", i), dinner_in.at[k], dinner, 9)
+        load(("states", i), states_in.at[k], states, 10)
+        load(("pack", i), pack_in.at[k], pack, 5)
+
+    def load_win(i):
+        load(("win", i), win_in.at[ORDER[i]], win, 11)
+
+    load("nint", nint_in, normt, 4)
+    load("cot", cot_in, cot, 6)
+    load_out(0)
+    load_out(1)
+    load_group(0)
+    load_win(0)
+    pre[pl.ds(0, 8), :] = jnp.zeros((8, 2 * GW), F32)
+    hgrad[...] = jnp.zeros_like(hgrad)
+    dg_ref[...] = jnp.zeros_like(dg_ref)
+    dbc_ref[...] = jnp.zeros_like(dbc_ref)
+    dstep[...] = jnp.zeros_like(dstep)
+    here.greet()
+    here.greeted()
+
+    one_block = parts.at[0, 0]
+
+    def part(u, f_):
+        return parts.at[u % 6, f_]
+
+    def add_into(dst, src):
+        rows, width = dst.shape
+
+        def body(i, _):
+            at = pl.ds(pl.multiple_of(i * ROWS, ROWS), ROWS)
+            dst[at, :] = (dst[at, :].astype(F32) + src[at, :].astype(F32)).astype(dst.dtype)
+            return 0
+
+        lax.fori_loop(0, rows // ROWS, body, 0)
+
+    def s1(u):
+        if u >= 8:
+            pl.semaphore_wait(credit1, 1)
+        for n, f_ in enumerate((f3, f4)):
+            links.send(("s1", u, n), part(u, f_), recv1.at[u % 8, n], recv_sems.at[u, n], here.at(f=f3), one_block)
+
+    def s2(u):
+        links.arrived(recv1.at[u % 8, 1], recv_sems.at[u, 1], here.at(f=f3))
+        add_into(part(u, f2), recv1.at[u % 8, 1])
+        if u >= 8:
+            pl.semaphore_wait(credit2, 1)
+        links.send(("s2", u), part(u, f2), recv2.at[u % 8], recv_sems.at[u, 2], here.at(f=f2), one_block)
+        links.arrived(recv1.at[u % 8, 0], recv_sems.at[u, 0], here.at(f=f3))
+        add_into(part(u, f), recv1.at[u % 8, 0])
+        if u < 4:
+            pl.semaphore_signal(credit1, inc=1, device_id=here.at(f=f3), device_id_type=MESH)
+
+    def give_credit(u):
+        if u < 4:
+            pl.semaphore_signal(credit2, inc=1, device_id=here.at(f=f2), device_id_type=MESH)
+
+    outs = {0: ginner_ref, 1: ggate_ref, 2: gout_ref}
+
+    def s3(u):
+        k, m = units[u]
+        links.arrived(recv2.at[u % 8], recv_sems.at[u, 2], here.at(f=f2))
+        add_into(part(u, f), recv2.at[u % 8])
+        give_credit(u)
+        links.send(("s3", u), part(u, f), recv3.at[m, k - 1], recv_sems.at[12 + m, k - 1], here.at(z=zk[k]), one_block)
+
+    def last_sum(u):
+        k, m = units[u]
+        links.arrived(recv2.at[u % 8], recv_sems.at[u, 2], here.at(f=f2))
+        for j in (1, 2, 3):
+            links.arrived(recv3.at[m, j - 1], recv_sems.at[12 + m, j - 1], here.at(z=zk[j]))
+        own = part(u, f)
+
+        def body(i, _):
+            at = pl.ds(pl.multiple_of(i * ROWS, ROWS), ROWS)
+            total = own[at, :].astype(F32) + recv2[u % 8, at, :].astype(F32)
+            for j in range(3):
+                total = total + recv3[m, j, at, :].astype(F32)
+            outs[m][at, :] = total
+            return 0
+
+        lax.fori_loop(0, GW // ROWS, body, 0)
+        give_credit(u)
+
+    loads["nint"].wait()
+    loads["cot"].wait()
+    for i, k in enumerate(ORDER):
+
+        def grad_out(j, _, i=i, k=k):
+            at = pl.ds(pl.multiple_of(j * ROWS, ROWS), ROWS)
+            src = pl.ds(pl.multiple_of(k * GW + j * ROWS, ROWS), ROWS)
+            total = mm(normt[src, :], cot[...])
+            for f_ in range(4):
+                parts[i, f_, at, :] = total[:, f_ * depth : (f_ + 1) * depth].astype(BF)
+            return 0
+
+        lax.fori_loop(0, GW // ROWS, grad_out, 0)
+        s1(i)
+        loads["nin", i].wait()
+        loads["wout", i].wait()
+
+        def mix_rows(j, _, i=i):
+            at = pl.ds(pl.multiple_of(j * 256, 256), 256)
+            total = mm(nin(i)[at, :], wouts[i % 2][...])
+            acc[at, :] = total if i == 0 else acc[at, :] + total
+            return 0
+
+        lax.fori_loop(0, SEQ // 256, mix_rows, 0)
+        if i + 2 < 4:
+            load_out(i + 2)
+
+    load("normt", normt_in, normt, 7)
+
+    def exchange(n):
+        if n:
+            links.left(("half", 0), core_sems.at[0], here.at(c=1 - here.c))
+
+        def body(j, _):
+            at = pl.ds(pl.multiple_of(j * ROWS, ROWS), ROWS)
+            src = pl.ds(pl.multiple_of((1 - here.c) * rows_own + j * ROWS, ROWS), ROWS)
+            half[at, :] = acc[src, :].astype(BF)
+            return 0
+
+        lax.fori_loop(0, rows_own // ROWS, body, 0)
+        links.send(("half", n), half, halfr.at[n], core_sems.at[n], here.at(c=1 - here.c))
+
+    def received(n):
+        links.arrived(halfr.at[n], core_sems.at[n], here.at(c=1 - here.c))
+
+    exchange(0)
+    received(0)
+
+    def layer(j, _):
+        at = pl.ds(pl.multiple_of(j * ROWS, ROWS), ROWS)
+        src = pl.ds(pl.multiple_of(here.c * rows_own + j * ROWS, ROWS), ROWS)
+        halfr[0, at, :] = (hid_ref[at, :].astype(F32) + acc[src, :] + halfr[0, at, :].astype(F32)).astype(BF)
+        return 0
+
+    lax.fori_loop(0, rows_own // ROWS, layer, 0)
+    load("layer", halfr.at[0], layer_out, 12)
+    loads["normt"].wait()
+
+    due = {
+        0: {0: [(s2, 0)], 1: [(s2, 1)], 2: [(s3, 0)], 4: [(s2, 2)], 5: [(s3, 1)], 7: [(s2, 3)]},
+        1: {0: [(s3, 2)], 5: [(s2, 4)], 7: [(s2, 5)]},
+        2: {0: [(s3, 4)], 1: [(s3, 5)], 3: [(s2, 6)], 4: [(last_sum, 3)], 5: [(s3, 6)], 6: [(s2, 7)]},
+        3: {0: [(s3, 7)], 3: [(s2, 8)], 5: [(s3, 8)], 6: [(s2, 9)], 7: [(s3, 9)]},
+    }
+    for i, k in enumerate(ORDER):
+        for name in ("pre", "dinner", "states", "pack"):
+            loads[name, i].wait()
+
+        def tick(step, i=i):
+            for at, events in due[i].items():
+                @pl.when(step == at)
+                def _(events=events):
+                    for event, u in events:
+                        event(u)
+
+        bwd_chunks(k, zk[k], tick, pre, dinner, par_ref.at[k], tok_ref, inv_ref, bc_ref, bct_ref, g_ref, pack,
+                   cumt_ref.at[k], states, hpar_ref, dcat, dstep, pgrad.at[k], hgrad, rt_ref, dg_ref, dbc_ref)
+        if i < 3:
+            load_group(i + 1)
+        u = 4 + 2 * i
+        if u >= 6:
+            for n in (u - 6, u - 5):
+                for name in (("s1", n, 0), ("s1", n, 1), ("s2", n), ("s3", n)):
+                    if name in links.number:
+                        links.left(name, core_sems.at[0], here.at(c=1 - here.c))
+
+        def grads(j, _, u=u):
+            at = pl.ds(pl.multiple_of(j * ROWS, ROWS), ROWS)
+            for f_ in range(4):
+                src = pl.ds(pl.multiple_of(f_ * depth + j * ROWS, ROWS), ROWS)
+                total = mm(normt[src, :], dcat[...])
+                parts[u % 6, f_, at, :] = total[:, :GW].astype(BF)
+                parts[(u + 1) % 6, f_, at, :] = total[:, GW:].astype(BF)
+            return 0
+
+        lax.fori_loop(0, depth // ROWS, grads, 0)
+        s1(u)
+        s1(u + 1)
+        loads["win", i].wait()
+
+        def to_normed(j, _, i=i):
+            at = pl.ds(pl.multiple_of(j * 256, 256), 256)
+            total = mm(dcat[at, :], win[...], ((1,), (1,)))
+            acc[at, :] = total if i == 0 else acc[at, :] + total
+            return 0
+
+        lax.fori_loop(0, SEQ // 256, to_normed, 0)
+        if i < 3:
+            load_win(i + 1)
+
+    state_chunks(statepre_ref, cst_ref, tok_ref, row_ref, bc_ref, dg_ref, dbc_ref, dstate, sgrad, spad_ref)
+    half_state = pl.ds(pl.multiple_of(here.c * 128, 128), 128)
+    rest_state = pl.ds(pl.multiple_of(128 - here.c * 128, 128), 128)
+    core = here.at(c=1 - here.c)
+    for f_ in range(4):
+        sums = mm(normt[pl.ds(f_ * depth, depth), :], dstate[...])
+        lower, upper = sums[:, :128], sums[:, 128:]
+        sparts[f_] = jnp.where(here.c == 0, lower, upper).astype(BF)
+        ssend[f_] = jnp.where(here.c == 0, upper, lower).astype(BF)
+    links.send("state_core", ssend, srecv, core_sems.at[2], core)
+
+    def finish_normed(j, _):
+        at = pl.ds(pl.multiple_of(j * 256, 256), 256)
+        total = mm(dstep[at, :64], stw_ref[...])
+        total = total + jnp.concatenate([mm(dstate[at, :], stbuf_ref[f_], ((1,), (1,))) for f_ in range(4)], 1)
+        acc[at, :] = acc[at, :] + total
+        return 0
+
+    lax.fori_loop(0, SEQ // 256, finish_normed, 0)
+    exchange(1)
+    links.arrived(srecv, core_sems.at[2], core)
+    for f_ in range(4):
+        sparts[f_] = (sparts[f_].astype(F32) + srecv[f_].astype(F32)).astype(BF)
+    links.send("state3", sparts.at[f3], srecv1.at[0], recv_sems.at[15, 0], here.at(f=f3))
+    links.send("state4", sparts.at[f4], srecv1.at[1], recv_sems.at[15, 1], here.at(f=f3))
+    step_rows = mm(dstep[:, :64], normt[...], ((0,), (1,)))
+    received(1)
+    gain = gains_ref[0:1, :]
+
+    def last(j, gain_grad):
+        at = pl.ds(pl.multiple_of(j * ROWS, ROWS), ROWS)
+        src = pl.ds(pl.multiple_of(here.c * rows_own + j * ROWS, ROWS), ROWS)
+        d = acc[src, :] + halfr[1, at, :].astype(F32)
+        x = hid_ref[at, :].astype(F32)
+        inv = lax.rsqrt(jnp.sum(x * x, 1, keepdims=True) / model + EPSILON)
+        weighted = d * gain
+        mean = jnp.sum(x * weighted, 1, keepdims=True) / model
+        d_hidden = inv * weighted - x * (inv * inv * inv * mean)
+        halfr[1, at, :] = (cot[src, :].astype(F32) + d_hidden).astype(BF)
+        return gain_grad + jnp.sum(d * x * inv, 0, keepdims=True)
+
+    gain_grad = lax.fori_loop(0, rows_own // ROWS, last, jnp.zeros((1, model), F32))
+    load("hidden", halfr.at[1], hidden_out, 13)
+    zeros = jnp.zeros((1, GW - 256), F32)
+    skips = jnp.zeros((8, 128), F32)
+    heads_of = (iota((GW, 128), 0) >> 6 == iota((GW, 128), 1)).astype(BF)
+    for k in range(4):
+        hi, lo = split2(pgrad[k])
+        skips = skips + pltpu.roll(mm(hi, heads_of) + mm(lo, heads_of), 16 * zk[k], 1)
+    head_rows = jnp.concatenate([hgrad[0:2, :], skips[P_SKIP : P_SKIP + 1, :]], 0)
+    head_rows = jnp.concatenate([head_rows, jnp.zeros((3, GW - 128), F32)], 1)
+    for f_ in range(4):
+        common = [gain_grad[:, f_ * depth : (f_ + 1) * depth]]
+        common += [jnp.concatenate([sgrad[r : r + 1, :], zeros], 1) for r in range(5)]
+        common.append(head_rows)
+        for k in range(4):
+            own = jnp.concatenate([pgrad[k, 0:5, :], gaingrad_ref[k, 0:1, :], jnp.zeros((1, GW), F32)], 0)
+            qparts[f_, k] = jnp.concatenate(
+                [step_rows[16 * k : 16 * k + 16, f_ * depth : (f_ + 1) * depth], own] + common, 0
+            ).astype(BF)
+    for n, f_ in enumerate((f2, f3, f4)):
+        links.send(("small", n), qparts.at[f_], qrecv1.at[n], recv_sems.at[16, n], here.at(f=f_))
+    links.arrived(srecv1.at[1], recv_sems.at[15, 1], here.at(f=f3))
+    sparts[f2] = (sparts[f2].astype(F32) + srecv1[1].astype(F32)).astype(BF)
+    links.send("state2", sparts.at[f2], srecv2, recv_sems.at[15, 2], here.at(f=f2))
+    links.arrived(srecv1.at[0], recv_sems.at[15, 0], here.at(f=f3))
+    s2(10)
+    for n, f_ in enumerate((f2, f3, f4)):
+        links.arrived(qrecv1.at[n], recv_sems.at[16, n], here.at(f=f_))
+    for k in range(4):
+        total = qparts[f, k].astype(F32)
+        for n in range(3):
+            total = total + qrecv1[n, k].astype(F32)
+        qsend[k] = total.astype(BF)
+        if k:
+            links.send(("small_z", k), qsend.at[k], qrecv3.at[k - 1], recv_sems.at[18, k - 1], here.at(z=zk[k]))
+    s2(11)
+    links.arrived(srecv2, recv_sems.at[15, 2], here.at(f=f2))
+    sparts[f] = (sparts[f].astype(F32) + srecv1[0].astype(F32) + srecv2[...].astype(F32)).astype(BF)
+    for k in (1, 2, 3):
+        links.send(("state", k), sparts.at[f], srecv3.at[k - 1], recv_sems.at[17, k - 1], here.at(z=zk[k]))
+    for k in (1, 2, 3):
+        links.arrived(qrecv3.at[k - 1], recv_sems.at[18, k - 1], here.at(z=zk[k]))
+    total = qsend[0].astype(F32)
+    for k in range(3):
+        total = total + qrecv3[k].astype(F32)
+    gsmall_ref[...] = total
+    qsend[0] = total.astype(BF)
+    links.send("small_core", qsend.at[0], qrecvc, core_sems.at[3], core)
+    last_sum(10)
+    last_sum(11)
+    for k in (1, 2, 3):
+        links.arrived(srecv3.at[k - 1], recv_sems.at[17, k - 1], here.at(z=zk[k]))
+    total = sparts[f].astype(F32)
+    for k in range(3):
+        total = total + srecv3[k].astype(F32)
+    links.left("state_core", core_sems.at[0], core)
+    ssend[0] = total.astype(BF)
+    links.send("state_back", ssend.at[0], srecvc, core_sems.at[4], core)
+    links.arrived(qrecvc, core_sems.at[3], core)
+    gother_ref[...] = qrecvc[...].astype(F32)
+    links.arrived(srecvc, core_sems.at[4], core)
+    rest = srecvc[...].astype(F32)
+    gstate_ref[...] = jnp.concatenate([jnp.where(here.c == 0, total, rest), jnp.where(here.c == 0, rest, total)], 1)
+    loads["layer"].wait()
+    loads["hidden"].wait()
+    links.finish(core_sems.at[0], core)
+
+
+def backward_call(model, hidden, saved):
+    (normt, cot, win, wout, pre, dinner, nin, nint, states, bc, bct, gs, pack, cumt, par, hpar, cst, stw, stbuf, gains,
+     statepre, invp, gaingrad, tok, row) = saved
+    rows = hidden.shape[0]
+    depth = model // 4
+    any_ = pl.BlockSpec(memory_space=pl.ANY)
+    sds = jax.ShapeDtypeStruct
+    block = (GW, GW)
+    state = (depth, 256)
+    part = (depth, 128)
+    small = (SMALL, GW)
+    return pl.pallas_call(
+        functools.partial(backward_kernel, model),
+        out_shape=(
+            sds((rows, model), BF), sds((rows, model), BF), sds(block, F32), sds(block, F32), sds(block, F32),
+            sds(state, F32), sds(small, F32), sds(small, F32),
+        ),
+        in_specs=[vm()] * 16 + [any_] * 10,
+        out_specs=tuple([any_] * 2 + [vm()] * 6),
+        scratch_shapes=[
+            pltpu.VMEM((model, SEQ), BF),
+            pltpu.VMEM((SEQ, model), BF),
+            pltpu.VMEM((model, 2 * GW), BF),
+            pltpu.VMEM((SEQ + 8, 2 * GW), F32),
+            pltpu.VMEM((SEQ, GW), F32),
+            pltpu.VMEM((CH, 128, GW), BF),
+            pltpu.VMEM((SEQ, 128), F32),
+            pltpu.VMEM((SEQ, model), F32),
+            pltpu.VMEM((rows, model), BF),
+            pltpu.VMEM((2, rows, model), BF),
+            pltpu.VMEM((SEQ, 2 * GW), BF),
+            pltpu.VMEM((6, 4) + block, BF),
+            pltpu.VMEM((8, 2) + block, BF),
+            pltpu.VMEM((8,) + block, BF),
+            pltpu.VMEM((3, 3) + block, BF),
+            pltpu.VMEM((4,) + part, BF),
+            pltpu.VMEM((4,) + part, BF),
+            pltpu.VMEM((4,) + part, BF),
+            pltpu.VMEM((2,) + part, BF),
+            pltpu.VMEM(part, BF),
+            pltpu.VMEM((3,) + part, BF),
+            pltpu.VMEM(part, BF),
+            pltpu.VMEM((4, 4) + small, BF),
+            pltpu.VMEM((3, 4) + small, BF),
+            pltpu.VMEM((3,) + small, BF),
+            pltpu.VMEM((4,) + small, BF),
+            pltpu.VMEM(small, BF),
+            pltpu.VMEM((SEQ, 128), BF),
+            pltpu.VMEM((SEQ, 256), BF),
+            pltpu.VMEM((4, 8, GW), F32),
+            pltpu.VMEM((8, 128), F32),
+            pltpu.VMEM((8, 256), F32),
+            pltpu.VMEM((128, GW), F32),
+            pltpu.VMEM((CH, L, L), F32),
+            pltpu.VMEM((SEQ, 256), F32),
+            pltpu.VMEM((SEQ + 8, 256), F32),
+            pltpu.SemaphoreType.DMA((72,)),
+            pltpu.SemaphoreType.DMA((19, 4)),
+            pltpu.SemaphoreType.DMA((5,)),
+            pltpu.SemaphoreType.DMA((14,)),
+            pltpu.SemaphoreType.REGULAR,
+            pltpu.SemaphoreType.REGULAR,
+        ],
+        compiler_params=pltpu.CompilerParams(vmem_limit_bytes=VMEM_LIMIT, collective_id=2, has_side_effects=True),
+        name="backward_and_scatter",
+    )(hidden, tok, row, invp, bc, bct, gs, cumt, par, hpar, cst, stw, stbuf, statepre, gaingrad, gains,
+      normt, cot, win, wout, pre, dinner, nin, nint, states, pack)
+
+
 def on_device(fsdp, halves, hidden_in, norm_gain, in_gate, in_inner, in_state, in_step, conv_inner, conv_inner_shift,
               conv_state, conv_state_shift, step_offset, log_rate, skip_gain, inner_gain, out_weight, segment_ids,
               grad_out):
@@ -591,6 +1687,38 @@
             grad_out_weight)
 
 
+def on_chip(hidden_in, norm_gain, in_gate, in_inner, in_state, in_step, conv_inner, conv_inner_shift, conv_state,
+            conv_state_shift, step_offset, log_rate, skip_gain, inner_gain, out_weight, segment_ids, grad_out):
+    depth = in_gate.shape[0]
+    model = depth * 4
+    f = lax.axis_index("fsdp")
+    core = lax.axis_index("core")
+
+    vec = [jnp.pad(v, (0, GW - v.shape[0])) for v in (norm_gain, conv_state_shift, step_offset, log_rate, skip_gain)]
+    vec = jnp.concatenate(vec + [jnp.zeros((3 * GW,), BF)]).reshape(8, GW).astype(F32)
+    saved = forward_call(model, hidden_in, grad_out, in_inner, in_gate, out_weight, in_state, vec, in_step, conv_inner,
+                         conv_inner_shift, inner_gain, conv_state, segment_ids.reshape(-1, L))
+    layer_out, grad_hidden, g_inner, g_gate, g_out, g_state, own, other = backward_call(model, hidden_in, saved)
+    shared = own[23:] + other[23:]
+
+    def my_part(v):
+        r, n = v.shape
+        return lax.dynamic_index_in_dim(v.reshape(r, n // (4 * 16), 4, 16), f, 2, False)
+
+    def heads(r):
+        mine = jnp.where(core == 0, own[r], other[r])[:64].reshape(4, 16)[:, :GH]
+        theirs = jnp.where(core == 0, other[r], own[r])[:64].reshape(4, 16)[:, :GH]
+        every = jnp.concatenate([mine, theirs], 1)
+        return lax.dynamic_index_in_dim(every, f, 0, False)
+
+    conv = my_part(own[16:20])
+    grad_state_conv = lax.dynamic_slice_in_dim(shared[1:6, :256], f * 64, 64, 1)
+    return (
+        layer_out, grad_hidden, shared[0], g_gate, g_inner, g_state, own[:GH].T, conv, my_part(own[20:21])[0],
+        grad_state_conv[:4], grad_state_conv[4], heads(30), heads(29), heads(31), my_part(own[21:22])[0], g_out,
+    )
+
+
 def solution(mesh):
     fsdp = mesh.shape["fsdp"]
     halves = mesh.shape["tensor"] // 2
@@ -600,7 +1728,7 @@
     grid = P("fsdp", tensor)
     heads = P(tensor, "fsdp")
     return jax.shard_map(
-        functools.partial(on_device, fsdp, halves),
+        on_chip if (fsdp, halves) == (4, 4) else functools.partial(on_device, fsdp, halves),
         mesh=fine,
         in_specs=(
             tokens, P("fsdp"), grid, grid, P("fsdp", None), grid, P(None, tensor, "fsdp"), heads, P(None, "fsdp"),

time: 1100 us -> 334 us (0.30)
  waiting for transfers between devices: 663 us -> 0 us
  Pallas kernels: 106 us -> 309 us
  local copies, waits for them, and re-layouts: 132 us -> 22.4 us
  matrix products: 98 us -> 0 us
  blocking collectives: 54.3 us -> 0 us
  other arithmetic: 25.4 us -> 1.98 us
  between operations: 16 us -> 0.74 us
    reduce_scatter x3 -> x0, waiting for transfers between devices: 418 us -> none  [the longest x2 280 us: scatter_columns(): return lax.psum_scatter(g, both, scatter_dimension=0).astype(F32)]
    pallas_call x3 -> x2, Pallas kernels: 106 us -> 309 us  [the longest x1 164 us: backward_call(): pl.pallas_call(functools.partial(backward_kernel, model), out_shape=(sds(...]
    all_gather x3 -> x0, waiting for transfers between devices: 140 us -> none  [the longest x2 110 us: columns(): lax.all_gather(w, both, axis=0).reshape(fsdp, halves, depth, width)]
    unnamed x13 -> x0, waiting for transfers between devices: 104 us -> none
    dot_general x12 -> x0, matrix products: 98 us -> none  [mm(): return lax.dot_general(a, b, (dims, ((), ())), preferred_element_type=F32)]
    reshape x32 -> x3, local copies, waits for them, and re-layouts: 62.6 us -> 0.27 us  [my_part(): v.reshape(r, n // (4 * 16), 4, 16)]
    psum x1 -> x0, blocking collectives: 39.6 us -> none  [on_device(): mine = lax.psum(stacked, ('fsdp', 'zz', 'core'))]
    transpose x6 -> x1, local copies, waits for them, and re-layouts: 16.8 us -> 1.31 us  [on_chip(): own[:GH]]
  transfers between devices with their start and end apart: 16 -> 0, of which waited for: 10 -> 0; matrix products, arithmetic and copies ran while one was open for 20% -> 0% of each run, Pallas kernels for 4% -> 0%
where the time goes in v2:
time: 334 us
  Pallas kernels  309 us (93%)
  local copies, waits for them, and re-layouts  22.4 us (7%)
    pallas_call x1, Pallas kernels, backward_call(): pl.pallas_call(functools.partial(backward_kernel, model), out_shape=(sds(...  164 us
    pallas_call x1, Pallas kernels, forward_call(): pl.pallas_call(functools.partial(forward_kernel, model), out_shape=(sds((...  145 us
    unnamed x25, local copies, waits for them, and re-layouts  12.7 us

profile of v2, /device:TPU:0, one launch (start us, length us, event | category | flops | bytes accessed | tf_op | source)
XLA Modules:
  0.0 334.0 jit_solution(4873459784006252111)
XLA Ops:
  0.6 1.5 copy.38.step_ref
  2.1 0.9 dynamic-update-slice
  3.0 0.7 pad.14
  3.8 0.7 pad.15
  4.7 0.7 pad.16
  5.5 0.7 pad.17
  6.6 0.6 reshape.89.vec_ref
  7.2 1.3 copy.39.conv_ref
  8.5 145.1 %gather_and_forward.1 = (bf16[1536,1024]{1,0:T(8,128)(2,1)}, bf16[1024,1536]{1,0:T(8,128)(2,1)}, bf16[4,1536,768]{2,1,0:T(8,128)(2,1)}, bf16[4,384,1536]{2,1,0:T...) custom-call(bf16[512,1536]{1,0:T(8,128)(2,1)} %hid_ref.3, ...), custom_call_target="tpu_custom_call" | custom-call | tf_op jit(solution)/shard_map/gather_and_forward/pallas_call | solution.py:1053
  153.6 163.8 %backward_and_scatter.1 = (bf16[512,1536]{1,0:T(8,128)(2,1)}, bf16[512,1536]{1,0:T(8,128)(2,1)}, f32[384,384]{1,0:T(8,128)}, f32[384,384]{1,0:T(8,128)}, f32[384...) custom-call(bf16[512,1536]{1,0:T(8,128)(2,1)} %hid_ref.3, ...), custom_call_target="tpu_custom_call" | custom-call | tf_op jit(solution)/shard_map/backward_and_scatter/pallas_call | solution.py:1456
  317.4 1.0 fusion.4
  320.4 0.6 copy.49
  321.0 0.6 copy.50
  321.6 0.8 slice_add_fusion
  323.5 0.6 slice_reduce_fusion
  324.1 0.7 slice.94
  325.0 0.6 copy.48
  325.6 1.3 slice_bitcast_fusion
  326.9 2.7 copy.63
  329.6 1.1 copy.64
  330.8 0.8 copy.65
  331.6 0.8 copy.66
  332.4 0.7 copy.67
  333.2 0.8 copy.68
  (43 shorter events, 4.3 us)
Async XLA Ops:
  317.4 12.2 %copy-start = (bf16[512,1536]{1,0:T(8,128)(2,1)S(1)}, bf16[512,1536]{1,0:T(8,128)(2,1)}, u32[]{:S(2)}) copy-start(bf16[512,1536]{1,0:T(8,128)(2,1)} %get-tuple-element.111) | copy-start | bytes 4718596
  326.9 3.9 %copy-start.3 = (f32[384,384]{1,0:T(8,128)S(1)}, f32[384,384]{1,0:T(8,128)}, u32[]{:S(2)}) copy-start(f32[384,384]{1,0:T(8,128)} %get-tuple-element.113) | copy-start | bytes 1769476
  326.9 4.7 %copy-start.2 = (f32[384,384]{1,0:T(8,128)S(1)}, f32[384,384]{1,0:T(8,128)}, u32[]{:S(2)}) copy-start(f32[384,384]{1,0:T(8,128)} %get-tuple-element.114) | copy-start | bytes 1769476
  329.6 2.8 copy-start.4
  329.6 3.5 %copy-start.1 = (f32[384,384]{1,0:T(8,128)S(1)}, f32[384,384]{1,0:T(8,128)}, u32[]{:S(2)}) copy-start(f32[384,384]{1,0:T(8,128)} %get-tuple-element.125) | copy-start | bytes 1769476

commit v3 on v2

--- a/solution.py
+++ b/solution.py
@@ -416,9 +416,7 @@
 
 
 def prep_chunks(state_ref, step_ref, tok_ref, row_ref, convst_ref, head_ref,
-                bc_ref, bct_ref, g_ref, pack_ref, cumt_ref, pad_ref):
-    pad_ref[pl.ds(0, 8), :] = jnp.zeros((8, 256), F32)
-    pad_ref[pl.ds(8, SEQ), :] = state_ref[...]
+                bc_ref, bct_ref, g_ref, pack_ref, cumt_ref):
     lane = lax.broadcasted_iota(jnp.int32, (L, L), 1)
     sub = lax.broadcasted_iota(jnp.int32, (L, L), 0)
     tri = (sub >= lane).astype(BF)
@@ -430,7 +428,7 @@
         base = pl.multiple_of(c * L, L)
         rows = pl.ds(base, L)
         tok = tok_ref[rows, :]
-        total = conv_of(pad_ref[pl.ds(base, L + 8), :], tok, convst)
+        total = conv_of(state_ref[pl.ds(base, L + 8), :], tok, convst)
         act = total * sigmoid(total)
         low = act.astype(BF)
         bc_ref[rows, :] = low
@@ -449,28 +447,32 @@
         sig = sigmoid(v)
         cumt = cum.T
         for g in range(4):
-            part = slice(16 * g, 16 * g + 8)
-            pieces = [values[:, part] for values in (steps, cum, enter, leave, sig)]
-            pieces.append(jnp.zeros((L, 88), F32))
+            cumt_ref[g, c] = cumt[16 * g : 16 * g + 8, :]
+        for g in range(2):
+            pieces = []
+            for part in (slice(32 * g, 32 * g + 8), slice(32 * g + 16, 32 * g + 24)):
+                pieces += [values[:, part] for values in (steps, cum, enter, leave, sig)] + [jnp.zeros((L, 24), F32)]
             pack_ref[g, rows, :] = jnp.concatenate(pieces, 1)
-            cumt_ref[g, c] = cumt[part, :]
         return 0
 
     lax.fori_loop(0, CH, chunk, 0)
 
 
-def fwd_chunks(pre_ref, par_ref, tok_ref, bc_ref, bct_ref, g_ref, pack_ref, cumt_ref,
+def fwd_chunks(group, tick, pre_ref, par_ref, tok_ref, bc_ref, bct_ref, g_ref, pack_ref, cumt_ref,
                gated_ref, states_ref, ss_ref, st_ref):
     st_ref[...] = jnp.zeros_like(st_ref)
     par = par_ref[...]
 
     def chunk(c, _):
+        tick(c)
         base = pl.multiple_of(c * L, L)
         rows = pl.ds(base, L)
         tok = tok_ref[rows, :]
         u = conv_of(pre_ref[pl.ds(base, L + 8), :GW], tok, par)
         act = u * sigmoid(u)
         pack = pack_ref[rows, :]
+        if group % 2:
+            pack = pltpu.roll(pack, 64, 1)
         cumt = cumt_ref[c]
         g = g_ref[c]
         weighted = act * spread(pack, ST)
@@ -498,7 +500,7 @@
     lax.fori_loop(0, CH, chunk, 0)
 
 
-def bwd_chunks(group, z_k, tick, pre_ref, dinner_ref, par_ref, tok_ref, inv_ref, bc_ref, bct_ref, g_ref, pack_ref,
+def bwd_chunks(group, z_k, tick, pre_ref, dinner_ref, par_ref, tok_ref, bc_ref, bct_ref, g_ref, pack_ref,
                cumt_ref, states_ref, hpar_ref, dcat_ref, dstep_ref, pgrad_ref, hgrad_ref, rt_ref, dg_ref, dbc_ref):
     rt_ref[...] = jnp.zeros_like(rt_ref)
     pgrad_ref[...] = jnp.zeros_like(pgrad_ref)
@@ -525,6 +527,8 @@
         su = sigmoid(u)
         act = u * su
         pack = pack_ref[rows, :]
+        if group % 2:
+            pack = pltpu.roll(pack, 64, 1)
         cumt = cumt_ref[c]
         g = g_ref[c]
         steps = spread(pack, ST)
@@ -544,9 +548,8 @@
         gate = pre_ref[pl.ds(base + 8, L), GW:]
         sg = sigmoid(gate)
         silu = gate * sg
-        scaled = dinner_ref[rows, :] * par[P_GAIN : P_GAIN + 1, :]
-        inv = inv_ref[rows, :]
-        d_gated = inv[:, 0:1] * scaled - (ssd * silu) * inv[:, 1:2]
+        scaled = dinner_ref[rows, :].astype(F32) * par[P_GAIN : P_GAIN + 1, :]
+        d_gated = tok[:, T_INV : T_INV + 1] * scaled - (ssd * silu) * tok[:, T_BACK : T_BACK + 1]
         dy = d_gated * silu
         dcat_ref[rows, GW:] = (d_gated * ssd * sg * (1.0 + gate * (1.0 - sg))).astype(BF)
         dy_low = dy.astype(BF)
@@ -602,9 +605,7 @@
     lax.fori_loop(0, CH, chunk, jnp.zeros((8, GW), F32))
 
 
-def state_chunks(statepre_ref, cst_ref, tok_ref, row_ref, bc_ref, dg_ref, dbc_ref, dstate_ref, sgrad_ref, spad_ref):
-    spad_ref[pl.ds(0, 8), :] = jnp.zeros((8, 256), F32)
-    spad_ref[pl.ds(8, SEQ), :] = statepre_ref[...]
+def state_chunks(statepre_ref, cst_ref, tok_ref, row_ref, bc_ref, dg_ref, dbc_ref, dstate_ref, sgrad_ref):
     sgrad_ref[...] = jnp.zeros_like(sgrad_ref)
     cst = cst_ref[...]
     lane = lax.broadcasted_iota(jnp.int32, (L, L), 1)
@@ -619,7 +620,7 @@
         ds = jnp.where(same, dg_ref[c], 0.0).astype(BF)
         d_c = dbc_ref[rows, 128:] + mm(ds, bc_ref[rows, :128])
         d_b = dbc_ref[rows, :128] + mm(ds, bc_ref[rows, 128:], ((0,), (0,)))
-        window = spad_ref[pl.ds(base, L + 8), :]
+        window = statepre_ref[pl.ds(base, L + 8), :]
         w = conv_of(window, tok, cst)
         sw = sigmoid(w)
         dw = jnp.concatenate([d_b, d_c], 1) * (sw * (1.0 + w * (1.0 - sw)))
@@ -768,17 +769,64 @@
         tok_ref[pl.ds(c * L, L), :] = jnp.concatenate(rows, 0).T
 
 
-def forward_kernel(model, hid_ref, cot_ref, w0_ref, w1_ref, w2_ref, wst_ref, vec_ref, step_ref, conv_ref, shift_ref, gain_ref,
-                   cvst_ref, seg_ref,
-                   normt_out, cot_out, win_out, wout_out, pre_out, dinner_out, nin_out, nint_out, states_out,
-                   bc_ref, bct_ref, g_ref, pack_ref, cumt_ref, par_ref, hpar_ref, cst_ref, stw_ref, stbuf, gains_ref,
-                   statepre_ref, invp_ref, gaingrad_ref, tok_ref, docs_ref,
-                   small_ref, hall, call, win, wout, sbuf, pre, flip, ninner, gated, states, dinner, ss_ref, ssr_ref, pr_ref, prr_ref,
-                   spad_ref, st_ref, stepre_ref,
-                   sends, recvs, small_recvs, state_recvs, core_recvs, outs_sem, pre_sem, back_sem):
+ORDER = (3, 2, 1, 0)
+ROWS = 128
+SCHEDULE = {
+    "s1": [("second", 0, 0)],
+    "s2": [("second", 1, 0), ("first", 0, 1)],
+    "s5": [("second", 0, 1), ("first", 1, 1)],
+    "m05": [("second", 1, 1), ("first", 0, 2)],
+    "m10": [("second", 0, 2), ("first", 1, 2)],
+    "p2": [("second", 1, 2), ("first", 0, 3)],
+    "m20": [("second", 0, 3), ("first", 1, 3)],
+    "p3": [("second", 1, 3), ("first", 2, 0)],
+    "m30": [("second", 2, 0), ("first", 2, 1)],
+    "n1": [("second", 2, 1), ("first", 2, 2)],
+    "b10": [("second", 2, 2), ("first", 2, 3)],
+    "b30": [("second", 2, 3), ("s1", 0), ("s1", 1), ("s1", 2)],
+    "b31": [("s1", 3)],
+    "x2": [("s2", 0)],
+    "g02": [("s3", 0), ("s2", 1)],
+    "g06": [("s3", 1)],
+    "g07": [("s2", 2)],
+    "h01": [("s3", 2)],
+    "h02": [("s2", 3)],
+    "g14": [("last", 3), ("s2", 4)],
+    "h10": [("s3", 4)],
+    "h11": [("s2", 5)],
+    "g23": [("s3", 5)],
+    "g24": [("s2", 6)],
+    "h20": [("s3", 6)],
+    "h21": [("s2", 7)],
+    "g33": [("s3", 7)],
+    "g34": [("s2", 8)],
+    "h30": [("s3", 8)],
+    "h31": [("s2", 9)],
+    "t1": [("s3", 9)],
+    "t2": [("s2", 10)],
+    "t4": [("s2", 11), ("last", 10)],
+    "t5": [("last", 11)],
+}
+T_INV, T_BACK = 16, 17
+
+
+def block_kernel(model, hid_ref, cot_ref, w0_ref, w1_ref, w2_ref, wst_ref, vec_ref, step_ref, conv_ref, shift_ref, gain_ref,
+                 cvst_ref, seg_ref,
+                 layer_out, hidden_out, normt_hbm, win_hbm, pre_hbm, states_hbm,
+                 ginner_out, ggate_out, gout_out, gstate_ref, gsmall_ref, gother_ref,
+                 hall, call, win, wout, pre, accr, flip, gated, states, halfr, recv1, recv2, recv3, stage,
+                 small_ref, sbuf, stbuf, statepre_ref, ss_ref, ssr_ref, tok_ref, docs_ref,
+                 bc_ref, bct_ref, g_ref, pack_ref, cumt_ref, par_ref, hpar_ref, cst_ref, stw_ref, gains_ref, gaingrad_ref, st_ref,
+                 srecv, srecv1, srecv3, srecvc, qrecv1, qrecv3, qsend, qrecvc, nparts, nrecv, nback,
+                 dstep, dstate, pgrad, hgrad, sgrad, rt_ref, dg_ref, dbc_ref,
+                 sends, recvs, small_recvs, state_recvs, core_recvs, recv_sems, core_sems, state_sems, gain_sems,
+                 outs_sem, pre_sem, state_sem, own_sem, load_sems, stage_sem, hid_sem, credit, free_out, free_core, free_half):
+    stepre_ref = pr_ref = ss_ref
+    dcat = hall.at[:, pl.ds(0, 2 * GW)]
     here = Place()
     z, zk = here.z, here.zk
     rows_own = hid_ref.shape[0]
+    wide = 2 * GW
     depth = model // 4
     links = Links(sends)
     shards = [w0_ref, w1_ref, w2_ref]
@@ -792,11 +840,13 @@
     here.greet()
     small_ref[...] = small_block(here.f, vec_ref, step_ref, conv_ref, shift_ref, gain_ref, cvst_ref)
     here.greeted()
+    mine = pl.ds(pl.multiple_of(here.c * rows_own, rows_own), rows_own)
+    other = pl.ds(pl.multiple_of((1 - here.c) * rows_own, rows_own), rows_own)
+    core = here.at(c=1 - here.c)
+    one_block = recv2.at[0]
     for k in (1, 2, 3):
         links.send(("small", k), small_ref, sbuf.at[here.f, z], small_recvs.at[k], here.at(z=zk[k]))
-    mine = pl.ds(pl.multiple_of(here.c * rows_own, rows_own), rows_own)
-    links.send("hidden", hid_ref, hall.at[mine], core_recvs.at[0], here.at(c=1 - here.c))
-    sbuf[here.f, z] = small_ref[...]
+    links.send("hidden", hid_ref, hall.at[mine], core_recvs.at[0], core)
 
     def recv_sem(m, f, z_):
         return recvs.at[m, f, z_]
@@ -806,39 +856,49 @@
             links.send(("z", m, k), shards[m], piece(win, wout, m, here.f, z), recv_sem(m, here.f, z), here.at(z=zk[k]))
 
     def first(m, k):
-        src = shards[m] if k == 0 else piece(win, wout, m, here.f, zk[k])
+        dst = piece(win, wout, m, here.f, zk[k])
+        src = shards[m] if k == 0 else dst
         if k:
-            links.arrived(src, recv_sem(m, here.f, zk[k]), here.at(z=zk[k]))
-        dst = piece(win, wout, m, here.f, zk[k])
-        links.send(("first", m, k, 2), src, dst, recv_sem(m, here.f, zk[k]), here.at(f=here.f2))
-        links.send(("first", m, k, 3), src, dst, recv_sem(m, here.f, zk[k]), here.at(f=here.f3))
+            links.arrived(dst, recv_sem(m, here.f, zk[k]), here.at(z=zk[k]))
+        links.send(("first", m, k, 2), src, dst, recv_sem(m, here.f, zk[k]), here.at(f=here.f2), one_block)
+        links.send(("first", m, k, 3), src, dst, recv_sem(m, here.f, zk[k]), here.at(f=here.f3), one_block)
 
     def second(m, k):
         src = piece(win, wout, m, here.f2, zk[k])
         links.arrived(src, recv_sem(m, here.f2, zk[k]), here.at(f=here.f2))
-        links.send(("second", m, k), src, src, recv_sem(m, here.f2, zk[k]), here.at(f=here.f3))
+        links.send(("second", m, k), src, src, recv_sem(m, here.f2, zk[k]), here.at(f=here.f3), one_block)
 
     def third(m, k):
         for f in (here.f3, here.f4):
             src = piece(win, wout, m, f, zk[k])
             links.arrived(src, recv_sem(m, f, zk[k]), here.at(f=here.f3))
 
+    events = {"first": first, "second": second}
+
+    def due(slot):
+        for name, *what in SCHEDULE.get(slot, ()):
+            events[name](*what)
+
+    def ticker(prefix):
+        def tick(step):
+            for at in range(CH):
+                if prefix + str(at) in SCHEDULE:
+                    pl.when(step == at)(functools.partial(due, prefix + str(at)))
+
+        return tick
+
+    def state_of(f, part):
+        return stbuf.at[f, :, part]
+
     push_z(0)
-    push_z(1)
-    first(0, 0)
-    first(1, 0)
-    first(2, 0)
-    half_state = pl.ds(pl.multiple_of(here.c * 128, 128), 128)
-    rest_state = pl.ds(pl.multiple_of(128 - here.c * 128, 128), 128)
-    links.send(("state", 0), wst_ref.at[:, half_state], stbuf.at[here.f, :, half_state], state_recvs.at[0], here.at(f=here.f2))
-    links.send(("state", 1), wst_ref.at[:, half_state], stbuf.at[here.f, :, half_state], state_recvs.at[1], here.at(f=here.f3))
-    links.send("cot", cot_ref, call.at[mine], core_recvs.at[1], here.at(c=1 - here.c))
-    win[z, pl.ds(pl.multiple_of(here.f * depth, depth), depth), pl.ds(0, GW)] = w0_ref[...]
-    win[z, pl.ds(pl.multiple_of(here.f * depth, depth), depth), pl.ds(GW, GW)] = w1_ref[...]
-    wout[z, :, pl.ds(pl.multiple_of(here.f * depth, depth), depth)] = w2_ref[...]
+    links.send("cot", cot_ref, call.at[mine], core_recvs.at[1], core)
+    own_copies = [pltpu.make_async_copy(shards[m], piece(win, wout, m, here.f, z), own_sem.at[m]) for m in range(3)]
+    own_copies.append(pltpu.make_async_copy(cot_ref, call.at[mine], own_sem.at[3]))
+    own_copies.append(pltpu.make_async_copy(hid_ref, hall.at[mine], hid_sem.at[4]))
+    for copy in own_copies:
+        copy.start()
+    sbuf[here.f, z] = small_ref[...]
     stbuf[here.f] = wst_ref[...]
-    hall[mine] = hid_ref[...]
-    call[mine] = cot_ref[...]
     docs = seg_ref[pl.ds(pl.multiple_of(z * CH, CH), CH), :].astype(F32)
     docs_ref[...] = docs
     token_masks(docs, tok_ref)
@@ -846,19 +906,20 @@
         links.arrived(sbuf.at[here.f, zk[k]], small_recvs.at[k], here.at(z=zk[k]))
     links.send(("small", 4), sbuf.at[here.f], sbuf.at[here.f], small_recvs.at[4], here.at(f=here.f2))
     links.send(("small", 5), sbuf.at[here.f], sbuf.at[here.f], small_recvs.at[5], here.at(f=here.f3))
+    half_state = pl.ds(pl.multiple_of(here.c * 128, 128), 128)
+    rest_state = pl.ds(pl.multiple_of(128 - here.c * 128, 128), 128)
+    links.send(("state", 0), wst_ref.at[:, half_state], state_of(here.f, half_state), state_recvs.at[0], here.at(f=here.f2))
+    links.send(("state", 1), wst_ref.at[:, half_state], state_of(here.f, half_state), state_recvs.at[1], here.at(f=here.f3))
+    first(0, 0)
+    push_z(1)
     links.arrived(sbuf.at[here.f2], small_recvs.at[4], here.at(f=here.f2))
     links.send(("small", 6), sbuf.at[here.f2], sbuf.at[here.f2], small_recvs.at[6], here.at(f=here.f3))
-    def state_of(f, part):
-        return stbuf.at[f, :, part]
-
     links.arrived(state_of(here.f2, half_state), state_recvs.at[0], here.at(f=here.f2))
     links.send(("state", 2), state_of(here.f2, half_state), state_of(here.f2, half_state), state_recvs.at[2], here.at(f=here.f3))
-    links.send(("state", 3), state_of(here.f2, half_state), state_of(here.f2, half_state), state_recvs.at[3], here.at(c=1 - here.c))
-    other = pl.ds(pl.multiple_of((1 - here.c) * rows_own, rows_own), rows_own)
-    links.arrived(hall.at[other], core_recvs.at[0], here.at(c=1 - here.c))
+    links.send(("state", 3), state_of(here.f2, half_state), state_of(here.f2, half_state), state_recvs.at[3], core)
+    first(1, 0)
     push_z(2)
-    first(0, 1)
-    second(0, 0)
+    due("s0")
     links.arrived(sbuf.at[here.f3], small_recvs.at[5], here.at(f=here.f3))
     links.arrived(sbuf.at[here.f4], small_recvs.at[6], here.at(f=here.f3))
 
@@ -887,6 +948,10 @@
     decay = -jnp.exp(own_heads[1:2, :])
     hpar_ref[...] = jnp.concatenate([own_heads[0:1], decay, own_heads[2:3], jnp.zeros((5, 128), F32)], 0)
 
+    due("s1")
+    own_copies[4].wait()
+    links.arrived(hall.at[other], core_recvs.at[0], core)
+
     def norm(i, _):
         rows = pl.ds(pl.multiple_of(i * L, L), L)
         x = hall[rows, :].astype(F32)
@@ -895,14 +960,13 @@
         return 0
 
     lax.fori_loop(0, SEQ // L, norm, 0)
-    first(1, 1)
-    second(1, 0)
+    due("s2")
     links.arrived(state_of(here.f3, half_state), state_recvs.at[1], here.at(f=here.f3))
-    links.send(("state", 4), state_of(here.f3, half_state), state_of(here.f3, half_state), state_recvs.at[4], here.at(c=1 - here.c))
+    links.send(("state", 4), state_of(here.f3, half_state), state_of(here.f3, half_state), state_recvs.at[4], core)
     links.arrived(state_of(here.f4, half_state), state_recvs.at[2], here.at(f=here.f3))
-    links.send(("state", 5), state_of(here.f4, half_state), state_of(here.f4, half_state), state_recvs.at[5], here.at(c=1 - here.c))
+    links.send(("state", 5), state_of(here.f4, half_state), state_of(here.f4, half_state), state_recvs.at[5], core)
     for n, f in ((3, here.f3), (4, here.f2), (5, here.f4)):
-        links.arrived(state_of(f, rest_state), state_recvs.at[n], here.at(c=1 - here.c))
+        links.arrived(state_of(f, rest_state), state_recvs.at[n], core)
 
     TILE = 256
 
@@ -911,12 +975,15 @@
         total = jnp.zeros((TILE, 256), F32)
         for f in range(4):
             total = total + mm(hall[rows, pl.ds(depth * f, depth)], stbuf[f])
-        statepre_ref[rows, :] = total
+        statepre_ref[pl.ds(pl.multiple_of(i * TILE + 8, 8), TILE), :] = total
         steps = mm(hall[rows, :], stw_ref[...], ((1,), (1,)))
         stepre_ref[rows, :] = jnp.concatenate([steps, jnp.zeros((TILE, 64), F32)], 1)
         return 0
 
+    statepre_ref[pl.ds(0, 8), :] = jnp.zeros((8, 256), F32)
     lax.fori_loop(0, SEQ // TILE, project_small, 0)
+
+    due("s3")
 
     def turn(i, _):
         for half in range(2):
@@ -926,34 +993,21 @@
 
     lax.fori_loop(0, model // 256, turn, 0)
     TURNED = len(outs)
-    put(flip, normt_out)
-    prep_chunks(statepre_ref, stepre_ref, tok_ref, docs_ref, cst_ref, hpar_ref, bc_ref, bct_ref, g_ref, pack_ref, cumt_ref,
-                spad_ref)
-    units = [(k, m) for k in range(4) for m in (0, 1)] + [(k, 2) for k in range(4)]
-    done = [3, 1]
-
-    def advance(i):
-        while done[0] < min(i + 3, len(units) - 1) or done[1] < min(i + 1, len(units) - 1):
-            if done[0] < min(i + 3, len(units) - 1):
-                done[0] += 1
-                k, m = units[done[0]]
-                if (k, m) != (0, 2):
-                    first(m, k)
-            if done[1] < min(i + 1, len(units) - 1):
-                done[1] += 1
-                k, m = units[done[1]]
-                second(m, k)
-
-    links.arrived(call.at[other], core_recvs.at[1], here.at(c=1 - here.c))
-    put(call, cot_out)
+    put(flip, normt_hbm)
+    due("s4")
+    prep_chunks(statepre_ref, stepre_ref, tok_ref, docs_ref, cst_ref, hpar_ref, bc_ref, bct_ref, g_ref, pack_ref, cumt_ref)
+    due("s5")
+    links.arrived(call.at[other], core_recvs.at[1], core)
+    for copy in own_copies[:4]:
+        copy.wait()
     ss_ref[...] = jnp.zeros_like(ss_ref)
     for slot in range(2):
         pre[slot, pl.ds(0, 8), :] = jnp.zeros((8, 2 * GW), F32)
     pre_copies = []
+    state_copies = []
     for k in range(4):
-        advance(2 * k)
+        due("p%d" % k)
         third(0, k)
-        advance(2 * k + 1)
         third(1, k)
         slot = k % 2
         if k >= 2:
@@ -966,159 +1020,48 @@
             return 0
 
         lax.fori_loop(0, SEQ // TILE, project, 0)
-        copy = pltpu.make_async_copy(pre.at[slot, pl.ds(8, SEQ)], pre_out.at[k], pre_sem.at[k])
+        copy = pltpu.make_async_copy(pre.at[slot, pl.ds(8, SEQ)], pre_hbm.at[k], pre_sem.at[k])
         copy.start()
         pre_copies.append(copy)
-        put(win.at[zk[k]], win_out.at[k])
-        advance(2 * k + 2)
-        fwd_chunks(pre.at[slot], par_ref.at[k], tok_ref, bc_ref, bct_ref, g_ref, pack_ref.at[k], cumt_ref.at[k],
-                   gated.at[k], states.at[k], ss_ref, st_ref)
-        put(states.at[k], states_out.at[k])
-    pre_copies[2].wait()
-    pre_copies[3].wait()
-
-    links.send("squares", ss_ref, ssr_ref, core_recvs.at[2], here.at(c=1 - here.c))
-    advance(8)
-    links.arrived(ssr_ref, core_recvs.at[2], here.at(c=1 - here.c))
+        put(win.at[zk[k]], win_hbm.at[k])
+        if k:
+            state_copies[k - 1].wait()
+        fwd_chunks(k, ticker("m%d" % k), pre.at[slot], par_ref.at[k], tok_ref, bc_ref, bct_ref, g_ref, pack_ref.at[k // 2], cumt_ref.at[k],
+                   gated.at[k], states, ss_ref, st_ref)
+        copy = pltpu.make_async_copy(states, states_hbm.at[k], state_sem.at[k])
+        copy.start()
+        state_copies.append(copy)
+    for copy in pre_copies[2:] + state_copies[3:]:
+        copy.wait()
+
+    links.send("squares", ss_ref, ssr_ref, core_recvs.at[2], core)
+    due("n0")
+    links.arrived(ssr_ref, core_recvs.at[2], core)
     inner_all = 2 * 4 * GW
 
     def inner_norm(i, _):
         rows = pl.ds(pl.multiple_of(i * L, L), L)
         total = jnp.sum(ss_ref[rows, :] + ssr_ref[rows, :], 1, keepdims=True)
         inv = lax.rsqrt(total / inner_all + EPSILON)
-        invp_ref[rows, :] = jnp.broadcast_to(inv, (L, 128))
+        tok_ref[rows, :] = jnp.where(iota((L, 128), 1) == T_INV, inv, tok_ref[rows, :])
         for k in range(4):
             gain = par_ref[k, P_GAIN : P_GAIN + 1, :]
             low = (gated[k, rows, :].astype(F32) * inv * gain).astype(BF)
-            ninner[k, rows, :] = low
+            hall[rows, pl.ds(k * GW, GW)] = low
             flip[pl.ds(k * GW, GW), rows] = low.T
         pr_ref[rows, :] = jnp.zeros((L, 128), F32)
         return 0
 
-    outs[TURNED].wait()
-    outs[TURNED] = None
+    links.left("squares", core_recvs.at[0], core)
+    for copy in outs:
+        copy.wait()
     lax.fori_loop(0, SEQ // L, inner_norm, 0)
-    put(ninner, nin_out)
-    put(flip, nint_out)
-    back_copies = []
-    for k in range(4):
-        advance(8 + k)
-        third(2, k)
-        slot = k % 2
-        if k >= 2:
-            back_copies[k - 2].wait()
-        gaingrad_ref[k] = jnp.zeros((8, GW), F32)
-
-        def back(i, _, slot=slot, k=k):
-            rows = pl.ds(pl.multiple_of(i * TILE, TILE), TILE)
-            d = mm(call[rows, :], wout[zk[k]], ((1,), (1,)))
-            dinner[slot, rows, :] = d
-            both = d * gated[k, rows, :].astype(F32)
-            gaingrad_ref[k, 0:1, :] += jnp.sum(both * invp_ref[rows, 0:1], 0, keepdims=True)
-            both = both * par_ref[k, P_GAIN : P_GAIN + 1, :]
-            pr_ref[rows, :] += both[:, :128] + both[:, 128:256] + both[:, 256:]
-            return 0
-
-        lax.fori_loop(0, SEQ // TILE, back, 0)
-        copy = pltpu.make_async_copy(dinner.at[slot], dinner_out.at[k], back_sem.at[k])
-        copy.start()
-        back_copies.append(copy)
-        put(wout.at[zk[k]], wout_out.at[k])
-    links.send("products", pr_ref, prr_ref, core_recvs.at[3], here.at(c=1 - here.c))
-    links.arrived(prr_ref, core_recvs.at[3], here.at(c=1 - here.c))
-
-    def scale(i, _):
-        rows = pl.ds(pl.multiple_of(i * L, L), L)
-        total = jnp.sum(pr_ref[rows, :] + prr_ref[rows, :], 1, keepdims=True)
-        inv = invp_ref[rows, :]
-        lane = lax.broadcasted_iota(jnp.int32, (L, 128), 1)
-        invp_ref[rows, :] = jnp.where(lane == 0, inv, inv * inv * inv * (total / inner_all))
-        return 0
-
-    lax.fori_loop(0, SEQ // L, scale, 0)
-    back_copies[2].wait()
-    back_copies[3].wait()
-    for copy in outs:
-        if copy is not None:
-            copy.wait()
-    links.finish(core_recvs.at[0], here.at(c=1 - here.c))
-
-
-def forward_call(model, hidden, cot, *args):
-    rows = hidden.shape[0]
-    any_ = pl.BlockSpec(memory_space=pl.ANY)
-    sds = jax.ShapeDtypeStruct
-    inner = 4 * GW
-    depth = model // 4
-    return pl.pallas_call(
-        functools.partial(forward_kernel, model),
-        out_shape=(
-            sds((model, SEQ), BF), sds((SEQ, model), BF), sds((4, model, 2 * GW), BF), sds((4, GW, model), BF),
-            sds((4, SEQ, 2 * GW), F32), sds((4, SEQ, GW), F32), sds((4, SEQ, GW), BF),
-            sds((4 * GW, SEQ), BF), sds((4, CH, 128, GW), BF),
-            sds((SEQ, 256), BF), sds((CH, 256, L), BF), sds((CH, L, L), F32), sds((4, SEQ, 128), F32),
-            sds((4, CH, 8, L), F32), sds((4, 8, GW), F32), sds((8, 128), F32), sds((8, 256), F32),
-            sds((64, model), BF), sds((4, depth, 256), BF), sds((8, model), F32), sds((SEQ, 256), F32), sds((SEQ, 128), F32),
-            sds((4, 8, GW), F32), sds((SEQ, 128), F32), sds((CH, L), F32),
-        ),
-        in_specs=[vm()] * (2 + len(args)),
-        out_specs=tuple([any_] * 9 + [vm()] * 16),
-        scratch_shapes=[
-            pltpu.VMEM((SMALL, GW), BF),
-            pltpu.VMEM((SEQ, model), BF),
-            pltpu.VMEM((SEQ, model), BF),
-            pltpu.VMEM((4, model, 2 * GW), BF),
-            pltpu.VMEM((4, GW, model), BF),
-            pltpu.VMEM((4, 4, SMALL, GW), BF),
-            pltpu.VMEM((2, SEQ + 8, 2 * GW), F32),
-            pltpu.VMEM((model, SEQ), BF),
-            pltpu.VMEM((4, SEQ, GW), BF),
-            pltpu.VMEM((4, SEQ, GW), BF),
-            pltpu.VMEM((4, CH, 128, GW), BF),
-            pltpu.VMEM((2, SEQ, GW), F32),
-            pltpu.VMEM((SEQ, 128), F32),
-            pltpu.VMEM((SEQ, 128), F32),
-            pltpu.VMEM((SEQ, 128), F32),
-            pltpu.VMEM((SEQ, 128), F32),
-            pltpu.VMEM((SEQ + 8, 256), F32),
-            pltpu.VMEM((128, GW), F32),
-            pltpu.VMEM((SEQ, 128), F32),
-            pltpu.SemaphoreType.DMA((64,)),
-            pltpu.SemaphoreType.DMA((3, 4, 4)),
-            pltpu.SemaphoreType.DMA((7,)),
-            pltpu.SemaphoreType.DMA((6,)),
-            pltpu.SemaphoreType.DMA((4,)),
-            pltpu.SemaphoreType.DMA((16,)),
-            pltpu.SemaphoreType.DMA((4,)),
-            pltpu.SemaphoreType.DMA((4,)),
-        ],
-        compiler_params=pltpu.CompilerParams(vmem_limit_bytes=VMEM_LIMIT, collective_id=1, has_side_effects=True),
-        name="gather_and_forward",
-    )(hidden, cot, *args)
-
-
-ORDER = (3, 2, 1, 0)
-
-
-def backward_kernel(model, hid_ref, tok_ref, row_ref, inv_ref, bc_ref, bct_ref, g_ref, cumt_ref, par_ref,
-                    hpar_ref, cst_ref, stw_ref, stbuf_ref, statepre_ref, gaingrad_ref, gains_ref,
-                    normt_in, cot_in, win_in, wout_in, pre_in, dinner_in, nin_in, nint_in, states_in, pack_in,
-                    layer_out, hidden_out, ginner_ref, ggate_ref, gout_ref, gstate_ref, gsmall_ref, gother_ref,
-                    normt, cot, win, pre, dinner, states, pack, acc, half, halfr, dcat, parts, recv1, recv2, recv3,
-                    sparts, ssend, srecv, srecv1, srecv2, srecv3, srecvc, qparts, qrecv1, qrecv3, qsend, qrecvc,
-                    dstep, dstate, pgrad, hgrad, sgrad, rt_ref, dg_ref, dbc_ref, spad_ref,
-                    sends, recv_sems, core_sems, load_sems, credit1, credit2):
-    here = Place()
-    zk = here.zk
+    pl.semaphore_signal(free_core, inc=1, device_id=core, device_id_type=MESH)
     f, f2, f3, f4 = here.f, here.f2, here.f3, here.f4
-    links = Links(sends)
-    depth = model // 4
-    rows_own = hid_ref.shape[0]
-    mine = pl.ds(pl.multiple_of(here.c * rows_own, rows_own), rows_own)
-    across = pl.ds(pl.multiple_of((1 - here.c) * rows_own, rows_own), rows_own)
-    units = [(k, 2) for k in ORDER] + [(k, m) for k in ORDER for m in (0, 1)]
-    ROWS = 128
-
+    for m in (0, 1):
+        for k in range(4):
+            for name in (("first", m, k, 2), ("first", m, k, 3), ("second", m, k)):
+                links.left(name, core_recvs.at[0], core)
     loads = {}
 
     def load(name, src, dst, sem):
@@ -1126,256 +1069,296 @@
         copy.start()
         loads[name] = copy
 
-    wouts = [halfr.at[1, pl.ds(0, GW)], half.at[pl.ds(0, GW)]]
-
-    def nin(i):
-        return dcat.at[:, pl.ds(GW * (i % 2), GW)]
-
-    def load_out(i):
+    accl = pre.at[0, pl.ds(8, SEQ)]
+
+    def slot_of(u):
+        return (u % 6) // 2, u % 2
+
+    def part(u, f_):
+        at, side = slot_of(u)
+        return win.at[at, pl.ds(pl.multiple_of(f_ * depth, depth), depth), pl.ds(side * GW, GW)]
+
+    def landing(u, n):
+        if u < 4:
+            return recv1.at[u, n]
+        n += 2 * (u - 4)
+        return wout.at[n // 4, :, pl.ds((n % 4) * GW, GW)]
+
+    def s1(u):
+        for n, f_ in enumerate((f3, f4)):
+            links.send(("s1", u, n), part(u, f_), landing(u, n), recv_sems.at[u, n], here.at(f=f3), one_block)
+
+    units = [(k, 2) for k in ORDER] + [(k, m) for k in ORDER for m in (0, 1)]
+
+    def add_into(dst, src):
+        rows, width = dst.shape
+
+        def body(i, _):
+            at = pl.ds(pl.multiple_of(i * ROWS, ROWS), ROWS)
+            dst[at, :] = (dst[at, :].astype(F32) + src[at, :].astype(F32)).astype(dst.dtype)
+            return 0
+
+        lax.fori_loop(0, rows // ROWS, body, 0)
+
+    def s2(u):
+        links.arrived(landing(u, 1), recv_sems.at[u, 1], here.at(f=f3))
+        add_into(part(u, f2), landing(u, 1))
+        if u >= 4:
+            pl.semaphore_wait(credit, 1)
+        links.send(("s2", u), part(u, f2), recv2.at[u % 4], recv_sems.at[u, 2], here.at(f=f2), one_block)
+        links.arrived(landing(u, 0), recv_sems.at[u, 0], here.at(f=f3))
+        add_into(part(u, f), landing(u, 0))
+
+    def give_credit(u):
+        if u < 8:
+            pl.semaphore_signal(credit, inc=1, device_id=here.at(f=f2), device_id_type=MESH)
+
+    outs = {0: ginner_out, 1: ggate_out, 2: gout_out}
+    results = [pltpu.make_async_copy(stage, outs[m], stage_sem.at[m]) for m in range(3)]
+    staged = []
+
+    def s3(u):
+        k, m = units[u]
+        links.arrived(recv2.at[u % 4], recv_sems.at[u, 2], here.at(f=f2))
+        add_into(part(u, f), recv2.at[u % 4])
+        give_credit(u)
+        links.send(("s3", u), part(u, f), recv3.at[m, k - 1], recv_sems.at[12 + m, k - 1], here.at(z=zk[k]), one_block)
+
+    def last_sum(u):
+        k, m = units[u]
+        links.arrived(recv2.at[u % 4], recv_sems.at[u, 2], here.at(f=f2))
+        for j in (1, 2, 3):
+            links.arrived(recv3.at[m, j - 1], recv_sems.at[12 + m, j - 1], here.at(z=zk[j]))
+        own = part(u, f)
+        if staged:
+            results[staged[-1]].wait()
+
+        def body(i, _):
+            at = pl.ds(pl.multiple_of(i * ROWS, ROWS), ROWS)
+            total = own[at, :].astype(F32) + recv2[u % 4, at, :].astype(F32)
+            for j in range(3):
+                total = total + recv3[m, j, at, :].astype(F32)
+            stage[at, :] = total
+            return 0
+
+        lax.fori_loop(0, GW // ROWS, body, 0)
+        give_credit(u)
+        staged.append(m)
+        results[m].start()
+
+    events.update({"s1": s1, "s2": s2, "s3": s3, "last": last_sum})
+
+    def grad_out(i):
         k = ORDER[i]
-        load(("nin", i), nin_in.at[k], nin(i), 2 * (i % 2))
-        load(("wout", i), wout_in.at[k], wouts[i % 2], 2 * (i % 2) + 1)
-
-    def load_group(i):
-        k = ORDER[i]
-        load(("pre", i), pre_in.at[k], pre.at[pl.ds(8, SEQ)], 8)
-        load(("dinner", i), dinner_in.at[k], dinner, 9)
-        load(("states", i), states_in.at[k], states, 10)
-        load(("pack", i), pack_in.at[k], pack, 5)
-
-    def load_win(i):
-        load(("win", i), win_in.at[ORDER[i]], win, 11)
-
-    load("nint", nint_in, normt, 4)
-    load("cot", cot_in, cot, 6)
-    load_out(0)
-    load_out(1)
-    load_group(0)
-    load_win(0)
-    pre[pl.ds(0, 8), :] = jnp.zeros((8, 2 * GW), F32)
+        at, side = slot_of(i)
+
+        def rows_of(j, _):
+            src = pl.ds(pl.multiple_of(k * GW + j * ROWS, ROWS), ROWS)
+            total = mm(flip[src, :], call[...])
+            for f_ in range(4):
+                to = pl.ds(pl.multiple_of(f_ * depth + j * ROWS, ROWS), ROWS)
+                win[at, to, pl.ds(side * GW, GW)] = total[:, f_ * depth : (f_ + 1) * depth].astype(BF)
+            return 0
+
+        lax.fori_loop(0, GW // ROWS, rows_of, 0)
+
+    hid_copies = []
+    for side in range(2):
+        src = hid_ref.at[:, pl.ds(side * wide, wide)]
+        hid_copies.append(pltpu.make_async_copy(src, halfr.at[pl.ds(side * rows_own, rows_own)], hid_sem.at[side]))
+        hid_copies[-1].start()
+    due("n1")
+    for k in range(4):
+        due("b%d0" % k)
+        grad_out(k)
+        due("b%d1" % k)
+        third(2, k)
+        gaingrad_ref[k] = jnp.zeros((8, GW), F32)
+
+        def back(i, _, k=k):
+            rows = pl.ds(pl.multiple_of(i * TILE, TILE), TILE)
+            d = mm(call[rows, :], wout[zk[k]], ((1,), (1,)))
+            both = d * gated[k, rows, :].astype(F32)
+            gated[k, rows, :] = d.astype(BF)
+            gaingrad_ref[k, 0:1, :] += jnp.sum(both * tok_ref[rows, T_INV : T_INV + 1], 0, keepdims=True)
+            both = both * par_ref[k, P_GAIN : P_GAIN + 1, :]
+            pr_ref[rows, :] += both[:, :128] + both[:, 128:256] + both[:, 256:]
+            return 0
+
+        lax.fori_loop(0, SEQ // TILE, back, 0)
+    pl.semaphore_wait(free_core, 1)
+    links.send("products", pr_ref, ssr_ref, core_recvs.at[3], core)
+    due("x0")
+    load("normt", normt_hbm, flip, 0)
+    load(("win", 0), win_hbm.at[ORDER[0]], win.at[3], 1)
+
+    def mix_rows(i, _):
+        rows = pl.ds(pl.multiple_of(i * TILE, TILE), TILE)
+        for k in range(4):
+            mixed = mm(hall[rows, pl.ds(k * GW, GW)], wout[zk[k]])
+            accl[rows, :] = mixed[:, :wide] if k == 0 else accl[rows, :] + mixed[:, :wide]
+            accr[rows, :] = mixed[:, wide:] if k == 0 else accr[rows, :] + mixed[:, wide:]
+        return 0
+
+    lax.fori_loop(0, SEQ // TILE, mix_rows, 0)
+    due("x1")
+    half = hall.at[:, pl.ds(0, wide)]
+    halves = [halfr, hall.at[:, pl.ds(wide, wide)]]
+
+    def exchange(n):
+        def body(j, _):
+            src = pl.ds(pl.multiple_of((1 - here.c) * rows_own + j * ROWS, ROWS), ROWS)
+            half[pl.ds(pl.multiple_of(j * ROWS, ROWS), ROWS), :] = accl[src, :].astype(BF)
+            half[pl.ds(pl.multiple_of(rows_own + j * ROWS, ROWS), ROWS), :] = accr[src, :].astype(BF)
+            return 0
+
+        lax.fori_loop(0, rows_own // ROWS, body, 0)
+        links.send(("half", n), half, halves[n], core_sems.at[n], core)
+
+    def received(n):
+        links.arrived(halves[n], core_sems.at[n], core)
+
+    def places(j):
+        own = pl.ds(pl.multiple_of(here.c * rows_own + j * ROWS, ROWS), ROWS)
+        at = pl.ds(pl.multiple_of(j * ROWS, ROWS), ROWS)
+        below = pl.ds(pl.multiple_of(rows_own + j * ROWS, ROWS), ROWS)
+        return own, at, below
+
+    def summed(n, j):
+        own, at, below = places(j)
+        left = accl[own, :] + halves[n][at, :].astype(F32)
+        right = accr[own, :] + halves[n][below, :].astype(F32)
+        return own, at, below, jnp.concatenate([left, right], 1)
+
+    def store(n, at, below, values):
+        halves[n][at, :] = values[:, :wide].astype(BF)
+        halves[n][below, :] = values[:, wide:].astype(BF)
+
+    def give(n, out, sem):
+        for side in range(2):
+            load((n, side), halves[n].at[pl.ds(side * rows_own, rows_own)], out.at[:, pl.ds(side * wide, wide)], sem + side)
+
+    def add_hidden(j, _):
+        own, at, below = places(j)
+        accl[own, :] = accl[own, :] + halfr[at, :].astype(F32)
+        accr[own, :] = accr[own, :] + halfr[below, :].astype(F32)
+        return 0
+
+    for copy in hid_copies:
+        copy.wait()
+    lax.fori_loop(0, rows_own // ROWS, add_hidden, 0)
+    pl.semaphore_signal(free_half, inc=1, device_id=core, device_id_type=MESH)
+    pl.semaphore_wait(free_half, 1)
+    exchange(0)
+    due("x2")
+    links.arrived(ssr_ref, core_recvs.at[3], core)
+
+    def scale(i, _):
+        rows = pl.ds(pl.multiple_of(i * L, L), L)
+        total = jnp.sum(pr_ref[rows, :] + ssr_ref[rows, :], 1, keepdims=True)
+        tok = tok_ref[rows, :]
+        inv = tok[:, T_INV : T_INV + 1]
+        tok_ref[rows, :] = jnp.where(iota((L, 128), 1) == T_BACK, inv * inv * inv * (total / inner_all), tok)
+        return 0
+
+    lax.fori_loop(0, SEQ // L, scale, 0)
+    for k in range(4):
+        for name in (("first", 2, k, 2), ("first", 2, k, 3), ("second", 2, k)):
+            links.left(name, core_recvs.at[0], core)
+    pl.semaphore_signal(free_out, inc=1, device_id=here.at(f=f3), device_id_type=MESH)
+    links.left(("half", 0), core_sems.at[0], core)
     hgrad[...] = jnp.zeros_like(hgrad)
     dg_ref[...] = jnp.zeros_like(dg_ref)
     dbc_ref[...] = jnp.zeros_like(dbc_ref)
     dstep[...] = jnp.zeros_like(dstep)
-    here.greet()
-    here.greeted()
-
-    one_block = parts.at[0, 0]
-
-    def part(u, f_):
-        return parts.at[u % 6, f_]
-
-    def add_into(dst, src):
-        rows, width = dst.shape
-
-        def body(i, _):
-            at = pl.ds(pl.multiple_of(i * ROWS, ROWS), ROWS)
-            dst[at, :] = (dst[at, :].astype(F32) + src[at, :].astype(F32)).astype(dst.dtype)
-            return 0
-
-        lax.fori_loop(0, rows // ROWS, body, 0)
-
-    def s1(u):
-        if u >= 8:
-            pl.semaphore_wait(credit1, 1)
-        for n, f_ in enumerate((f3, f4)):
-            links.send(("s1", u, n), part(u, f_), recv1.at[u % 8, n], recv_sems.at[u, n], here.at(f=f3), one_block)
-
-    def s2(u):
-        links.arrived(recv1.at[u % 8, 1], recv_sems.at[u, 1], here.at(f=f3))
-        add_into(part(u, f2), recv1.at[u % 8, 1])
-        if u >= 8:
-            pl.semaphore_wait(credit2, 1)
-        links.send(("s2", u), part(u, f2), recv2.at[u % 8], recv_sems.at[u, 2], here.at(f=f2), one_block)
-        links.arrived(recv1.at[u % 8, 0], recv_sems.at[u, 0], here.at(f=f3))
-        add_into(part(u, f), recv1.at[u % 8, 0])
-        if u < 4:
-            pl.semaphore_signal(credit1, inc=1, device_id=here.at(f=f3), device_id_type=MESH)
-
-    def give_credit(u):
-        if u < 4:
-            pl.semaphore_signal(credit2, inc=1, device_id=here.at(f=f2), device_id_type=MESH)
-
-    outs = {0: ginner_ref, 1: ggate_ref, 2: gout_ref}
-
-    def s3(u):
-        k, m = units[u]
-        links.arrived(recv2.at[u % 8], recv_sems.at[u, 2], here.at(f=f2))
-        add_into(part(u, f), recv2.at[u % 8])
-        give_credit(u)
-        links.send(("s3", u), part(u, f), recv3.at[m, k - 1], recv_sems.at[12 + m, k - 1], here.at(z=zk[k]), one_block)
-
-    def last_sum(u):
-        k, m = units[u]
-        links.arrived(recv2.at[u % 8], recv_sems.at[u, 2], here.at(f=f2))
-        for j in (1, 2, 3):
-            links.arrived(recv3.at[m, j - 1], recv_sems.at[12 + m, j - 1], here.at(z=zk[j]))
-        own = part(u, f)
-
-        def body(i, _):
-            at = pl.ds(pl.multiple_of(i * ROWS, ROWS), ROWS)
-            total = own[at, :].astype(F32) + recv2[u % 8, at, :].astype(F32)
-            for j in range(3):
-                total = total + recv3[m, j, at, :].astype(F32)
-            outs[m][at, :] = total
-            return 0
-
-        lax.fori_loop(0, GW // ROWS, body, 0)
-        give_credit(u)
-
-    loads["nint"].wait()
-    loads["cot"].wait()
+    def to_normed(fresh, j, _):
+        at = pl.ds(pl.multiple_of(j * 256, 256), 256)
+        total = mm(dcat[at, :], win[3], ((1,), (1,)))
+        accl[at, :] = total[:, :wide] if fresh else accl[at, :] + total[:, :wide]
+        accr[at, :] = total[:, wide:] if fresh else accr[at, :] + total[:, wide:]
+        return 0
+
     for i, k in enumerate(ORDER):
-
-        def grad_out(j, _, i=i, k=k):
-            at = pl.ds(pl.multiple_of(j * ROWS, ROWS), ROWS)
-            src = pl.ds(pl.multiple_of(k * GW + j * ROWS, ROWS), ROWS)
-            total = mm(normt[src, :], cot[...])
-            for f_ in range(4):
-                parts[i, f_, at, :] = total[:, f_ * depth : (f_ + 1) * depth].astype(BF)
-            return 0
-
-        lax.fori_loop(0, GW // ROWS, grad_out, 0)
-        s1(i)
-        loads["nin", i].wait()
-        loads["wout", i].wait()
-
-        def mix_rows(j, _, i=i):
-            at = pl.ds(pl.multiple_of(j * 256, 256), 256)
-            total = mm(nin(i)[at, :], wouts[i % 2][...])
-            acc[at, :] = total if i == 0 else acc[at, :] + total
-            return 0
-
-        lax.fori_loop(0, SEQ // 256, mix_rows, 0)
-        if i + 2 < 4:
-            load_out(i + 2)
-
-    load("normt", normt_in, normt, 7)
-
-    def exchange(n):
-        if n:
-            links.left(("half", 0), core_sems.at[0], here.at(c=1 - here.c))
-
-        def body(j, _):
-            at = pl.ds(pl.multiple_of(j * ROWS, ROWS), ROWS)
-            src = pl.ds(pl.multiple_of((1 - here.c) * rows_own + j * ROWS, ROWS), ROWS)
-            half[at, :] = acc[src, :].astype(BF)
-            return 0
-
-        lax.fori_loop(0, rows_own // ROWS, body, 0)
-        links.send(("half", n), half, halfr.at[n], core_sems.at[n], here.at(c=1 - here.c))
-
-    def received(n):
-        links.arrived(halfr.at[n], core_sems.at[n], here.at(c=1 - here.c))
-
-    exchange(0)
-    received(0)
-
-    def layer(j, _):
-        at = pl.ds(pl.multiple_of(j * ROWS, ROWS), ROWS)
-        src = pl.ds(pl.multiple_of(here.c * rows_own + j * ROWS, ROWS), ROWS)
-        halfr[0, at, :] = (hid_ref[at, :].astype(F32) + acc[src, :] + halfr[0, at, :].astype(F32)).astype(BF)
-        return 0
-
-    lax.fori_loop(0, rows_own // ROWS, layer, 0)
-    load("layer", halfr.at[0], layer_out, 12)
-    loads["normt"].wait()
-
-    due = {
-        0: {0: [(s2, 0)], 1: [(s2, 1)], 2: [(s3, 0)], 4: [(s2, 2)], 5: [(s3, 1)], 7: [(s2, 3)]},
-        1: {0: [(s3, 2)], 5: [(s2, 4)], 7: [(s2, 5)]},
-        2: {0: [(s3, 4)], 1: [(s3, 5)], 3: [(s2, 6)], 4: [(last_sum, 3)], 5: [(s3, 6)], 6: [(s2, 7)]},
-        3: {0: [(s3, 7)], 3: [(s2, 8)], 5: [(s3, 8)], 6: [(s2, 9)], 7: [(s3, 9)]},
-    }
-    for i, k in enumerate(ORDER):
-        for name in ("pre", "dinner", "states", "pack"):
-            loads[name, i].wait()
-
-        def tick(step, i=i):
-            for at, events in due[i].items():
-                @pl.when(step == at)
-                def _(events=events):
-                    for event, u in events:
-                        event(u)
-
-        bwd_chunks(k, zk[k], tick, pre, dinner, par_ref.at[k], tok_ref, inv_ref, bc_ref, bct_ref, g_ref, pack,
-                   cumt_ref.at[k], states, hpar_ref, dcat, dstep, pgrad.at[k], hgrad, rt_ref, dg_ref, dbc_ref)
+        if i:
+            for name in ("pre", "states"):
+                loads[name, i].wait()
+
+        bwd_chunks(k, zk[k], ticker("g%d" % i), pre.at[1], gated.at[k], par_ref.at[k], tok_ref, bc_ref, bct_ref, g_ref,
+                   pack_ref.at[k // 2], cumt_ref.at[k], states, hpar_ref, dcat, dstep, pgrad.at[k], hgrad, rt_ref, dg_ref, dbc_ref)
         if i < 3:
-            load_group(i + 1)
+            load(("pre", i + 1), pre_hbm.at[ORDER[i + 1]], pre.at[1, pl.ds(8, SEQ)], 2)
+            load(("states", i + 1), states_hbm.at[ORDER[i + 1]], states, 3)
+        else:
+            loads[0, 0].wait()
+            loads[0, 1].wait()
         u = 4 + 2 * i
+        due("h%d0" % i)
         if u >= 6:
             for n in (u - 6, u - 5):
                 for name in (("s1", n, 0), ("s1", n, 1), ("s2", n), ("s3", n)):
                     if name in links.number:
                         links.left(name, core_sems.at[0], here.at(c=1 - here.c))
 
+        if i == 0:
+            loads["normt"].wait()
+            pl.semaphore_wait(free_out, 1)
+
         def grads(j, _, u=u):
             at = pl.ds(pl.multiple_of(j * ROWS, ROWS), ROWS)
-            for f_ in range(4):
-                src = pl.ds(pl.multiple_of(f_ * depth + j * ROWS, ROWS), ROWS)
-                total = mm(normt[src, :], dcat[...])
-                parts[u % 6, f_, at, :] = total[:, :GW].astype(BF)
-                parts[(u + 1) % 6, f_, at, :] = total[:, GW:].astype(BF)
+            win[slot_of(u)[0], at, :] = mm(flip[at, :], dcat[...]).astype(BF)
             return 0
 
-        lax.fori_loop(0, depth // ROWS, grads, 0)
+        lax.fori_loop(0, model // ROWS, grads, 0)
         s1(u)
         s1(u + 1)
-        loads["win", i].wait()
-
-        def to_normed(j, _, i=i):
-            at = pl.ds(pl.multiple_of(j * 256, 256), 256)
-            total = mm(dcat[at, :], win[...], ((1,), (1,)))
-            acc[at, :] = total if i == 0 else acc[at, :] + total
-            return 0
-
-        lax.fori_loop(0, SEQ // 256, to_normed, 0)
+        if i == 0:
+            received(0)
+
+            def layer(j, _):
+                own, at, below, total = summed(0, j)
+                store(0, at, below, total)
+                return 0
+
+            lax.fori_loop(0, rows_own // ROWS, layer, 0)
+            give(0, layer_out, 4)
+        due("h%d1" % i)
         if i < 3:
-            load_win(i + 1)
-
-    state_chunks(statepre_ref, cst_ref, tok_ref, row_ref, bc_ref, dg_ref, dbc_ref, dstate, sgrad, spad_ref)
-    half_state = pl.ds(pl.multiple_of(here.c * 128, 128), 128)
-    rest_state = pl.ds(pl.multiple_of(128 - here.c * 128, 128), 128)
-    core = here.at(c=1 - here.c)
+            loads["win", i].wait()
+            lax.fori_loop(0, SEQ // 256, functools.partial(to_normed, i == 0), 0)
+            load(("win", i + 1), win_hbm.at[ORDER[i + 1]], win.at[3], 1)
+            due("h%d2" % i)
+
+    last_tokens = []
+    for k in range(4):
+        src = hid_ref.at[:, pl.ds(k * GW, GW)]
+        last_tokens.append(pltpu.make_async_copy(src, gated.at[k, pl.ds(0, rows_own)], hid_sem.at[k]))
+        last_tokens[-1].start()
+    state_chunks(statepre_ref, cst_ref, tok_ref, docs_ref, bc_ref, dg_ref, dbc_ref, dstate, sgrad)
+    due("t0")
+
+    def state_part(f_, n=0):
+        at = pl.ds(pl.multiple_of((f_ % 2) * depth, depth), depth)
+        return halfr.at[at, pl.ds(pl.multiple_of((f_ // 2) * 256 + n * 128, 128), 128)]
+
+    def small_part(f_):
+        at = pl.ds(pl.multiple_of(2 * depth + (f_ // 2) * 4 * SMALL, 4 * SMALL), 4 * SMALL)
+        return halfr.at[at, pl.ds(pl.multiple_of((f_ % 2) * GW, GW), GW)]
+
+    def add_to(ref, *others):
+        total = ref[...].astype(F32)
+        for other in others:
+            total = total + other.astype(F32)
+        ref[...] = total.astype(BF)
+        return total
+
     for f_ in range(4):
-        sums = mm(normt[pl.ds(f_ * depth, depth), :], dstate[...])
+        sums = mm(flip[pl.ds(f_ * depth, depth), :], dstate[...])
         lower, upper = sums[:, :128], sums[:, 128:]
-        sparts[f_] = jnp.where(here.c == 0, lower, upper).astype(BF)
-        ssend[f_] = jnp.where(here.c == 0, upper, lower).astype(BF)
-    links.send("state_core", ssend, srecv, core_sems.at[2], core)
-
-    def finish_normed(j, _):
-        at = pl.ds(pl.multiple_of(j * 256, 256), 256)
-        total = mm(dstep[at, :64], stw_ref[...])
-        total = total + jnp.concatenate([mm(dstate[at, :], stbuf_ref[f_], ((1,), (1,))) for f_ in range(4)], 1)
-        acc[at, :] = acc[at, :] + total
-        return 0
-
-    lax.fori_loop(0, SEQ // 256, finish_normed, 0)
-    exchange(1)
-    links.arrived(srecv, core_sems.at[2], core)
-    for f_ in range(4):
-        sparts[f_] = (sparts[f_].astype(F32) + srecv[f_].astype(F32)).astype(BF)
-    links.send("state3", sparts.at[f3], srecv1.at[0], recv_sems.at[15, 0], here.at(f=f3))
-    links.send("state4", sparts.at[f4], srecv1.at[1], recv_sems.at[15, 1], here.at(f=f3))
-    step_rows = mm(dstep[:, :64], normt[...], ((0,), (1,)))
-    received(1)
-    gain = gains_ref[0:1, :]
-
-    def last(j, gain_grad):
-        at = pl.ds(pl.multiple_of(j * ROWS, ROWS), ROWS)
-        src = pl.ds(pl.multiple_of(here.c * rows_own + j * ROWS, ROWS), ROWS)
-        d = acc[src, :] + halfr[1, at, :].astype(F32)
-        x = hid_ref[at, :].astype(F32)
-        inv = lax.rsqrt(jnp.sum(x * x, 1, keepdims=True) / model + EPSILON)
-        weighted = d * gain
-        mean = jnp.sum(x * weighted, 1, keepdims=True) / model
-        d_hidden = inv * weighted - x * (inv * inv * inv * mean)
-        halfr[1, at, :] = (cot[src, :].astype(F32) + d_hidden).astype(BF)
-        return gain_grad + jnp.sum(d * x * inv, 0, keepdims=True)
-
-    gain_grad = lax.fori_loop(0, rows_own // ROWS, last, jnp.zeros((1, model), F32))
-    load("hidden", halfr.at[1], hidden_out, 13)
+        state_part(f_)[...] = jnp.where(here.c == 0, lower, upper).astype(BF)
+        state_part(f_, 1)[...] = jnp.where(here.c == 0, upper, lower).astype(BF)
+        links.send(("state_core", f_), state_part(f_, 1), srecv.at[f_], state_sems.at[f_], core)
+    due("t1")
+    step_rows = mm(dstep[:, :64], flip[...], ((0,), (1,)))
     zeros = jnp.zeros((1, GW - 256), F32)
     skips = jnp.zeros((8, 128), F32)
     heads_of = (iota((GW, 128), 0) >> 6 == iota((GW, 128), 1)).astype(BF)
@@ -1384,131 +1367,174 @@
         skips = skips + pltpu.roll(mm(hi, heads_of) + mm(lo, heads_of), 16 * zk[k], 1)
     head_rows = jnp.concatenate([hgrad[0:2, :], skips[P_SKIP : P_SKIP + 1, :]], 0)
     head_rows = jnp.concatenate([head_rows, jnp.zeros((3, GW - 128), F32)], 1)
+    common = [jnp.zeros((1, GW), F32)]
+    common += [jnp.concatenate([sgrad[r : r + 1, :], zeros], 1) for r in range(5)]
+    common.append(head_rows)
     for f_ in range(4):
-        common = [gain_grad[:, f_ * depth : (f_ + 1) * depth]]
-        common += [jnp.concatenate([sgrad[r : r + 1, :], zeros], 1) for r in range(5)]
-        common.append(head_rows)
+        blocks = []
         for k in range(4):
             own = jnp.concatenate([pgrad[k, 0:5, :], gaingrad_ref[k, 0:1, :], jnp.zeros((1, GW), F32)], 0)
-            qparts[f_, k] = jnp.concatenate(
-                [step_rows[16 * k : 16 * k + 16, f_ * depth : (f_ + 1) * depth], own] + common, 0
-            ).astype(BF)
+            blocks += [step_rows[16 * k : 16 * k + 16, f_ * depth : (f_ + 1) * depth], own] + common
+        small_part(f_)[...] = jnp.concatenate(blocks, 0).astype(BF)
     for n, f_ in enumerate((f2, f3, f4)):
-        links.send(("small", n), qparts.at[f_], qrecv1.at[n], recv_sems.at[16, n], here.at(f=f_))
-    links.arrived(srecv1.at[1], recv_sems.at[15, 1], here.at(f=f3))
-    sparts[f2] = (sparts[f2].astype(F32) + srecv1[1].astype(F32)).astype(BF)
-    links.send("state2", sparts.at[f2], srecv2, recv_sems.at[15, 2], here.at(f=f2))
-    links.arrived(srecv1.at[0], recv_sems.at[15, 0], here.at(f=f3))
-    s2(10)
+        links.send(("sums", n), small_part(f_), qrecv1.at[n], recv_sems.at[16, n], here.at(f=f_))
+    loads["win", 3].wait()
+    lax.fori_loop(0, SEQ // 256, functools.partial(to_normed, False), 0)
+
+    def finish_normed(j, _):
+        at = pl.ds(pl.multiple_of(j * 256, 256), 256)
+        total = mm(dstep[at, :64], stw_ref[...])
+        total = total + jnp.concatenate([mm(dstate[at, :], stbuf[f_], ((1,), (1,))) for f_ in range(4)], 1)
+        accl[at, :] = accl[at, :] + total[:, :wide]
+        accr[at, :] = accr[at, :] + total[:, wide:]
+        return 0
+
+    lax.fori_loop(0, SEQ // 256, finish_normed, 0)
+    due("t2")
+    exchange(1)
+    for f_ in range(4):
+        links.arrived(srecv.at[f_], state_sems.at[f_], core)
+        add_to(state_part(f_), srecv[f_])
+    for n, f_ in enumerate((f2, f3, f4)):
+        links.send(("state", f"f{n}"), state_part(f_), srecv1.at[n], recv_sems.at[15, n], here.at(f=f_))
+    due("t3")
+    received(1)
+    gain = gains_ref[0:1, :]
+    for copy in last_tokens:
+        copy.wait()
+
+    def last(j, gain_grad):
+        own, at, below, d = summed(1, j)
+        x = jnp.concatenate([gated[k, at, :] for k in range(4)], 1).astype(F32)
+        inv = lax.rsqrt(jnp.sum(x * x, 1, keepdims=True) / model + EPSILON)
+        weighted = d * gain
+        mean = jnp.sum(x * weighted, 1, keepdims=True) / model
+        d_hidden = inv * weighted - x * (inv * inv * inv * mean)
+        store(1, at, below, call[own, :].astype(F32) + d_hidden)
+        return gain_grad + jnp.sum(d * x * inv, 0, keepdims=True)
+
+    gain_grad = lax.fori_loop(0, rows_own // ROWS, last, jnp.zeros((1, model), F32))
+    give(1, hidden_out, 6)
+    for f_ in range(4):
+        nparts[f_] = jnp.broadcast_to(gain_grad[:, f_ * depth : (f_ + 1) * depth], (16, GW)).astype(BF)
+    for n, f_ in enumerate((f2, f3, f4)):
+        links.send(("gain", n), nparts.at[f_], nrecv.at[n], gain_sems.at[n], here.at(f=f_))
+    due("t4")
     for n, f_ in enumerate((f2, f3, f4)):
         links.arrived(qrecv1.at[n], recv_sems.at[16, n], here.at(f=f_))
+    sums = add_to(small_part(f), qrecv1[0], qrecv1[1], qrecv1[2])
     for k in range(4):
-        total = qparts[f, k].astype(F32)
-        for n in range(3):
-            total = total + qrecv1[n, k].astype(F32)
-        qsend[k] = total.astype(BF)
+        qsend[k] = sums[k * SMALL : (k + 1) * SMALL].astype(BF)
         if k:
             links.send(("small_z", k), qsend.at[k], qrecv3.at[k - 1], recv_sems.at[18, k - 1], here.at(z=zk[k]))
-    s2(11)
-    links.arrived(srecv2, recv_sems.at[15, 2], here.at(f=f2))
-    sparts[f] = (sparts[f].astype(F32) + srecv1[0].astype(F32) + srecv2[...].astype(F32)).astype(BF)
+    for n, f_ in enumerate((f2, f3, f4)):
+        links.arrived(srecv1.at[n], recv_sems.at[15, n], here.at(f=f_))
+    add_to(state_part(f), srecv1[0], srecv1[1], srecv1[2])
     for k in (1, 2, 3):
-        links.send(("state", k), sparts.at[f], srecv3.at[k - 1], recv_sems.at[17, k - 1], here.at(z=zk[k]))
+        links.send(("state_z", k), state_part(f), srecv3.at[k - 1], recv_sems.at[17, k - 1], here.at(z=zk[k]))
+    for n, f_ in enumerate((f2, f3, f4)):
+        links.arrived(nrecv.at[n], gain_sems.at[n], here.at(f=f_))
+    add_to(nparts.at[f], nrecv[0], nrecv[1], nrecv[2])
+    for k in (1, 2, 3):
+        links.send(("gain_z", k), nparts.at[f], nrecv.at[k + 2], gain_sems.at[k + 2], here.at(z=zk[k]))
+    due("t5")
     for k in (1, 2, 3):
         links.arrived(qrecv3.at[k - 1], recv_sems.at[18, k - 1], here.at(z=zk[k]))
-    total = qsend[0].astype(F32)
+    small_total = qsend[0].astype(F32)
     for k in range(3):
-        total = total + qrecv3[k].astype(F32)
-    gsmall_ref[...] = total
-    qsend[0] = total.astype(BF)
+        small_total = small_total + qrecv3[k].astype(F32)
+    qsend[0] = small_total.astype(BF)
     links.send("small_core", qsend.at[0], qrecvc, core_sems.at[3], core)
-    last_sum(10)
-    last_sum(11)
+    due("t6")
+    for k in (1, 2, 3):
+        links.arrived(nrecv.at[k + 2], gain_sems.at[k + 2], here.at(z=zk[k]))
+    gain_total = nparts[f].astype(F32)
+    for k in (3, 4, 5):
+        gain_total = gain_total + nrecv[k].astype(F32)
+    nback[...] = gain_total.astype(BF)
+    links.send("gain_core", nback, nrecv.at[6], gain_sems.at[6], core)
     for k in (1, 2, 3):
         links.arrived(srecv3.at[k - 1], recv_sems.at[17, k - 1], here.at(z=zk[k]))
-    total = sparts[f].astype(F32)
+    total = state_part(f)[...].astype(F32)
     for k in range(3):
         total = total + srecv3[k].astype(F32)
-    links.left("state_core", core_sems.at[0], core)
-    ssend[0] = total.astype(BF)
-    links.send("state_back", ssend.at[0], srecvc, core_sems.at[4], core)
+    back = halfr.at[pl.ds(0, depth), pl.ds(512, 128)]
+    back[...] = total.astype(BF)
+    links.send("state_back", back, srecvc, core_sems.at[4], core)
+    due("t7")
+    gain_row = iota((SMALL, GW), 0) == 23
     links.arrived(qrecvc, core_sems.at[3], core)
-    gother_ref[...] = qrecvc[...].astype(F32)
+    links.arrived(nrecv.at[6], gain_sems.at[6], core)
+    gsmall_ref[...] = jnp.where(gain_row, gain_total[0:1, :], small_total)
+    gother_ref[...] = jnp.where(gain_row, nrecv[6][0:1, :].astype(F32), qrecvc[...].astype(F32))
     links.arrived(srecvc, core_sems.at[4], core)
     rest = srecvc[...].astype(F32)
     gstate_ref[...] = jnp.concatenate([jnp.where(here.c == 0, total, rest), jnp.where(here.c == 0, rest, total)], 1)
-    loads["layer"].wait()
-    loads["hidden"].wait()
+    for side in range(2):
+        loads[1, side].wait()
+    results[staged[-1]].wait()
     links.finish(core_sems.at[0], core)
 
 
-def backward_call(model, hidden, saved):
-    (normt, cot, win, wout, pre, dinner, nin, nint, states, bc, bct, gs, pack, cumt, par, hpar, cst, stw, stbuf, gains,
-     statepre, invp, gaingrad, tok, row) = saved
+def block_call(model, hidden, *args):
     rows = hidden.shape[0]
     depth = model // 4
     any_ = pl.BlockSpec(memory_space=pl.ANY)
     sds = jax.ShapeDtypeStruct
     block = (GW, GW)
-    state = (depth, 256)
     part = (depth, 128)
     small = (SMALL, GW)
+
+    def v(kind, *shape):
+        return pltpu.VMEM(shape, kind)
+
     return pl.pallas_call(
-        functools.partial(backward_kernel, model),
+        functools.partial(block_kernel, model),
         out_shape=(
-            sds((rows, model), BF), sds((rows, model), BF), sds(block, F32), sds(block, F32), sds(block, F32),
-            sds(state, F32), sds(small, F32), sds(small, F32),
+            sds((rows, model), BF), sds((rows, model), BF),
+            sds((model, SEQ), BF), sds((4, model, 2 * GW), BF), sds((4, SEQ, 2 * GW), F32), sds((4, CH, 128, GW), BF),
+            sds(block, F32), sds(block, F32), sds(block, F32), sds((depth, 256), F32), sds(small, F32), sds(small, F32),
         ),
-        in_specs=[vm()] * 16 + [any_] * 10,
-        out_specs=tuple([any_] * 2 + [vm()] * 6),
+        in_specs=[any_] * 5 + [vm()] * (len(args) - 4),
+        out_specs=tuple([any_] * 9 + [vm()] * 3),
         scratch_shapes=[
-            pltpu.VMEM((model, SEQ), BF),
-            pltpu.VMEM((SEQ, model), BF),
-            pltpu.VMEM((model, 2 * GW), BF),
-            pltpu.VMEM((SEQ + 8, 2 * GW), F32),
-            pltpu.VMEM((SEQ, GW), F32),
-            pltpu.VMEM((CH, 128, GW), BF),
-            pltpu.VMEM((SEQ, 128), F32),
-            pltpu.VMEM((SEQ, model), F32),
-            pltpu.VMEM((rows, model), BF),
-            pltpu.VMEM((2, rows, model), BF),
-            pltpu.VMEM((SEQ, 2 * GW), BF),
-            pltpu.VMEM((6, 4) + block, BF),
-            pltpu.VMEM((8, 2) + block, BF),
-            pltpu.VMEM((8,) + block, BF),
-            pltpu.VMEM((3, 3) + block, BF),
-            pltpu.VMEM((4,) + part, BF),
-            pltpu.VMEM((4,) + part, BF),
-            pltpu.VMEM((4,) + part, BF),
-            pltpu.VMEM((2,) + part, BF),
-            pltpu.VMEM(part, BF),
-            pltpu.VMEM((3,) + part, BF),
-            pltpu.VMEM(part, BF),
-            pltpu.VMEM((4, 4) + small, BF),
-            pltpu.VMEM((3, 4) + small, BF),
-            pltpu.VMEM((3,) + small, BF),
-            pltpu.VMEM((4,) + small, BF),
-            pltpu.VMEM(small, BF),
-            pltpu.VMEM((SEQ, 128), BF),
-            pltpu.VMEM((SEQ, 256), BF),
-            pltpu.VMEM((4, 8, GW), F32),
-            pltpu.VMEM((8, 128), F32),
-            pltpu.VMEM((8, 256), F32),
-            pltpu.VMEM((128, GW), F32),
-            pltpu.VMEM((CH, L, L), F32),
-            pltpu.VMEM((SEQ, 256), F32),
-            pltpu.VMEM((SEQ + 8, 256), F32),
-            pltpu.SemaphoreType.DMA((72,)),
+            v(BF, SEQ, model), v(BF, SEQ, model), v(BF, 4, model, 2 * GW), v(BF, 4, GW, model),
+            v(F32, 2, SEQ + 8, 2 * GW), v(F32, SEQ, 2 * GW), v(BF, model, SEQ), v(BF, 4, SEQ, GW), v(BF, CH, 128, GW),
+            v(BF, SEQ, 2 * GW), v(BF, 4, 2, GW, GW), v(BF, 4, GW, GW), v(BF, 3, 3, GW, GW), v(F32, GW, GW),
+            v(BF, *small), v(BF, 4, 4, *small), v(BF, 4, depth, 256), v(F32, SEQ + 8, 256),
+            v(F32, SEQ, 128), v(F32, SEQ, 128), v(F32, SEQ, 128), v(F32, CH, L),
+            v(BF, SEQ, 256), v(BF, CH, 256, L), v(F32, CH, L, L), v(F32, 2, SEQ, 128), v(F32, 4, CH, 8, L),
+            v(F32, 4, 8, GW), v(F32, 8, 128), v(F32, 8, 256), v(BF, 64, model), v(F32, 8, model), v(F32, 4, 8, GW),
+            v(F32, 128, GW),
+            v(BF, 4, *part), v(BF, 3, *part), v(BF, 3, *part), v(BF, *part),
+            v(BF, 3, 4 * SMALL, GW), v(BF, 3, *small), v(BF, 4, *small), v(BF, *small),
+            v(BF, 4, 16, GW), v(BF, 7, 16, GW), v(BF, 16, GW),
+            v(BF, SEQ, 128), v(BF, SEQ, 256), v(F32, 4, 8, GW), v(F32, 8, 128), v(F32, 8, 256), v(F32, 128, GW),
+            v(F32, CH, L, L), v(F32, SEQ, 256),
+            pltpu.SemaphoreType.DMA((144,)),
+            pltpu.SemaphoreType.DMA((3, 4, 4)),
+            pltpu.SemaphoreType.DMA((7,)),
+            pltpu.SemaphoreType.DMA((6,)),
+            pltpu.SemaphoreType.DMA((4,)),
             pltpu.SemaphoreType.DMA((19, 4)),
             pltpu.SemaphoreType.DMA((5,)),
-            pltpu.SemaphoreType.DMA((14,)),
+            pltpu.SemaphoreType.DMA((4,)),
+            pltpu.SemaphoreType.DMA((7,)),
+            pltpu.SemaphoreType.DMA((16,)),
+            pltpu.SemaphoreType.DMA((4,)),
+            pltpu.SemaphoreType.DMA((4,)),
+            pltpu.SemaphoreType.DMA((4,)),
+            pltpu.SemaphoreType.DMA((8,)),
+            pltpu.SemaphoreType.DMA((3,)),
+            pltpu.SemaphoreType.DMA((5,)),
+            pltpu.SemaphoreType.REGULAR,
+            pltpu.SemaphoreType.REGULAR,
             pltpu.SemaphoreType.REGULAR,
             pltpu.SemaphoreType.REGULAR,
         ],
-        compiler_params=pltpu.CompilerParams(vmem_limit_bytes=VMEM_LIMIT, collective_id=2, has_side_effects=True),
-        name="backward_and_scatter",
-    )(hidden, tok, row, invp, bc, bct, gs, cumt, par, hpar, cst, stw, stbuf, statepre, gaingrad, gains,
-      normt, cot, win, wout, pre, dinner, nin, nint, states, pack)
+        compiler_params=pltpu.CompilerParams(vmem_limit_bytes=VMEM_LIMIT, collective_id=1, has_side_effects=True),
+        name="whole_block",
+    )(hidden, *args)
 
 
 def on_device(fsdp, halves, hidden_in, norm_gain, in_gate, in_inner, in_state, in_step, conv_inner, conv_inner_shift,
@@ -1696,9 +1722,9 @@
 
     vec = [jnp.pad(v, (0, GW - v.shape[0])) for v in (norm_gain, conv_state_shift, step_offset, log_rate, skip_gain)]
     vec = jnp.concatenate(vec + [jnp.zeros((3 * GW,), BF)]).reshape(8, GW).astype(F32)
-    saved = forward_call(model, hidden_in, grad_out, in_inner, in_gate, out_weight, in_state, vec, in_step, conv_inner,
-                         conv_inner_shift, inner_gain, conv_state, segment_ids.reshape(-1, L))
-    layer_out, grad_hidden, g_inner, g_gate, g_out, g_state, own, other = backward_call(model, hidden_in, saved)
+    result = block_call(model, hidden_in, grad_out, in_inner, in_gate, out_weight, in_state, vec, in_step, conv_inner,
+                        conv_inner_shift, inner_gain, conv_state, segment_ids.reshape(-1, L))
+    layer_out, grad_hidden, g_inner, g_gate, g_out, g_state, own, other = result[:2] + result[6:]
     shared = own[23:] + other[23:]
 
     def my_part(v):

time: 334 us -> 323 us (0.967)
  Pallas kernels: 309 us -> 297 us
    pallas_call x2 -> x1, Pallas kernels: 309 us -> 297 us  [block_call(): pl.pallas_call(functools.partial(block_kernel, model), out_shape=(sds((ro...]
where the time goes in v3:
time: 323 us; the launch traced here: 322 us
  Pallas kernels  297 us (92%)
  local copies, waits for them, and re-layouts  22.7 us (7%)
    pallas_call x1, Pallas kernels, block_call(): pl.pallas_call(functools.partial(block_kernel, model), out_shape=(sds((ro...  297 us
    unnamed x25, local copies, waits for them, and re-layouts  13 us

profile of v3, /device:TPU:0, one launch (start us, length us, event | category | flops | bytes accessed | tf_op | source)
XLA Modules:
  0.0 322.3 jit_solution(17255267210852217850)
XLA Ops:
  0.6 1.5 copy.38.step_ref
  2.1 0.9 dynamic-update-slice
  3.0 0.7 pad.14
  3.8 0.7 pad.15
  4.7 0.7 pad.16
  5.5 0.7 pad.17
  6.6 0.6 reshape.89.vec_ref
  7.2 1.3 copy.39.conv_ref
  8.5 296.9 %whole_block.1 = (bf16[512,1536]{1,0:T(8,128)(2,1)}, bf16[512,1536]{1,0:T(8,128)(2,1)}, bf16[1536,1024]{1,0:T(8,128)(2,1)}, bf16[4,1536,768]{2,1,0:T(8,128)(2,1)...) custom-call(bf16[512,1536]{1,0:T(8,128)(2,1)} %hid_ref.1, ...), custom_call_target="tpu_custom_call" | custom-call | tf_op jit(solution)/shard_map/whole_block/pallas_call | solution.py:1491
  305.4 0.9 fusion.4
  307.6 0.6 copy.49
  308.2 0.6 copy.50
  309.6 0.8 slice_add_fusion
  310.4 0.6 slice.97
  311.5 0.7 slice.94
  312.3 0.6 copy.48
  312.9 0.6 slice_reduce_fusion
  313.5 1.3 slice_bitcast_fusion
  314.8 2.8 copy.63
  317.6 1.1 copy.64
  319.1 0.8 copy.65
  319.9 0.8 copy.66
  320.7 0.7 copy.67
  321.4 0.8 copy.68
  (42 shorter events, 4.0 us)
Async XLA Ops:
  314.8 2.8 copy-start
  317.6 1.4 copy-start.3
  317.6 2.3 copy-start.2
  319.1 1.6 copy-start.4
  319.1 2.4 copy-start.1

commit v4 on v3

--- a/solution.py
+++ b/solution.py
@@ -458,43 +458,55 @@
     lax.fori_loop(0, CH, chunk, 0)
 
 
+def spread_masks(tok):
+    return [jnp.broadcast_to(tok[:, i : i + 1], (L, 128)) for i in range(3, 9)]
+
+
+def pair_conv(window, masks, par):
+    total = par[K : K + 1, :] + par[K - 1 : K, :] * back_conv_input(window, 0)
+    moved = [back_conv_input(window, 0)]
+    for k in range(1, K):
+        moved.append(back_conv_input(window, k) * masks[k - 1])
+        total = total + par[K - 1 - k : K - k, :] * moved[k]
+    return total, moved
+
+
 def fwd_chunks(group, tick, pre_ref, par_ref, tok_ref, bc_ref, bct_ref, g_ref, pack_ref, cumt_ref,
                gated_ref, states_ref, ss_ref, st_ref):
     st_ref[...] = jnp.zeros_like(st_ref)
-    par = par_ref[...]
 
     def chunk(c, _):
         tick(c)
         base = pl.multiple_of(c * L, L)
         rows = pl.ds(base, L)
-        tok = tok_ref[rows, :]
-        u = conv_of(pre_ref[pl.ds(base, L + 8), :GW], tok, par)
-        act = u * sigmoid(u)
+        masks = spread_masks(tok_ref[rows, :])
         pack = pack_ref[rows, :]
         if group % 2:
             pack = pltpu.roll(pack, 64, 1)
         cumt = cumt_ref[c]
         g = g_ref[c]
-        weighted = act * spread(pack, ST)
-        low = weighted.astype(BF)
-        enter = spread(pack, EE)
-        state = st_ref[...]
-        low_state = state.astype(BF)
-        states_ref[c] = low_state
-        y = mm(bc_ref[rows, 128:], low_state) * enter
-        locals_ = []
+        squares = jnp.zeros((L, 128), F32)
         for q in range(3):
+            lanes = pl.ds(128 * q, 128)
+            par = par_ref[:, lanes]
+            u, _ = pair_conv(pre_ref[pl.ds(base, L + 8), lanes], masks, par)
+            act = u * sigmoid(u)
+            weighted = act * pair_lanes(pack, ST, q)
             kernels = [(g * decay_kernel(pack, cumt, 2 * q + e)).astype(BF) for e in range(2)]
-            locals_.append(mm(jnp.concatenate(kernels, 1), block_diag(low[:, 128 * q : 128 * q + 128])))
-        y = y + jnp.concatenate(locals_, 1)
-        out = weighted * spread(pack, FF)
-        st_ref[...] = enter[L - 1 : L, :] * state + mm(bct_ref[c, pl.ds(0, 128), :], out.astype(BF))
-        ssd = y + par[P_SKIP : P_SKIP + 1, :] * act
-        gate = pre_ref[pl.ds(base + 8, L), GW:]
-        gated = ssd * (gate * sigmoid(gate))
-        gated_ref[rows, :] = gated.astype(BF)
-        sq = gated * gated
-        ss_ref[rows, :] += sq[:, :128] + sq[:, 128:256] + sq[:, 256:]
+            y = mm(jnp.concatenate(kernels, 1), block_diag(weighted.astype(BF)))
+            enter = pair_lanes(pack, EE, q)
+            state = st_ref[:, lanes]
+            low_state = state.astype(BF)
+            states_ref[c, :, lanes] = low_state
+            y = y + mm(bc_ref[rows, 128:], low_state) * enter
+            out = (weighted * pair_lanes(pack, FF, q)).astype(BF)
+            st_ref[:, lanes] = enter[L - 1 : L, :] * state + mm(bct_ref[c, pl.ds(0, 128), :], out)
+            ssd = y + par[P_SKIP : P_SKIP + 1, :] * act
+            gate = pre_ref[pl.ds(base + 8, L), pl.ds(GW + 128 * q, 128)]
+            gated = ssd * (gate * sigmoid(gate))
+            gated_ref[rows, lanes] = gated.astype(BF)
+            squares = squares + gated * gated
+        ss_ref[rows, :] += squares
         return 0
 
     lax.fori_loop(0, CH, chunk, 0)
@@ -504,17 +516,11 @@
                cumt_ref, states_ref, hpar_ref, dcat_ref, dstep_ref, pgrad_ref, hgrad_ref, rt_ref, dg_ref, dbc_ref):
     rt_ref[...] = jnp.zeros_like(rt_ref)
     pgrad_ref[...] = jnp.zeros_like(pgrad_ref)
-    par = par_ref[...]
     decay = pltpu.roll(hpar_ref[...], (128 - 16 * group) % 128, 1)[1:2, :]
     lane = lax.broadcasted_iota(jnp.int32, (L, L), 1)
     sub = lax.broadcasted_iota(jnp.int32, (L, L), 0)
     upper = (sub <= lane).astype(BF)
-    per_head = (lax.broadcasted_iota(jnp.int32, (GW, 128), 0) >> 6
-                == lax.broadcasted_iota(jnp.int32, (GW, 128), 1)).astype(BF)
-
-    def head_sums(x):
-        hi, lo = split2(x)
-        return mm(hi, per_head) + mm(lo, per_head)
+    heads = lane < GH
 
     def chunk(step, later):
         tick(step)
@@ -522,85 +528,94 @@
         base = pl.multiple_of(c * L, L)
         rows = pl.ds(base, L)
         tok = tok_ref[rows, :]
-        window = pre_ref[pl.ds(base, L + 8), :GW]
-        u = conv_of(window, tok, par)
-        su = sigmoid(u)
-        act = u * su
+        masks = spread_masks(tok)
+        inv = jnp.broadcast_to(tok[:, T_INV : T_INV + 1], (L, 128))
+        inv_back = jnp.broadcast_to(tok[:, T_BACK : T_BACK + 1], (L, 128))
         pack = pack_ref[rows, :]
         if group % 2:
             pack = pltpu.roll(pack, 64, 1)
         cumt = cumt_ref[c]
         g = g_ref[c]
-        steps = spread(pack, ST)
-        enter = spread(pack, EE)
-        leave = spread(pack, FF)
-        weighted = act * steps
-        low = weighted.astype(BF)
-        low_state = states_ref[c]
-        bmat = bc_ref[rows, :128]
-        cmat = bc_ref[rows, 128:]
-        diags = [block_diag(low[:, 128 * q : 128 * q + 128]) for q in range(3)]
-        decays = [decay_kernel(pack, cumt, h) for h in range(GH)]
-        kernels = [jnp.concatenate([(g * decays[2 * q + e]).astype(BF) for e in range(2)], 1) for q in range(3)]
-        y = mm(cmat, low_state) * enter + jnp.concatenate([mm(kernels[q], diags[q]) for q in range(3)], 1)
-        skip = par[P_SKIP : P_SKIP + 1, :]
-        ssd = y + skip * act
-        gate = pre_ref[pl.ds(base + 8, L), GW:]
-        sg = sigmoid(gate)
-        silu = gate * sg
-        scaled = dinner_ref[rows, :].astype(F32) * par[P_GAIN : P_GAIN + 1, :]
-        d_gated = tok[:, T_INV : T_INV + 1] * scaled - (ssd * silu) * tok[:, T_BACK : T_BACK + 1]
-        dy = d_gated * silu
-        dcat_ref[rows, GW:] = (d_gated * ssd * sg * (1.0 + gate * (1.0 - sg))).astype(BF)
-        dy_low = dy.astype(BF)
-        dy_in = (dy * enter).astype(BF)
-        rt = rt_ref[...]
-        rt_low = rt.astype(BF)
-        carried = mm(bmat, rt_low) * leave
-        pieces = []
         d_scores = jnp.zeros((L, L), F32)
+        sums = jnp.zeros((3 * L + 16, 128), F32)
+        d_c = dbc_ref[rows, 128:]
+        d_b = dbc_ref[rows, :128]
+        heads_of_pair = []
         for q in range(3):
-            dq = dy_low[:, 128 * q : 128 * q + 128]
-            dm = mm(dq, diags[q], ((1,), (1,)))
-            d_scores = d_scores + dm[:, :L] * decays[2 * q] + dm[:, L:] * decays[2 * q + 1]
-            both = mm(kernels[q], dq, ((0,), (0,)))
-            pieces.append(jnp.where(lane < 64, both[:L], both[L:]))
-        d_weighted = jnp.concatenate(pieces, 1) + carried
+            lanes = pl.ds(128 * q, 128)
+            gate_lanes = pl.ds(GW + 128 * q, 128)
+            par = par_ref[:, lanes]
+            u, moved = pair_conv(pre_ref[pl.ds(base, L + 8), lanes], masks, par)
+            su = sigmoid(u)
+            act = u * su
+            steps = pair_lanes(pack, ST, q)
+            weighted = act * steps
+            low = weighted.astype(BF)
+            diag = block_diag(low)
+            decays = [decay_kernel(pack, cumt, 2 * q + e) for e in range(2)]
+            kernels = jnp.concatenate([(g * d).astype(BF) for d in decays], 1)
+            enter = pair_lanes(pack, EE, q)
+            low_state = states_ref[c, :, lanes]
+            y = mm(bc_ref[rows, 128:], low_state) * enter + mm(kernels, diag)
+            skip = par[P_SKIP : P_SKIP + 1, :]
+            ssd = y + skip * act
+            gate = pre_ref[pl.ds(base + 8, L), gate_lanes]
+            sg = sigmoid(gate)
+            silu = gate * sg
+            scaled = dinner_ref[rows, lanes].astype(F32) * par[P_GAIN : P_GAIN + 1, :]
+            d_gated = inv * scaled - (ssd * silu) * inv_back
+            dy = d_gated * silu
+            dcat_ref[rows, gate_lanes] = (d_gated * ssd * (sg + silu * (1.0 - sg))).astype(BF)
+            dy_low = dy.astype(BF)
+            dy_in = (dy * enter).astype(BF)
+            d_c = d_c + mm(dy_in, low_state, ((1,), (1,)))
+            dm = mm(dy_low, diag, ((1,), (1,)))
+            d_scores = d_scores + dm[:, :L] * decays[0] + dm[:, L:] * decays[1]
+            both = mm(kernels, dy_low, ((0,), (0,)))
+            rt = rt_ref[:, lanes]
+            rt_low = rt.astype(BF)
+            leave = pair_lanes(pack, FF, q)
+            carried = mm(bc_ref[rows, :128], rt_low) * leave
+            d_weighted = jnp.where(lane < 64, both[:L], both[L:]) + carried
+            d_b = d_b + mm((weighted * leave).astype(BF), rt_low, ((1,), (1,)))
+            keep = enter[L - 1 : L, :]
+            rt_ref[:, lanes] = keep * rt + mm(bct_ref[c, pl.ds(128, 128), :], dy_in)
+            low32 = low.astype(F32)
+            at_end = jnp.sum(low32 * carried, 0, keepdims=True)
+            at_end = at_end + keep * jnp.sum(rt * low_state.astype(F32), 0, keepdims=True)
+            cum_high, cum_low = split2(dy_low.astype(F32) * y - low32 * d_weighted)
+            end_high, end_low = split2(jnp.concatenate([at_end, jnp.zeros((7, 128), F32)], 0))
+            ends = jnp.concatenate([end_high, end_low], 0)
+            per_head = ((sub >> 6) + 2 * q == lane).astype(BF)
+            sums = sums + mm(jnp.concatenate([cum_high, cum_low, (act * d_weighted).astype(BF), ends], 0), per_head)
+            d_act = skip * dy + steps * d_weighted
+            du = d_act * (su + act * (1.0 - su))
+            pgrad_ref[K : K + 1, lanes] += jnp.sum(du, 0, keepdims=True)
+            pgrad_ref[P_SKIP : P_SKIP + 1, lanes] += jnp.sum(dy * act, 0, keepdims=True)
+            ahead = jnp.concatenate([du, later[:, 128 * q : 128 * q + 128]], 0)
+            d_pre = par[K - 1 : K, :] * du
+            for k in range(K):
+                pgrad_ref[K - 1 - k : K - k, lanes] += jnp.sum(du * moved[k], 0, keepdims=True)
+                if k:
+                    d_pre = d_pre + par[K - 1 - k : K - k, :] * (ahead[k : k + L] * masks[2 + k])
+            dcat_ref[rows, lanes] = d_pre.astype(BF)
+            heads_of_pair.append(du[:8])
         dg_ref[c] += d_scores
-        out = (weighted * leave).astype(BF)
-        dbc_ref[rows, 128:] += mm(dy_in, low_state, ((1,), (1,)))
-        dbc_ref[rows, :128] += mm(out, rt_low, ((1,), (1,)))
-        keep = enter[L - 1 : L, :]
-        low32 = low.astype(F32)
-        d_cum = head_sums(dy_low.astype(F32) * y - low32 * d_weighted)
-        at_end = jnp.sum(low32 * carried, 0, keepdims=True) + keep * jnp.sum(rt * low_state.astype(F32), 0, keepdims=True)
-        d_last = head_sums(jnp.concatenate([at_end, jnp.zeros((7, GW), F32)], 0))[0:1, :]
-        hi, mid, lo = split3(d_cum)
-        d_log = mm(upper, hi) + mm(upper, mid) + mm(upper, lo) + d_last
-        rt_ref[...] = keep * rt + mm(bct_ref[c, pl.ds(128, 128), :], dy_in)
-        d_step = head_sums(act * d_weighted) + decay * d_log
-        heads = lane < GH
+        dbc_ref[rows, 128:] = d_c
+        dbc_ref[rows, :128] = d_b
+        d_last = sums[3 * L : 3 * L + 1] + sums[3 * L + 8 : 3 * L + 9]
+        hi, mid, lo = split3(sums[:L] + sums[L : 2 * L])
+        parts = hi.astype(F32) + pltpu.roll(mid.astype(F32), 8, 1) + pltpu.roll(lo.astype(F32), 16, 1)
+        d_log = mm(upper, parts.astype(BF))
+        d_log = d_log + pltpu.roll(d_log, 120, 1) + pltpu.roll(d_log, 112, 1) + d_last
+        d_step = sums[2 * L : 3 * L] + decay * d_log
         d_step_pre = jnp.where(heads, d_step * pltpu.roll(pack, 128 - SG, 1), 0.0)
         dstep_ref[rows, :] += pltpu.roll(d_step_pre, 16 * group, 1).astype(BF)
         rate = jnp.sum(jnp.where(heads, pack, 0.0) * d_log, 0, keepdims=True) * decay
         offs = jnp.sum(d_step_pre, 0, keepdims=True)
         hgrad_ref[0:1, :] += pltpu.roll(jnp.concatenate([rate, jnp.zeros((7, 128), F32)], 0), 16 * z_k, 1)[0:1]
         hgrad_ref[1:2, :] += pltpu.roll(jnp.concatenate([offs, jnp.zeros((7, 128), F32)], 0), 16 * z_k, 1)[0:1]
-        d_act = skip * dy + steps * d_weighted
-        du = d_act * su * (1.0 + u * (1.0 - su))
-        pgrad_ref[K : K + 1, :] += jnp.sum(du, 0, keepdims=True)
-        pgrad_ref[P_SKIP : P_SKIP + 1, :] += jnp.sum(dy * act, 0, keepdims=True)
-        for k in range(K):
-            moved = back_conv_input(window, k)
-            if k:
-                moved = moved * tok[:, 2 + k : 3 + k]
-            pgrad_ref[K - 1 - k : K - k, :] += jnp.sum(du * moved, 0, keepdims=True)
-        ahead = jnp.concatenate([du, later], 0)
-        d_pre = par[K - 1 : K, :] * du
-        for k in range(1, K):
-            d_pre = d_pre + par[K - 1 - k : K - k, :] * (ahead[k : k + L] * tok[:, 5 + k : 6 + k])
-        dcat_ref[rows, :GW] = d_pre.astype(BF)
-        return du[:8]
+        return jnp.concatenate(heads_of_pair, 1)
 
     lax.fori_loop(0, CH, chunk, jnp.zeros((8, GW), F32))
 
@@ -737,17 +752,19 @@
     return jnp.sum(jnp.where((iota(rows.shape, 1) >> 6) == iota(rows.shape, 0), rows, 0.0), 0, keepdims=True)
 
 
-def small_block(f, vec_ref, step_ref, conv_ref, shift_ref, gain_ref, cst_ref):
-    units = own_block(f, conv_ref.shape[2], conv_ref.shape[2])
-    states = at_block(f, cst_ref.shape[1], cst_ref.shape[1])
+def small_block(f, refs):
+    norm, step, conv, shift, gain, cst, cst_shift, offset, rate, skip = [r[...].astype(F32) for r in refs]
+    units = own_block(f, conv.shape[2], conv.shape[2])
+    states = at_block(f, cst.shape[1], cst.shape[1])
     heads = at_block(f, 16, 12)
-    steps = jnp.concatenate([step_ref[...].astype(F32), jnp.zeros((step_ref.shape[0], 128 - GH), F32)], 1).T
-    rows = [steps[:GH], vec_ref[0:1, :]]
-    rows += [spread_units(conv_ref[k], units) for k in range(K)]
-    rows += [spread_units(shift_ref[...], units), spread_units(gain_ref[...], units)]
-    rows.append(mm(vec_ref[2:5, :16].astype(BF), heads))
-    rows.append(mm(cst_ref[...], states))
-    rows.append(mm(vec_ref[1:2, :64].astype(BF), states))
+    rows = [step, norm.reshape(1, -1)]
+    rows += [spread_units(conv[:, k].astype(BF), units) for k in range(K)]
+    rows += [spread_units(shift.astype(BF), units), spread_units(gain.astype(BF), units)]
+    per_head = jnp.concatenate([v.reshape(1, -1) for v in (offset, rate, skip)], 0)
+    per_head = jnp.concatenate([per_head, jnp.zeros((3, 16 - per_head.shape[1]), F32)], 1)
+    rows.append(mm(per_head.astype(BF), heads))
+    rows.append(mm(cst.astype(BF), states))
+    rows.append(mm(cst_shift.reshape(1, -1).astype(BF), states))
     rows.append(jnp.zeros((SMALL - 21, GW), F32))
     return jnp.concatenate(rows, 0).astype(BF)
 
@@ -772,26 +789,26 @@
 ORDER = (3, 2, 1, 0)
 ROWS = 128
 SCHEDULE = {
-    "s1": [("second", 0, 0)],
-    "s2": [("second", 1, 0), ("first", 0, 1)],
-    "s5": [("second", 0, 1), ("first", 1, 1)],
-    "m05": [("second", 1, 1), ("first", 0, 2)],
-    "m10": [("second", 0, 2), ("first", 1, 2)],
-    "p2": [("second", 1, 2), ("first", 0, 3)],
-    "m20": [("second", 0, 3), ("first", 1, 3)],
-    "p3": [("second", 1, 3), ("first", 2, 0)],
-    "m30": [("second", 2, 0), ("first", 2, 1)],
-    "n1": [("second", 2, 1), ("first", 2, 2)],
-    "b10": [("second", 2, 2), ("first", 2, 3)],
-    "b30": [("second", 2, 3), ("s1", 0), ("s1", 1), ("s1", 2)],
+    "s1": [("second", 0, 0), ("first", 0, 1)],
+    "s2": [("second", 1, 0), ("first", 1, 1)],
+    "s5": [("second", 0, 1), ("first", 0, 2)],
+    "m00": [("second", 1, 1), ("first", 1, 2), ("second", 0, 2), ("first", 0, 3)],
+    "m10": [("second", 1, 2), ("first", 1, 3), ("second", 0, 3), ("first", 2, 0)],
+    "m20": [("second", 1, 3), ("first", 2, 1), ("second", 2, 0), ("first", 2, 2)],
+    "m30": [("second", 2, 1), ("first", 2, 3), ("second", 2, 2)],
+    "n1": [("second", 2, 3)],
+    "b01": [("s1", 0)],
+    "b11": [("s1", 1)],
+    "b21": [("s1", 2)],
     "b31": [("s1", 3)],
-    "x2": [("s2", 0)],
-    "g02": [("s3", 0), ("s2", 1)],
+    "x1": [("s2", 0)],
+    "g01": [("s3", 0)],
+    "g02": [("s2", 1)],
     "g06": [("s3", 1)],
     "g07": [("s2", 2)],
     "h01": [("s3", 2)],
     "h02": [("s2", 3)],
-    "g14": [("last", 3), ("s2", 4)],
+    "g14": [("s2", 4), ("last", 3)],
     "h10": [("s3", 4)],
     "h11": [("s2", 5)],
     "g23": [("s3", 5)],
@@ -802,16 +819,15 @@
     "g34": [("s2", 8)],
     "h30": [("s3", 8)],
     "h31": [("s2", 9)],
-    "t1": [("s3", 9)],
-    "t2": [("s2", 10)],
+    "t2": [("s3", 9), ("s2", 10)],
     "t4": [("s2", 11), ("last", 10)],
     "t5": [("last", 11)],
 }
 T_INV, T_BACK = 16, 17
 
 
-def block_kernel(model, hid_ref, cot_ref, w0_ref, w1_ref, w2_ref, wst_ref, vec_ref, step_ref, conv_ref, shift_ref, gain_ref,
-                 cvst_ref, seg_ref,
+def block_kernel(model, hid_ref, cot_ref, w0_ref, w1_ref, w2_ref, wst_ref, norm_ref, step_ref, conv_ref, shift_ref, gain_ref,
+                 cvst_ref, cvst_shift_ref, offset_ref, rate_ref, skip_ref, seg_ref,
                  layer_out, hidden_out, normt_hbm, win_hbm, pre_hbm, states_hbm,
                  ginner_out, ggate_out, gout_out, gstate_ref, gsmall_ref, gother_ref,
                  hall, call, win, wout, pre, accr, flip, gated, states, halfr, recv1, recv2, recv3, stage,
@@ -838,7 +854,9 @@
         outs.append(copy)
 
     here.greet()
-    small_ref[...] = small_block(here.f, vec_ref, step_ref, conv_ref, shift_ref, gain_ref, cvst_ref)
+    small_ref[...] = small_block(
+        here.f, (norm_ref, step_ref, conv_ref, shift_ref, gain_ref, cvst_ref, cvst_shift_ref, offset_ref, rate_ref, skip_ref)
+    )
     here.greeted()
     mine = pl.ds(pl.multiple_of(here.c * rows_own, rows_own), rows_own)
     other = pl.ds(pl.multiple_of((1 - here.c) * rows_own, rows_own), rows_own)
@@ -969,6 +987,7 @@
         links.arrived(state_of(f, rest_state), state_recvs.at[n], core)
 
     TILE = 256
+    WIDE_TILE = 512
 
     def project_small(i, _):
         rows = pl.ds(pl.multiple_of(i * TILE, TILE), TILE)
@@ -1014,12 +1033,12 @@
             pre_copies[k - 2].wait()
 
         def project(i, _, slot=slot, k=k):
-            rows = pl.ds(pl.multiple_of(i * TILE, TILE), TILE)
-            to = pl.ds(pl.multiple_of(i * TILE + 8, 8), TILE)
+            rows = pl.ds(pl.multiple_of(i * WIDE_TILE, WIDE_TILE), WIDE_TILE)
+            to = pl.ds(pl.multiple_of(i * WIDE_TILE + 8, 8), WIDE_TILE)
             pre[slot, to, :] = mm(hall[rows, :], win[zk[k]])
             return 0
 
-        lax.fori_loop(0, SEQ // TILE, project, 0)
+        lax.fori_loop(0, SEQ // WIDE_TILE, project, 0)
         copy = pltpu.make_async_copy(pre.at[slot, pl.ds(8, SEQ)], pre_hbm.at[k], pre_sem.at[k])
         copy.start()
         pre_copies.append(copy)
@@ -1152,15 +1171,13 @@
         k = ORDER[i]
         at, side = slot_of(i)
 
-        def rows_of(j, _):
-            src = pl.ds(pl.multiple_of(k * GW + j * ROWS, ROWS), ROWS)
-            total = mm(flip[src, :], call[...])
-            for f_ in range(4):
-                to = pl.ds(pl.multiple_of(f_ * depth + j * ROWS, ROWS), ROWS)
-                win[at, to, pl.ds(side * GW, GW)] = total[:, f_ * depth : (f_ + 1) * depth].astype(BF)
+        def columns_of(f_, _):
+            lanes = pl.ds(pl.multiple_of(f_ * depth, depth), depth)
+            total = mm(flip[pl.ds(k * GW, GW), :], call[:, lanes])
+            win[at, lanes, pl.ds(side * GW, GW)] = total.astype(BF)
             return 0
 
-        lax.fori_loop(0, GW // ROWS, rows_of, 0)
+        lax.fori_loop(0, 4, columns_of, 0)
 
     hid_copies = []
     for side in range(2):
@@ -1176,7 +1193,7 @@
         gaingrad_ref[k] = jnp.zeros((8, GW), F32)
 
         def back(i, _, k=k):
-            rows = pl.ds(pl.multiple_of(i * TILE, TILE), TILE)
+            rows = pl.ds(pl.multiple_of(i * WIDE_TILE, WIDE_TILE), WIDE_TILE)
             d = mm(call[rows, :], wout[zk[k]], ((1,), (1,)))
             both = d * gated[k, rows, :].astype(F32)
             gated[k, rows, :] = d.astype(BF)
@@ -1185,7 +1202,7 @@
             pr_ref[rows, :] += both[:, :128] + both[:, 128:256] + both[:, 256:]
             return 0
 
-        lax.fori_loop(0, SEQ // TILE, back, 0)
+        lax.fori_loop(0, SEQ // WIDE_TILE, back, 0)
     pl.semaphore_wait(free_core, 1)
     links.send("products", pr_ref, ssr_ref, core_recvs.at[3], core)
     due("x0")
@@ -1193,14 +1210,12 @@
     load(("win", 0), win_hbm.at[ORDER[0]], win.at[3], 1)
 
     def mix_rows(i, _):
-        rows = pl.ds(pl.multiple_of(i * TILE, TILE), TILE)
-        for k in range(4):
-            mixed = mm(hall[rows, pl.ds(k * GW, GW)], wout[zk[k]])
-            accl[rows, :] = mixed[:, :wide] if k == 0 else accl[rows, :] + mixed[:, :wide]
-            accr[rows, :] = mixed[:, wide:] if k == 0 else accr[rows, :] + mixed[:, wide:]
+        rows = pl.ds(pl.multiple_of(i * WIDE_TILE, WIDE_TILE), WIDE_TILE)
+        for acc, first_lane in ((accl, 0), (accr, wide)):
+            acc[rows, :] = sum(mm(hall[rows, pl.ds(k * GW, GW)], wout[zk[k], :, pl.ds(first_lane, wide)]) for k in range(4))
         return 0
 
-    lax.fori_loop(0, SEQ // TILE, mix_rows, 0)
+    lax.fori_loop(0, SEQ // WIDE_TILE, mix_rows, 0)
     due("x1")
     half = hall.at[:, pl.ds(0, wide)]
     halves = [halfr, hall.at[:, pl.ds(wide, wide)]]
@@ -1272,10 +1287,10 @@
     dbc_ref[...] = jnp.zeros_like(dbc_ref)
     dstep[...] = jnp.zeros_like(dstep)
     def to_normed(fresh, j, _):
-        at = pl.ds(pl.multiple_of(j * 256, 256), 256)
-        total = mm(dcat[at, :], win[3], ((1,), (1,)))
-        accl[at, :] = total[:, :wide] if fresh else accl[at, :] + total[:, :wide]
-        accr[at, :] = total[:, wide:] if fresh else accr[at, :] + total[:, wide:]
+        at = pl.ds(pl.multiple_of(j * WIDE_TILE, WIDE_TILE), WIDE_TILE)
+        for acc, first_row in ((accl, 0), (accr, wide)):
+            total = mm(dcat[at, :], win[3, pl.ds(first_row, wide), :], ((1,), (1,)))
+            acc[at, :] = total if fresh else acc[at, :] + total
         return 0
 
     for i, k in enumerate(ORDER):
@@ -1304,11 +1319,11 @@
             pl.semaphore_wait(free_out, 1)
 
         def grads(j, _, u=u):
-            at = pl.ds(pl.multiple_of(j * ROWS, ROWS), ROWS)
+            at = pl.ds(pl.multiple_of(j * depth, depth), depth)
             win[slot_of(u)[0], at, :] = mm(flip[at, :], dcat[...]).astype(BF)
             return 0
 
-        lax.fori_loop(0, model // ROWS, grads, 0)
+        lax.fori_loop(0, 4, grads, 0)
         s1(u)
         s1(u + 1)
         if i == 0:
@@ -1324,7 +1339,7 @@
         due("h%d1" % i)
         if i < 3:
             loads["win", i].wait()
-            lax.fori_loop(0, SEQ // 256, functools.partial(to_normed, i == 0), 0)
+            lax.fori_loop(0, SEQ // WIDE_TILE, functools.partial(to_normed, i == 0), 0)
             load(("win", i + 1), win_hbm.at[ORDER[i + 1]], win.at[3], 1)
             due("h%d2" % i)
 
@@ -1379,7 +1394,7 @@
     for n, f_ in enumerate((f2, f3, f4)):
         links.send(("sums", n), small_part(f_), qrecv1.at[n], recv_sems.at[16, n], here.at(f=f_))
     loads["win", 3].wait()
-    lax.fori_loop(0, SEQ // 256, functools.partial(to_normed, False), 0)
+    lax.fori_loop(0, SEQ // WIDE_TILE, functools.partial(to_normed, False), 0)
 
     def finish_normed(j, _):
         at = pl.ds(pl.multiple_of(j * 256, 256), 256)
@@ -1537,6 +1552,67 @@
     )(hidden, *args)
 
 
+def exact(values, places):
+    return sum(mm(part, places, ((1,), (1,))) for part in split3(values))
+
+
+def finish_kernel(layer_in, hidden_in, gate_in, inner_in, out_in, state_in, own_ref, other_ref,
+                  layer_out, hidden_out, gain_out, gate_out, inner_out, state_out, step_out, conv_out, shift_out, cst_out,
+                  cst_shift_out, offset_out, rate_out, skip_out, inner_gain_out, out_out, sems):
+    pairs = [(layer_in, layer_out), (hidden_in, hidden_out), (gate_in, gate_out), (inner_in, inner_out), (out_in, out_out),
+             (state_in, state_out)]
+    copies = [pltpu.make_async_copy(a, b, sems.at[n]) for n, (a, b) in enumerate(pairs)]
+    for copy in copies:
+        copy.start()
+    f, core = lax.axis_index("fsdp"), lax.axis_index("core")
+    own, other = own_ref[...], other_ref[...]
+    shared = own + other
+    gain_out[...] = shared[23:24].reshape(GW)
+    step_out[...] = own[:GH]
+    unit = conv_out.shape[2]
+    heads = iota((8, GW), 1) >> 6 == iota((8, GW), 0)
+    rows = [jnp.where(heads, own[r : r + 1], 0.0) for r in range(16, 22)]
+    picked = exact(jnp.concatenate(rows, 0), own_block(f, unit, unit))
+    for k in range(K):
+        conv_out[:, k : k + 1, :] = picked[8 * k : 8 * k + GH].reshape(GH, 1, unit)
+    shift_out[...] = picked[8 * K : 8 * K + GH]
+    inner_gain_out[...] = picked[8 * K + 8 : 8 * K + 8 + GH]
+    size = cst_out.shape[1]
+    states = exact(shared[24:32], at_block(f, size, size))
+    cst_out[...] = states[:K]
+    cst_shift_out[...] = states[K : K + 1].reshape(size)
+    place, lane = iota((16, GW), 0), iota((16, GW), 1)
+    lower = ((lane == 16 * f + place) & (place < GH)).astype(BF)
+    upper = ((lane == 16 * f + place - GH) & (place >= GH) & (place < 2 * GH)).astype(BF)
+    first = jnp.where(core == 0, own[24:32], other[24:32])
+    second = jnp.where(core == 0, other[24:32], own[24:32])
+    per_head = exact(first, lower) + exact(second, upper)
+    rate_out[...] = per_head[5:6, : 2 * GH].reshape(2 * GH)
+    offset_out[...] = per_head[6:7, : 2 * GH].reshape(2 * GH)
+    skip_out[...] = per_head[7:8, : 2 * GH].reshape(2 * GH)
+    for copy in copies:
+        copy.wait()
+
+
+def finish_call(*args):
+    any_ = pl.BlockSpec(memory_space=pl.ANY)
+    sds = jax.ShapeDtypeStruct
+    layer, hidden, gate, inner, out, state = [sds(v.shape, v.dtype) for v in args[:6]]
+    return pl.pallas_call(
+        finish_kernel,
+        out_shape=(
+            layer, hidden, sds((GW,), F32), gate, inner, state, sds((GH, GW), F32), sds((GH, K, 16), F32), sds((GH, 16), F32),
+            sds((K, 64), F32), sds((64,), F32), sds((2 * GH,), F32), sds((2 * GH,), F32), sds((2 * GH,), F32),
+            sds((GH, 16), F32), out,
+        ),
+        in_specs=[vm()] * 8,
+        out_specs=tuple([any_] * 2 + [vm()] + [any_] * 3 + [vm()] * 9 + [any_]),
+        scratch_shapes=[pltpu.SemaphoreType.DMA((6,))],
+        compiler_params=pltpu.CompilerParams(vmem_limit_bytes=VMEM_LIMIT),
+        name="finish",
+    )(*args)
+
+
 def on_device(fsdp, halves, hidden_in, norm_gain, in_gate, in_inner, in_state, in_step, conv_inner, conv_inner_shift,
               conv_state, conv_state_shift, step_offset, log_rate, skip_gain, inner_gain, out_weight, segment_ids,
               grad_out):
@@ -1715,34 +1791,17 @@
 
 def on_chip(hidden_in, norm_gain, in_gate, in_inner, in_state, in_step, conv_inner, conv_inner_shift, conv_state,
             conv_state_shift, step_offset, log_rate, skip_gain, inner_gain, out_weight, segment_ids, grad_out):
-    depth = in_gate.shape[0]
-    model = depth * 4
-    f = lax.axis_index("fsdp")
-    core = lax.axis_index("core")
-
-    vec = [jnp.pad(v, (0, GW - v.shape[0])) for v in (norm_gain, conv_state_shift, step_offset, log_rate, skip_gain)]
-    vec = jnp.concatenate(vec + [jnp.zeros((3 * GW,), BF)]).reshape(8, GW).astype(F32)
-    result = block_call(model, hidden_in, grad_out, in_inner, in_gate, out_weight, in_state, vec, in_step, conv_inner,
-                        conv_inner_shift, inner_gain, conv_state, segment_ids.reshape(-1, L))
+    model = in_gate.shape[0] * 4
+    result = block_call(
+        model, hidden_in, grad_out, in_inner, in_gate, out_weight, in_state, norm_gain, in_step.T,
+        conv_inner.transpose(1, 0, 2), conv_inner_shift, inner_gain, conv_state, conv_state_shift, step_offset, log_rate,
+        skip_gain, segment_ids.reshape(-1, L),
+    )
     layer_out, grad_hidden, g_inner, g_gate, g_out, g_state, own, other = result[:2] + result[6:]
-    shared = own[23:] + other[23:]
-
-    def my_part(v):
-        r, n = v.shape
-        return lax.dynamic_index_in_dim(v.reshape(r, n // (4 * 16), 4, 16), f, 2, False)
-
-    def heads(r):
-        mine = jnp.where(core == 0, own[r], other[r])[:64].reshape(4, 16)[:, :GH]
-        theirs = jnp.where(core == 0, other[r], own[r])[:64].reshape(4, 16)[:, :GH]
-        every = jnp.concatenate([mine, theirs], 1)
-        return lax.dynamic_index_in_dim(every, f, 0, False)
-
-    conv = my_part(own[16:20])
-    grad_state_conv = lax.dynamic_slice_in_dim(shared[1:6, :256], f * 64, 64, 1)
-    return (
-        layer_out, grad_hidden, shared[0], g_gate, g_inner, g_state, own[:GH].T, conv, my_part(own[20:21])[0],
-        grad_state_conv[:4], grad_state_conv[4], heads(30), heads(29), heads(31), my_part(own[21:22])[0], g_out,
-    )
+    outs = list(finish_call(layer_out, grad_hidden, g_gate, g_inner, g_out, g_state, own, other))
+    outs[6] = outs[6].T
+    outs[7] = outs[7].transpose(1, 0, 2)
+    return tuple(outs)
 
 
 def solution(mesh):

time: 323 us -> 295 us (0.913)
  local copies, waits for them, and re-layouts: 22.7 us -> 0 us
    unnamed x25 -> x0, local copies, waits for them, and re-layouts: 13 us -> none
    pallas_call x1, Pallas kernels: 297 us -> 289 us  [block_call(): pl.pallas_call(functools.partial(block_kernel, model), out_shape=(sds((ro...]
    pallas_call x0 -> x1, Pallas kernels: none -> 5.53 us  [finish_call(): pl.pallas_call(finish_kernel, out_shape=(layer, hidden, sds((GW,), F32),...]
where the time goes in v4:
time: 295 us
  Pallas kernels  294 us (100%)
    pallas_call x1, Pallas kernels, block_call(): pl.pallas_call(functools.partial(block_kernel, model), out_shape=(sds((ro...  289 us

profile of v4, /device:TPU:0, one launch (start us, length us, event | category | flops | bytes accessed | tf_op | source)
XLA Modules:
  0.0 294.9 jit_solution(4139191872860978327)
XLA Ops:
  0.7 288.6 %whole_block.1 = (bf16[512,1536]{1,0:T(8,128)(2,1)}, bf16[512,1536]{1,0:T(8,128)(2,1)}, bf16[1536,1024]{1,0:T(8,128)(2,1)}, bf16[4,1536,768]{2,1,0:T(8,128)(2,1)...) custom-call(bf16[512,1536]{1,0:T(8,128)(2,1)} %hid_ref.1, ...), custom_call_target="tpu_custom_call" | custom-call | tf_op jit(solution)/shard_map/whole_block/pallas_call | solution.py:1506
  289.2 5.5 %finish.1 = (bf16[512,1536]{1,0:T(8,128)(2,1)}, bf16[512,1536]{1,0:T(8,128)(2,1)}, f32[384]{0:T(512)}, f32[384,384]{1,0:T(8,128)}, f32[384,384]{1,0:T(8,128)}, /...) custom-call(bf16[512,1536]{1,0:T(8,128)(2,1)} %get-tuple-element.40., ...), custom_call_target="tpu_custom_call" | custom-call | tf_op jit(solution)/shard_map/finish/pallas_call | solution.py:1601

commit v5 on v4

--- a/solution.py
+++ b/solution.py
@@ -521,6 +521,8 @@
     sub = lax.broadcasted_iota(jnp.int32, (L, L), 0)
     upper = (sub <= lane).astype(BF)
     heads = lane < GH
+    per_head = (lax.broadcasted_iota(jnp.int32, (GW, 128), 0) >> 6
+                == lax.broadcasted_iota(jnp.int32, (GW, 128), 1)).astype(BF)
 
     def chunk(step, later):
         tick(step)
@@ -537,7 +539,7 @@
         cumt = cumt_ref[c]
         g = g_ref[c]
         d_scores = jnp.zeros((L, L), F32)
-        sums = jnp.zeros((3 * L + 16, 128), F32)
+        to_sum = []
         d_c = dbc_ref[rows, 128:]
         d_b = dbc_ref[rows, :128]
         heads_of_pair = []
@@ -586,8 +588,7 @@
             cum_high, cum_low = split2(dy_low.astype(F32) * y - low32 * d_weighted)
             end_high, end_low = split2(jnp.concatenate([at_end, jnp.zeros((7, 128), F32)], 0))
             ends = jnp.concatenate([end_high, end_low], 0)
-            per_head = ((sub >> 6) + 2 * q == lane).astype(BF)
-            sums = sums + mm(jnp.concatenate([cum_high, cum_low, (act * d_weighted).astype(BF), ends], 0), per_head)
+            to_sum.append(jnp.concatenate([cum_high, cum_low, (act * d_weighted).astype(BF), ends], 0))
             d_act = skip * dy + steps * d_weighted
             du = d_act * (su + act * (1.0 - su))
             pgrad_ref[K : K + 1, lanes] += jnp.sum(du, 0, keepdims=True)
@@ -603,6 +604,7 @@
         dg_ref[c] += d_scores
         dbc_ref[rows, 128:] = d_c
         dbc_ref[rows, :128] = d_b
+        sums = mm(jnp.concatenate(to_sum, 1), per_head)
         d_last = sums[3 * L : 3 * L + 1] + sums[3 * L + 8 : 3 * L + 9]
         hi, mid, lo = split3(sums[:L] + sums[L : 2 * L])
         parts = hi.astype(F32) + pltpu.roll(mid.astype(F32), 8, 1) + pltpu.roll(lo.astype(F32), 16, 1)
@@ -696,6 +698,9 @@
                 self.left(name, recv_sem, device)
 
 
+OUT_MAIN = 256
+
+
 class Place:
     def __init__(self):
         self.f = lax.axis_index("fsdp")
@@ -730,7 +735,7 @@
     depth = out_ref.shape[2] // 4
     at = pl.ds(pl.multiple_of(f * depth, depth), depth)
     if m == 2:
-        return out_ref.at[z, :, at]
+        return out_ref.at[z, pl.ds(0, OUT_MAIN), at]
     return inout_ref.at[z, at, pl.ds(m * GW, GW)]
 
 
@@ -789,39 +794,41 @@
 ORDER = (3, 2, 1, 0)
 ROWS = 128
 SCHEDULE = {
-    "s1": [("second", 0, 0), ("first", 0, 1)],
-    "s2": [("second", 1, 0), ("first", 1, 1)],
-    "s5": [("second", 0, 1), ("first", 0, 2)],
-    "m00": [("second", 1, 1), ("first", 1, 2), ("second", 0, 2), ("first", 0, 3)],
-    "m10": [("second", 1, 2), ("first", 1, 3), ("second", 0, 3), ("first", 2, 0)],
-    "m20": [("second", 1, 3), ("first", 2, 1), ("second", 2, 0), ("first", 2, 2)],
-    "m30": [("second", 2, 1), ("first", 2, 3), ("second", 2, 2)],
-    "n1": [("second", 2, 3)],
-    "b01": [("s1", 0)],
-    "b11": [("s1", 1)],
+    "s1": [("second", 0, 0)],
+    "s2": [("second", 1, 0), ("first", 0, 1)],
+    "s5": [("second", 0, 1), ("first", 1, 1)],
+    "m07": [("second", 1, 1), ("first", 0, 2)],
+    "m10": [("second", 0, 2), ("first", 1, 2)],
+    "p2": [("second", 1, 2), ("first", 0, 3)],
+    "m20": [("second", 0, 3), ("first", 1, 3)],
+    "p3": [("second", 1, 3), ("first", 2, 0)],
+    "m30": [("second", 2, 0), ("first", 2, 1)],
+    "m37": [("second", 2, 1), ("first", 2, 2)],
+    "b00": [("second", 2, 2), ("first", 2, 3)],
+    "b11": [("second", 2, 3), ("s1", 0), ("s1", 1)],
     "b21": [("s1", 2)],
     "b31": [("s1", 3)],
     "x1": [("s2", 0)],
-    "g01": [("s3", 0)],
-    "g02": [("s2", 1)],
-    "g06": [("s3", 1)],
-    "g07": [("s2", 2)],
-    "h01": [("s3", 2)],
-    "h02": [("s2", 3)],
-    "g14": [("s2", 4), ("last", 3)],
-    "h10": [("s3", 4)],
-    "h11": [("s2", 5)],
-    "g23": [("s3", 5)],
-    "g24": [("s2", 6)],
-    "h20": [("s3", 6)],
-    "h21": [("s2", 7)],
-    "g33": [("s3", 7)],
-    "g34": [("s2", 8)],
-    "h30": [("s3", 8)],
-    "h31": [("s2", 9)],
-    "t2": [("s3", 9), ("s2", 10)],
-    "t4": [("s2", 11), ("last", 10)],
-    "t5": [("last", 11)],
+    "g01": [("s3", 0), ("s2", 1)],
+    "g05": [("s3", 1)],
+    "g06": [("s2", 2)],
+    "h01": [("s3", 2), ("s2", 3)],
+    "g13": [("s2", 4), ("last", 3)],
+    "g17": [("s3", 4)],
+    "h10": [("s2", 5)],
+    "h12": [("s3", 5)],
+    "g23": [("s2", 6)],
+    "g27": [("s3", 6)],
+    "h20": [("s2", 7)],
+    "h22": [("s3", 7)],
+    "g33": [("s2", 8)],
+    "g37": [("s3", 8)],
+    "h30": [("s2", 9)],
+    "t0": [("s3", 9)],
+    "t1": [("s2", 10)],
+    "t2": [("last", 10)],
+    "t4": [("s2", 11)],
+    "t7": [("last", 11)],
 }
 T_INV, T_BACK = 16, 17
 
@@ -835,7 +842,7 @@
                  bc_ref, bct_ref, g_ref, pack_ref, cumt_ref, par_ref, hpar_ref, cst_ref, stw_ref, gains_ref, gaingrad_ref, st_ref,
                  srecv, srecv1, srecv3, srecvc, qrecv1, qrecv3, qsend, qrecvc, nparts, nrecv, nback,
                  dstep, dstate, pgrad, hgrad, sgrad, rt_ref, dg_ref, dbc_ref,
-                 sends, recvs, small_recvs, state_recvs, core_recvs, recv_sems, core_sems, state_sems, gain_sems,
+                 sends, recvs, small_recvs, state_recvs, core_recvs, recv_sems, core_sems, state_sems, gain_sems, rest_sems,
                  outs_sem, pre_sem, state_sem, own_sem, load_sems, stage_sem, hid_sem, credit, free_out, free_core, free_half):
     stepre_ref = pr_ref = ss_ref
     dcat = hall.at[:, pl.ds(0, 2 * GW)]
@@ -845,7 +852,7 @@
     wide = 2 * GW
     depth = model // 4
     links = Links(sends)
-    shards = [w0_ref, w1_ref, w2_ref]
+    shards = [w0_ref, w1_ref, w2_ref.at[pl.ds(0, OUT_MAIN)]]
     outs = []
 
     def put(src, dst):
@@ -862,6 +869,7 @@
     other = pl.ds(pl.multiple_of((1 - here.c) * rows_own, rows_own), rows_own)
     core = here.at(c=1 - here.c)
     one_block = recv2.at[0]
+    like = [one_block, one_block, recv2.at[0, pl.ds(0, OUT_MAIN)]]
     for k in (1, 2, 3):
         links.send(("small", k), small_ref, sbuf.at[here.f, z], small_recvs.at[k], here.at(z=zk[k]))
     links.send("hidden", hid_ref, hall.at[mine], core_recvs.at[0], core)
@@ -878,18 +886,38 @@
         src = shards[m] if k == 0 else dst
         if k:
             links.arrived(dst, recv_sem(m, here.f, zk[k]), here.at(z=zk[k]))
-        links.send(("first", m, k, 2), src, dst, recv_sem(m, here.f, zk[k]), here.at(f=here.f2), one_block)
-        links.send(("first", m, k, 3), src, dst, recv_sem(m, here.f, zk[k]), here.at(f=here.f3), one_block)
+        links.send(("first", m, k, 2), src, dst, recv_sem(m, here.f, zk[k]), here.at(f=here.f2), like[m])
+        links.send(("first", m, k, 3), src, dst, recv_sem(m, here.f, zk[k]), here.at(f=here.f3), like[m])
 
     def second(m, k):
         src = piece(win, wout, m, here.f2, zk[k])
         links.arrived(src, recv_sem(m, here.f2, zk[k]), here.at(f=here.f2))
-        links.send(("second", m, k), src, src, recv_sem(m, here.f2, zk[k]), here.at(f=here.f3), one_block)
+        links.send(("second", m, k), src, src, recv_sem(m, here.f2, zk[k]), here.at(f=here.f3), like[m])
 
     def third(m, k):
         for f in (here.f3, here.f4):
             src = piece(win, wout, m, f, zk[k])
             links.arrived(src, recv_sem(m, f, zk[k]), here.at(f=here.f3))
+
+    rest = pl.ds(OUT_MAIN, GW - OUT_MAIN)
+
+    def rest_of(f):
+        return wout.at[z, rest, pl.ds(pl.multiple_of(f * depth, depth), depth)]
+
+    def rest_first():
+        for n, f in enumerate((here.f2, here.f3)):
+            links.send(("rest", n), w2_ref.at[rest], rest_of(here.f), rest_sems.at[n], here.at(f=f))
+
+    def rest_second():
+        links.arrived(rest_of(here.f2), rest_sems.at[0], here.at(f=here.f2))
+        links.send(("rest", 2), rest_of(here.f2), rest_of(here.f2), rest_sems.at[2], here.at(f=here.f3))
+
+    def rest_third():
+        links.arrived(rest_of(here.f3), rest_sems.at[1], here.at(f=here.f3))
+        links.arrived(rest_of(here.f4), rest_sems.at[2], here.at(f=here.f3))
+        own_copies[2].wait()
+        for k in (1, 2, 3):
+            links.send(("rest", 2 + k), wout.at[z, rest], wout.at[z, rest], rest_sems.at[2 + k], here.at(z=zk[k]))
 
     events = {"first": first, "second": second}
 
@@ -910,7 +938,9 @@
 
     push_z(0)
     links.send("cot", cot_ref, call.at[mine], core_recvs.at[1], core)
-    own_copies = [pltpu.make_async_copy(shards[m], piece(win, wout, m, here.f, z), own_sem.at[m]) for m in range(3)]
+    own_copies = [pltpu.make_async_copy(shards[m], piece(win, wout, m, here.f, z), own_sem.at[m]) for m in range(2)]
+    own_out = wout.at[z, :, pl.ds(pl.multiple_of(here.f * depth, depth), depth)]
+    own_copies.append(pltpu.make_async_copy(w2_ref, own_out, own_sem.at[2]))
     own_copies.append(pltpu.make_async_copy(cot_ref, call.at[mine], own_sem.at[3]))
     own_copies.append(pltpu.make_async_copy(hid_ref, hall.at[mine], hid_sem.at[4]))
     for copy in own_copies:
@@ -936,6 +966,7 @@
     links.send(("state", 2), state_of(here.f2, half_state), state_of(here.f2, half_state), state_recvs.at[2], here.at(f=here.f3))
     links.send(("state", 3), state_of(here.f2, half_state), state_of(here.f2, half_state), state_recvs.at[3], core)
     first(1, 0)
+    rest_first()
     push_z(2)
     due("s0")
     links.arrived(sbuf.at[here.f3], small_recvs.at[5], here.at(f=here.f3))
@@ -967,6 +998,7 @@
     hpar_ref[...] = jnp.concatenate([own_heads[0:1], decay, own_heads[2:3], jnp.zeros((5, 128), F32)], 0)
 
     due("s1")
+    rest_second()
     own_copies[4].wait()
     links.arrived(hall.at[other], core_recvs.at[0], core)
 
@@ -1014,10 +1046,11 @@
     TURNED = len(outs)
     put(flip, normt_hbm)
     due("s4")
+    rest_third()
     prep_chunks(statepre_ref, stepre_ref, tok_ref, docs_ref, cst_ref, hpar_ref, bc_ref, bct_ref, g_ref, pack_ref, cumt_ref)
     due("s5")
     links.arrived(call.at[other], core_recvs.at[1], core)
-    for copy in own_copies[:4]:
+    for copy in (own_copies[0], own_copies[1], own_copies[3]):
         copy.wait()
     ss_ref[...] = jnp.zeros_like(ss_ref)
     for slot in range(2):
@@ -1190,6 +1223,8 @@
         grad_out(k)
         due("b%d1" % k)
         third(2, k)
+        if k:
+            links.arrived(wout.at[zk[k], rest], rest_sems.at[2 + k], here.at(z=zk[k]))
         gaingrad_ref[k] = jnp.zeros((8, GW), F32)
 
         def back(i, _, k=k):
@@ -1280,6 +1315,8 @@
     for k in range(4):
         for name in (("first", 2, k, 2), ("first", 2, k, 3), ("second", 2, k)):
             links.left(name, core_recvs.at[0], core)
+    for n in range(6):
+        links.left(("rest", n), core_recvs.at[0], core)
     pl.semaphore_signal(free_out, inc=1, device_id=here.at(f=f3), device_id_type=MESH)
     links.left(("half", 0), core_sems.at[0], core)
     hgrad[...] = jnp.zeros_like(hgrad)
@@ -1535,6 +1572,7 @@
             pltpu.SemaphoreType.DMA((5,)),
             pltpu.SemaphoreType.DMA((4,)),
             pltpu.SemaphoreType.DMA((7,)),
+            pltpu.SemaphoreType.DMA((6,)),
             pltpu.SemaphoreType.DMA((16,)),
             pltpu.SemaphoreType.DMA((4,)),
             pltpu.SemaphoreType.DMA((4,)),

time: 295 us -> 292 us (0.990)
  Pallas kernels: 294 us -> 291 us
where the time goes in v5:
time: 292 us
  Pallas kernels  291 us (100%)
    pallas_call x1, Pallas kernels, block_call(): pl.pallas_call(functools.partial(block_kernel, model), out_shape=(sds((ro...  286 us

profile of v5, /device:TPU:0, one launch (start us, length us, event | category | flops | bytes accessed | tf_op | source)
XLA Modules:
  0.0 292.1 jit_solution(17229103621057519418)
XLA Ops:
  0.7 285.8 %whole_block.1 = (bf16[512,1536]{1,0:T(8,128)(2,1)}, bf16[512,1536]{1,0:T(8,128)(2,1)}, bf16[1536,1024]{1,0:T(8,128)(2,1)}, bf16[4,1536,768]{2,1,0:T(8,128)(2,1)...) custom-call(bf16[512,1536]{1,0:T(8,128)(2,1)} %hid_ref.1, ...), custom_call_target="tpu_custom_call" | custom-call | tf_op jit(solution)/shard_map/whole_block/pallas_call | solution.py:1543
  286.4 5.5 %finish.1 = (bf16[512,1536]{1,0:T(8,128)(2,1)}, bf16[512,1536]{1,0:T(8,128)(2,1)}, f32[384]{0:T(512)}, f32[384,384]{1,0:T(8,128)}, f32[384,384]{1,0:T(8,128)}, /...) custom-call(bf16[512,1536]{1,0:T(8,128)(2,1)} %get-tuple-element.40., ...), custom_call_target="tpu_custom_call" | custom-call | tf_op jit(solution)/shard_map/finish/pallas_call | solution.py:1639
